TPU v7x, 32 devices: a whole 2x2x4 slice. The times are simulated.
32 devices in a mesh: members: 2 (over y), gx: 4 (over z), gy: 2 (over x), wa: 2 (over core).
Axes of the slice: x: 2, y: 2, z: 4, core: 2. Of those that a mesh axis runs over, the one named last changes fastest.
Arguments:
- adjoint: float32 [3, 128, 32, 256], P(None, ('members', 'gx'), 'gy', 'wa'), parts along dimension 1, may hold values from -6 to 6
- permeability: float32 [3, 128, 32, 256], P(None, ('members', 'gx'), 'gy', 'wa'), parts along dimension 1, may hold values from 0.1 to 10
- pore_volume: float32 [128, 32, 256], P(('members', 'gx'), 'gy', 'wa'), parts along dimension 0, may hold values from 0.05 to 0.5
- rock_type: int32 [128, 32, 256], P(('members', 'gx'), 'gy', 'wa'), parts along dimension 0, may hold values from 0 to 7
- rock_table: float32 [8, 3], replicated, may hold values from 0.2 to 2
- perf_column: int32 [1024], P(('gx', 'gy')), may hold values from 0 to 255
- perf_owner: int32 [1024, 1], P(('gx', 'gy')), may hold values from 0 to 7; in each aligned block of 128 rows (0 to 127, 128 to 255, ...) at most 32 rows name the same one
- perf_slot: int32 [1024], P(('gx', 'gy')), may hold values from 0 to 7
- observed: float32 [64, 256], P(('gx', 'gy'), 'wa'), may hold values from -4 to 4
Outputs:
- adjoint_out: float32 [3, 128, 32, 256], P(None, ('members', 'gx'), 'gy', 'wa'), parts along dimension 1
- well_sens: float32 [128, 256], P(('members', 'gx', 'gy'), 'wa'), parts along dimension 0
There are 2 independent parts, one for each index of `members`. A program takes and returns all parts, laid end to end along the dimension named above; an argument that names none is the same for every part. Nothing has to cross between parts.
Inputs may be any that keep to these rules, and one draw needn't show every extreme that they name: `perf_owner`: within the rows of one grid block (aligned blocks of 128 rows) no value appears more than 32 times, and some value appears exactly 32 times.
All inputs are finite; a program needn't handle non-finite values.
Results may differ from a plain program's by a relative error of at most 0.0001.
Values sent between devices are 32-bit elements; how exact they have to be, the bound alone decides.
No kernel may reach another device: no remote copies, remote signals or barrier semaphores. Data moves between devices by JAX's collectives and lax.ppermute only.
A program may use at most 64 MiB of HBM per device.

v0:
```python
import jax
import jax.numpy as jnp
from jax import lax
from jax.sharding import PartitionSpec as P

STEPS = 4


def with_halo(cells, sides, width):
    for axis, dim in sides:
        count = lax.axis_size(axis)
        ends = count - 1
        head = lax.slice_in_dim(cells, 0, width, axis=dim)
        tail = lax.slice_in_dim(cells, cells.shape[dim] - width, cells.shape[dim], axis=dim)
        cells = jnp.concatenate(
            [
                lax.ppermute(tail, axis, [(i, (i + 1) % count) for i in range(ends)]),
                cells,
                lax.ppermute(head, axis, [((i + 1) % count, i) for i in range(ends)]),
            ],
            axis=dim,
        )
    return cells


def harmonic(first, second):
    return 2.0 * first * second / (first + second)


def local(
    adjoint,
    permeability,
    pore_volume,
    rock_type,
    rock_table,
    perf_column,
    perf_owner,
    perf_slot,
    observed,
):
    size_x = lax.axis_size("gx")
    size_y = lax.axis_size("gy")
    owners = size_x * size_y
    cells_x = adjoint.shape[1]
    cells_y = adjoint.shape[2]
    layers = adjoint.shape[3]
    columns = cells_x * cells_y
    perf_rows = perf_column.shape[0]
    well_slots = observed.shape[0]
    capacity = max(2, 2 * perf_rows // owners)
    padded_perm = with_halo(permeability, (("gx", 1), ("gy", 2), ("wa", 3)), 1)
    t_xm = harmonic(permeability[0], padded_perm[0, :-2, 1:-1, 1:-1])
    t_xp = harmonic(permeability[0], padded_perm[0, 2:, 1:-1, 1:-1])
    t_ym = harmonic(permeability[1], padded_perm[1, 1:-1, :-2, 1:-1])
    t_yp = harmonic(permeability[1], padded_perm[1, 1:-1, 2:, 1:-1])
    t_zm = harmonic(permeability[2], padded_perm[2, 1:-1, 1:-1, :-2])
    t_zp = harmonic(permeability[2], padded_perm[2, 1:-1, 1:-1, 2:])
    weight_sum = t_xm + t_xp + t_ym + t_yp + t_zm + t_zp
    rock_ids = jnp.arange(rock_table.shape[0], dtype=jnp.int32)
    matches = (rock_type[None] == rock_ids[:, None, None, None]).astype(jnp.float32)
    mobility = jnp.einsum("rxyz,rp->pxyz", matches, rock_table, precision=lax.Precision.HIGHEST)
    root_perm = jnp.sqrt(permeability[0] * permeability[1])
    well_index = root_perm / (1.0 + root_perm)
    mobility_cols = mobility.reshape(3, columns, layers)
    index_cols = well_index.reshape(columns, layers)
    destination = perf_owner[:, 0]
    owner_hits = (destination[:, None] == jnp.arange(owners, dtype=jnp.int32)[None, :]).astype(
        jnp.int32
    )
    earlier = jnp.cumsum(owner_hits, axis=0) - owner_hits
    position = jnp.sum(earlier * owner_hits, axis=1)
    flat_position = destination * capacity + position
    slot_send = jnp.full((owners * capacity,), -1, jnp.int32).at[flat_position].set(perf_slot)
    slot_recv = lax.all_to_all(
        slot_send.reshape(owners, capacity), ("gx", "gy"), split_axis=0, concat_axis=0, tiled=True
    ).reshape(-1)
    slot_match = (jnp.arange(well_slots, dtype=jnp.int32)[:, None] == slot_recv[None, :]).astype(
        jnp.float32
    )
    well_sens = jnp.zeros((well_slots, layers), jnp.float32)
    for iteration in range(STEPS):
        combined = (
            index_cols * jnp.sum(mobility_cols * adjoint.reshape(3, columns, layers), axis=0) / 4.0
        )
        flow = jnp.take(combined, perf_column, axis=0)
        outgoing = jnp.zeros((owners * capacity, layers), jnp.float32).at[flat_position].set(flow)
        arrived = lax.all_to_all(
            outgoing.reshape(owners, capacity, layers),
            ("gx", "gy"),
            split_axis=0,
            concat_axis=0,
            tiled=True,
        )
        arrived = arrived.reshape(owners * capacity, layers)
        well_sens = jnp.dot(slot_match, arrived, precision=lax.Precision.HIGHEST)
        response = jnp.tanh(well_sens - observed)
        returning = jnp.dot(slot_match.T, response, precision=lax.Precision.HIGHEST)
        returned = lax.all_to_all(
            returning.reshape(owners, capacity, layers),
            ("gx", "gy"),
            split_axis=0,
            concat_axis=0,
            tiled=True,
        )
        back_rows = jnp.take(returned.reshape(owners * capacity, layers), flat_position, axis=0)
        column_sum = jnp.zeros((columns, layers), jnp.float32).at[perf_column].add(back_rows)
        source = (index_cols[None] * mobility_cols * column_sum[None]).reshape(
            3, cells_x, cells_y, layers
        )
        padded = with_halo(adjoint, (("gx", 1), ("gy", 2), ("wa", 3)), 1)
        beside = t_xm * padded[:, :-2, 1:-1, 1:-1] + t_xp * padded[:, 2:, 1:-1, 1:-1]
        beside = beside + t_ym * padded[:, 1:-1, :-2, 1:-1] + t_yp * padded[:, 1:-1, 2:, 1:-1]
        beside = beside + t_zm * padded[:, 1:-1, 1:-1, :-2] + t_zp * padded[:, 1:-1, 1:-1, 2:]
        adjoint = (pore_volume * adjoint + mobility * beside + source) / (
            pore_volume + mobility * weight_sum
        )
    return (adjoint, well_sens)


def solution(mesh):
    placed = (
        P(None, ("members", "gx"), "gy", "wa"),
        P(None, ("members", "gx"), "gy", "wa"),
        P(("members", "gx"), "gy", "wa"),
        P(("members", "gx"), "gy", "wa"),
        P(),
        P(("gx", "gy")),
        P(("gx", "gy"), None),
        P(("gx", "gy")),
        P(("gx", "gy"), "wa"),
    )
    return jax.shard_map(
        local,
        mesh=mesh,
        in_specs=placed,
        out_specs=(P(None, ("members", "gx"), "gy", "wa"), P(("members", "gx", "gy"), "wa")),
        check_vma=False,
    )
```

profile of v0, /device:TPU:0, one launch (start us, length us, event | category | flops | bytes accessed | tf_op | source)
XLA Modules:
  0.0 256.3 jit_solution(14796098265949592109)
XLA Ops:
  1.5 4.9 %collective-permute-start = (f32[3,1,16,128]{3,2,1,0:T(8,128)S(1)}, f32[3,1,16,128]{3,2,1,0:T(8,128)S(1)}, u32[]{:S(2)}, u32[]{:S(2)}) collective-permute-start(f32[3,1,16,128]{3,2,1,0:T(8,128)S(1)} %get-tuple-element.58), channel_id=1, source_target_pairs={{0,4},{4,8},{8,12},{1,5},{5,9},{9,13},{2,6},{6,10},{10,14},{3,7},{... | collective-permute-start | bytes 73736 | tf_op jit(solution)/shard_map/ppermute | solution.py:17
  9.8 4.5 %collective-permute-start.1 = (f32[3,1,16,128]{3,0,2,1:T(4,128)S(1)}, f32[3,1,16,128]{3,0,2,1:T(4,128)S(1)}, u32[]{:S(2)}, u32[]{:S(2)}) collective-permute-start(f32[3,1,16,128]{3,0,2,1:T(4,128)S(1)} %get-tuple-element.53), channel_id=1, source_target_pairs={{0,4},{4,8},{8,12},{1,5},{5,9},{9,13},{2,6},{6,10},{10,14},{3,7},{... | collective-permute-start | bytes 73736 | tf_op jit(solution)/shard_map/ppermute | solution.py:17
  18.6 4.8 %all-to-all-start = ((s32[8,1,32]{2,1,0:T(1,128)}), s32[8,1,32]{2,1,0:T(1,128)S(1)}, u32[]{:S(2)}, u32[]{:S(2)}) async-start(s32[8,1,32]{2,1,0:T(1,128)} %all_to_all.30), calls=%async_computation | async-start | bytes 8192 | tf_op jit(solution)/shard_map/all_to_all | solution.py:74
  30.0 3.4 %copy.107 = f32[3,18,16,128]{2,1,3,0:T(8,128)} copy(f32[3,18,16,128]{3,2,1,0:T(8,128)S(1)} %constant_dynamic-update-slice_fusion) | data formatting | bytes 884736 | tf_op jit(solution)/shard_map/concatenate | solution.py:15
  33.3 3.9 %collective-permute-start.4 = (f32[3,18,1,128]{3,1,2,0:T(8,128)S(1)}, f32[3,18,1,128]{3,1,2,0:T(8,128)S(1)}, u32[]{:S(2)}, u32[]{:S(2)}) collective-permute-start(f32[3,18,1,128]{3,1,2,0:T(8,128)S(1)} %copy.132), channel_id=1, source_target_pairs={{0,2},{1,3},{4,6},{5,7},{8,10},{9,11},{12,14},{13,15},{16,18},{17,... | collective-permute-start | bytes 82952 | tf_op jit(solution)/shard_map/ppermute | solution.py:17
  40.4 4.5 %collective-permute-start.5 = (f32[3,18,1,128]{3,0,2,1:T(4,128)S(1)}, f32[3,18,1,128]{3,0,2,1:T(4,128)S(1)}, u32[]{:S(2)}, u32[]{:S(2)}) collective-permute-start(f32[3,18,1,128]{3,0,2,1:T(4,128)S(1)} %get-tuple-element.44), channel_id=1, source_target_pairs={{0,2},{1,3},{4,6},{5,7},{8,10},{9,11},{12,14},{13,15},{16,18},{17,... | collective-permute-start | bytes 82952 | tf_op jit(solution)/shard_map/ppermute | solution.py:17
  46.3 1.8 scatter_custom_fusion.1
  48.1 3.4 %copy.106 = f32[3,18,1,128]{2,1,3,0:T(8,128)} copy(f32[3,18,1,128]{3,1,2,0:T(8,128)S(1)} %collective-permute-done.4) | data formatting | bytes 55296 | tf_op jit(solution)/shard_map/ppermute | solution.py:17
  51.4 3.4 %copy.108 = f32[3,18,1,128]{2,1,3,0:T(8,128)} copy(f32[3,18,1,128]{3,1,2,0:T(8,128)S(1)} %collective-permute-done.6) | data formatting | bytes 55296 | tf_op jit(solution)/shard_map/ppermute | solution.py:19
  54.8 7.6 %pad_maximum_fusion = f32[3,18,18,128]{2,1,3,0:T(8,128)S(1)} fusion(f32[3,18,1,128]{2,1,3,0:T(8,128)} %copy.108, f32[3,18,16,128]{2,1,3,0:T(8,128)} %copy.107, f32[3,18,1,128]{2,1,3,0:T(8,128)} %copy.106), kind=kLoop, calls=%fused_computation.17 | loop fusion | flops 248832 | bytes 995328 | tf_op jit(solution)/shard_map/concatenate | solution.py:15
  62.4 2.1 copy-done.1
  65.2 1.9 collective-permute-start.8
  69.1 7.8 %all-to-all-start.1 = ((f32[8,32,128]{2,1,0:T(8,128)}), f32[8,32,128]{2,1,0:T(8,128)}, u32[]{:S(2)}, u32[]{:S(2)}) async-start(f32[8,32,128]{2,1,0:T(8,128)} %bitcast.15), calls=%async_computation.1 | async-start | bytes 262144 | tf_op jit(solution)/shard_map/all_to_all | solution.py:87
  77.7 3.3 %collective-permute-start.9 = (f32[3,18,18,1]{2,3,1,0:T(1,128)S(1)}, f32[3,18,18,1]{2,3,1,0:T(1,128)S(1)}, u32[]{:S(2)}, u32[]{:S(2)}) collective-permute-start(f32[3,18,18,1]{2,3,1,0:T(1,128)S(1)} %copy.111), channel_id=1, source_target_pairs={{0,1},{2,3},{4,5},{6,7},{8,9},{10,11},{12,13},{14,15},{16,17},{18,... | collective-permute-start | bytes 11672 | tf_op jit(solution)/shard_map/ppermute | solution.py:17
  81.5 1.4 collective-permute-start.11
  84.3 4.5 %copy.110 = f32[3,18,18,128]{3,2,1,0:T(8,128)} copy(f32[3,18,18,128]{2,1,3,0:T(8,128)} %copy-done.1) | data formatting | bytes 995328 | tf_op jit(solution)/shard_map/concatenate | solution.py:15
  88.8 2.0 copy.109
  90.9 2.0 copy.114
  92.9 1.4 copy.112
  94.3 1.4 copy.116
  97.7 5.7 %all-to-all-start.2 = ((f32[8,32,128]{2,1,0:T(8,128)}), f32[8,32,128]{2,1,0:T(8,128)S(1)}, u32[]{:S(2)}, u32[]{:S(2)}) async-start(f32[8,32,128]{2,1,0:T(8,128)} %bitcast.17), calls=%async_computation.2 | async-start | bytes 262144 | tf_op jit(solution)/shard_map/all_to_all | solution.py:98
  103.5 1.5 add_bitcast_fusion
  105.0 6.7 %all-to-all-done.2 = f32[8,32,128]{2,1,0:T(8,128)S(1)} async-done(((f32[8,32,128]{2,1,0:T(8,128)}), f32[8,32,128]{2,1,0:T(8,128)S(1)}, u32[]{:S(2)}, u32[]{:S(2)}) %all-to-all-start.2) | async-done | bytes 131104 | tf_op jit(solution)/shard_map/all_to_all | solution.py:98
  111.7 1.6 scatter_custom_fusion.2
  113.3 4.9 %multiply_reduce_fusion.2 = (f32[16,16,128]{2,1,0:T(8,128)S(1)}, f32[3,16,16,128]{3,0,2,1:T(4,128)S(1)}) fusion(f32[3,16,16,128]{3,0,2,1:T(4,128)S(1)} %get-tuple-element.60, f32[16,16,128]{2,1,0:T(8,128)S(1)} %get-tuple-element.21, f32[16,16,128]{2,1,0:T(8,128)S(1)} %bitcast.106, f32[16,16,128]{2,1,0:T(8,128)S(1)} %get-tuple-element.17, ...), kind=kLoop, calls=%fused_computation.156 | loop fusion | flops 3112960 | bytes 3176032 | tf_op jit(solution)/shard_map/reduce_sum | solution.py:83
  118.2 1.8 collective-permute-start.12
  121.4 1.9 scatter_custom_fusion.3
  123.3 5.5 %all-to-all-start.3 = ((f32[8,32,128]{2,1,0:T(8,128)}), f32[8,32,128]{2,1,0:T(8,128)S(1)}, u32[]{:S(2)}, u32[]{:S(2)}) async-start(f32[8,32,128]{2,1,0:T(8,128)} %bitcast.22), calls=%async_computation.3 | async-start | bytes 262144 | tf_op jit(solution)/shard_map/all_to_all | solution.py:87
  128.9 3.9 %collective-permute-start.14 = (f32[3,18,1,128]{3,0,2,1:T(4,128)S(1)}, f32[3,18,1,128]{3,0,2,1:T(4,128)S(1)}, u32[]{:S(2)}, u32[]{:S(2)}) collective-permute-start(f32[3,18,1,128]{3,0,2,1:T(4,128)S(1)} %get-tuple-element.42), channel_id=1, source_target_pairs={{0,2},{1,3},{4,6},{5,7},{8,10},{9,11},{12,14},{13,15},{16,18},{17,... | collective-permute-start | bytes 82952 | tf_op jit(solution)/shard_map/ppermute | solution.py:17
  134.4 4.2 %collective-permute-done.15 = f32[3,18,1,128]{3,0,2,1:T(4,128)S(1)} collective-permute-done((f32[3,18,1,128]{3,0,2,1:T(4,128)S(1)}, f32[3,18,1,128]{3,0,2,1:T(4,128)S(1)}, u32[]{:S(2)}, u32[]{:S(2)}) %collective-permute-start.15) | collective-permute-done | bytes 27680 | tf_op jit(solution)/shard_map/ppermute | solution.py:19
  140.0 4.5 %all-to-all-start.4 = ((f32[8,32,128]{2,1,0:T(8,128)}), f32[8,32,128]{2,1,0:T(8,128)}, u32[]{:S(2)}, u32[]{:S(2)}) async-start(f32[8,32,128]{2,1,0:T(8,128)} %bitcast.24), calls=%async_computation.4 | async-start | bytes 262144 | tf_op jit(solution)/shard_map/all_to_all | solution.py:98
  144.5 1.5 fusion.142
  146.0 1.5 copy.118
  148.8 1.5 copy.120
  153.4 1.4 copy.121
  154.8 3.2 %scatter_custom_fusion.4 = f32[256,128]{1,0:T(8,128)} fusion(s32[128]{0:T(128)} %copy-done.44, f32[]{:T(128)} %constant.7.clone.1, f32[]{:T(128)} %constant.15.clone.8, pred[128]{0:T(512)(128)(4,1)} %get-tuple-element.19, f32[256,128]{1,0:T(8,128)} %bitcast.25, s32[1024]{0:T(1024)} %copy-done.27), kind=kCustom, calls=%fused_computation.192 | custom fusion | flops 32768 | bytes 267776 | tf_op jit(solution)/shard_map/scatter-add | solution.py:106
  158.0 3.9 %multiply_reduce_fusion.1 = (f32[16,16,128]{2,1,0:T(8,128)S(1)}, f32[3,16,16,128]{3,0,2,1:T(4,128)S(1)}) fusion(f32[3,16,16,128]{3,0,2,1:T(4,128)S(1)} %get-tuple-element.60, f32[16,16,128]{2,1,0:T(8,128)S(1)} %get-tuple-element.21, f32[16,16,128]{2,1,0:T(8,128)} %bitcast.107, f32[16,16,128]{2,1,0:T(8,128)S(1)} %get-tuple-element.17, ...), kind=kLoop, calls=%fused_computation.155 | loop fusion | flops 3899392 | bytes 2733664 | tf_op jit(solution)/shard_map/reduce_sum | solution.py:83
  162.0 3.9 %collective-permute-start.18 = (f32[3,1,16,128]{3,0,2,1:T(4,128)S(1)}, f32[3,1,16,128]{3,0,2,1:T(4,128)S(1)}, u32[]{:S(2)}, u32[]{:S(2)}) collective-permute-start(f32[3,1,16,128]{3,0,2,1:T(4,128)S(1)} %get-tuple-element.48), channel_id=1, source_target_pairs={{0,4},{4,8},{8,12},{1,5},{5,9},{9,13},{2,6},{6,10},{10,14},{3,7},{... | collective-permute-start | bytes 73736 | tf_op jit(solution)/shard_map/ppermute | solution.py:17
  167.2 1.9 scatter_custom_fusion.5
  169.2 6.6 %all-to-all-start.5 = ((f32[8,32,128]{2,1,0:T(8,128)}), f32[8,32,128]{2,1,0:T(8,128)S(1)}, u32[]{:S(2)}, u32[]{:S(2)}) async-start(f32[8,32,128]{2,1,0:T(8,128)} %bitcast.28), calls=%async_computation.5 | async-start | bytes 262144 | tf_op jit(solution)/shard_map/all_to_all | solution.py:87
  175.9 3.9 %collective-permute-start.20 = (f32[3,18,1,128]{3,0,2,1:T(4,128)S(1)}, f32[3,18,1,128]{3,0,2,1:T(4,128)S(1)}, u32[]{:S(2)}, u32[]{:S(2)}) collective-permute-start(f32[3,18,1,128]{3,0,2,1:T(4,128)S(1)} %get-tuple-element.40), channel_id=1, source_target_pairs={{0,2},{1,3},{4,6},{5,7},{8,10},{9,11},{12,14},{13,15},{16,18},{17,... | collective-permute-start | bytes 82952 | tf_op jit(solution)/shard_map/ppermute | solution.py:17
  181.4 4.2 %collective-permute-done.21 = f32[3,18,1,128]{3,0,2,1:T(4,128)S(1)} collective-permute-done((f32[3,18,1,128]{3,0,2,1:T(4,128)S(1)}, f32[3,18,1,128]{3,0,2,1:T(4,128)S(1)}, u32[]{:S(2)}, u32[]{:S(2)}) %collective-permute-start.21) | collective-permute-done | bytes 27680 | tf_op jit(solution)/shard_map/ppermute | solution.py:19
  186.7 1.6 fusion.111
  188.3 4.5 %all-to-all-start.6 = ((f32[8,32,128]{2,1,0:T(8,128)}), f32[8,32,128]{2,1,0:T(8,128)S(1)}, u32[]{:S(2)}, u32[]{:S(2)}) async-start(f32[8,32,128]{2,1,0:T(8,128)} %bitcast.30), calls=%async_computation.6 | async-start | bytes 262144 | tf_op jit(solution)/shard_map/all_to_all | solution.py:98
  192.8 1.5 fusion.141
  194.4 1.5 copy.122
  197.1 1.5 copy.124
  198.7 1.5 collective-permute-start.23
  201.7 1.4 copy.125
  203.2 2.2 scatter_custom_fusion.6
  205.4 3.9 %multiply_reduce_fusion = (f32[16,16,128]{2,1,0:T(8,128)S(1)}, f32[3,16,16,128]{3,0,2,1:T(4,128)S(1)}) fusion(f32[3,16,16,128]{3,0,2,1:T(4,128)S(1)} %get-tuple-element.60, f32[16,16,128]{2,1,0:T(8,128)S(1)} %get-tuple-element.21, f32[16,16,128]{2,1,0:T(8,128)} %bitcast.108, f32[16,16,128]{2,1,0:T(8,128)S(1)} %get-tuple-element.17, ...), kind=kLoop, calls=%fused_computation.154 | loop fusion | flops 3899392 | bytes 2733664 | tf_op jit(solution)/shard_map/reduce_sum | solution.py:83
  209.3 3.9 %collective-permute-start.24 = (f32[3,1,16,128]{3,0,2,1:T(4,128)S(1)}, f32[3,1,16,128]{3,0,2,1:T(4,128)S(1)}, u32[]{:S(2)}, u32[]{:S(2)}) collective-permute-start(f32[3,1,16,128]{3,0,2,1:T(4,128)S(1)} %get-tuple-element.46), channel_id=1, source_target_pairs={{0,4},{4,8},{8,12},{1,5},{5,9},{9,13},{2,6},{6,10},{10,14},{3,7},{... | collective-permute-start | bytes 73736 | tf_op jit(solution)/shard_map/ppermute | solution.py:17
  214.6 1.9 scatter_custom_fusion.7
  216.5 6.6 %all-to-all-start.7 = ((f32[8,32,128]{2,1,0:T(8,128)}), f32[8,32,128]{2,1,0:T(8,128)S(1)}, u32[]{:S(2)}, u32[]{:S(2)}) async-start(f32[8,32,128]{2,1,0:T(8,128)} %bitcast.34), calls=%async_computation.7 | async-start | bytes 262144 | tf_op jit(solution)/shard_map/all_to_all | solution.py:87
  223.2 3.9 %collective-permute-start.26 = (f32[3,18,1,128]{3,0,2,1:T(4,128)S(1)}, f32[3,18,1,128]{3,0,2,1:T(4,128)S(1)}, u32[]{:S(2)}, u32[]{:S(2)}) collective-permute-start(f32[3,18,1,128]{3,0,2,1:T(4,128)S(1)} %get-tuple-element.38), channel_id=1, source_target_pairs={{0,2},{1,3},{4,6},{5,7},{8,10},{9,11},{12,14},{13,15},{16,18},{17,... | collective-permute-start | bytes 82952 | tf_op jit(solution)/shard_map/ppermute | solution.py:17
  228.8 4.2 %collective-permute-done.27 = f32[3,18,1,128]{3,0,2,1:T(4,128)S(1)} collective-permute-done((f32[3,18,1,128]{3,0,2,1:T(4,128)S(1)}, f32[3,18,1,128]{3,0,2,1:T(4,128)S(1)}, u32[]{:S(2)}, u32[]{:S(2)}) %collective-permute-start.27) | collective-permute-done | bytes 27680 | tf_op jit(solution)/shard_map/ppermute | solution.py:19
  234.0 1.7 fusion.109
  235.7 4.6 %all-to-all-start.8 = ((f32[8,32,128]{2,1,0:T(8,128)}), f32[8,32,128]{2,1,0:T(8,128)S(1)}, u32[]{:S(2)}, u32[]{:S(2)}) async-start(f32[8,32,128]{2,1,0:T(8,128)} %bitcast.36), calls=%async_computation.8 | async-start | bytes 262144 | tf_op jit(solution)/shard_map/all_to_all | solution.py:98
  240.2 1.5 fusion.140
  241.8 1.5 copy.126
  244.5 1.5 copy.128
  249.1 1.4 copy.129
  250.6 1.6 scatter_custom_fusion.8
  252.2 3.3 %fusion.8 = f32[3,16,16,128]{3,0,2,1:T(4,128)S(1)} fusion(f32[3,16,16,128]{3,0,2,1:T(4,128)S(1)} %get-tuple-element.60, f32[3,18,18,1]{3,0,2,1:T(4,128)} %copy.129, f32[3,18,1,128]{3,0,2,1:T(4,128)} %copy-done.19, f32[3,18,1,128]{3,0,2,1:T(4,128)} %copy-done.18, f32[3,1,16,128]{3,0,2,1:T(4,128)} %copy-done.9, f32[3,16,16,128]{3,0,2,1:T(4,128)S(1)} %get-tuple-element.12, ...), kind=kLoop, calls=%fused_computation.36 | loop fusion | flops 3735552 | bytes 2602592 | tf_op jit(solution)/shard_map/div | solution.py:114
  (200 shorter events, 51.0 us)
Async XLA Ops:
  0.6 38.0 %copy-start = (f32[8,3]{0,1:T(4,128)S(1)}, f32[8,3]{0,1:T(4,128)}, u32[]{:S(2)}) copy-start(f32[8,3]{0,1:T(4,128)} %param.15) | copy-start | bytes 292
  0.6 38.0 %copy-start.4 = (f32[3,16,16,128]{3,2,1,0:T(8,128)S(1)}, f32[3,16,16,128]{3,2,1,0:T(8,128)}, u32[]{:S(2)}) copy-start(f32[3,16,16,128]{3,2,1,0:T(8,128)} %param.11) | copy-start | bytes 1179652
  0.7 38.0 %copy-start.26 = (s32[16,16,128]{2,1,0:T(8,128)S(1)}, s32[16,16,128]{2,1,0:T(8,128)}, u32[]{:S(2)}) copy-start(s32[16,16,128]{2,1,0:T(8,128)} %param.14) | copy-start | bytes 393220
  1.5 26.8 %collective-permute-start = (f32[3,1,16,128]{3,2,1,0:T(8,128)S(1)}, f32[3,1,16,128]{3,2,1,0:T(8,128)S(1)}, u32[]{:S(2)}, u32[]{:S(2)}) collective-permute-start(f32[3,1,16,128]{3,2,1,0:T(8,128)S(1)} %get-tuple-element.58), channel_id=1, source_target_pairs={{0,4},{4,8},{8,12},{1,5},{5,9},{9,13},{2,6},{6,10},{10,14},{3,7},{... | collective-permute-start | bytes 73736 | tf_op jit(solution)/shard_map/ppermute | solution.py:17
  6.4 22.9 %collective-permute-start.2 = (f32[3,1,16,128]{3,2,1,0:T(8,128)S(1)}, f32[3,1,16,128]{3,2,1,0:T(8,128)S(1)}, u32[]{:S(2)}, u32[]{:S(2)}) collective-permute-start(f32[3,1,16,128]{3,2,1,0:T(8,128)S(1)} %get-tuple-element.59), channel_id=1, source_target_pairs={{4,0},{8,4},{12,8},{5,1},{9,5},{13,9},{6,2},{10,6},{14,10},{7,3},{... | collective-permute-start | bytes 73736 | tf_op jit(solution)/shard_map/ppermute | solution.py:19
  9.8 28.8 %collective-permute-start.1 = (f32[3,1,16,128]{3,0,2,1:T(4,128)S(1)}, f32[3,1,16,128]{3,0,2,1:T(4,128)S(1)}, u32[]{:S(2)}, u32[]{:S(2)}) collective-permute-start(f32[3,1,16,128]{3,0,2,1:T(4,128)S(1)} %get-tuple-element.53), channel_id=1, source_target_pairs={{0,4},{4,8},{8,12},{1,5},{5,9},{9,13},{2,6},{6,10},{10,14},{3,7},{... | collective-permute-start | bytes 73736 | tf_op jit(solution)/shard_map/ppermute | solution.py:17
  16.8 31.3 %copy-start.45 = (s32[128]{0:T(128)}, s32[128]{0:T(128)S(1)}, u32[]{:S(2)}) copy-start(s32[128]{0:T(128)S(1)} %fusion.125) | copy-start | bytes 1540
  18.6 50.1 %all-to-all-start = ((s32[8,1,32]{2,1,0:T(1,128)}), s32[8,1,32]{2,1,0:T(1,128)S(1)}, u32[]{:S(2)}, u32[]{:S(2)}) async-start(s32[8,1,32]{2,1,0:T(1,128)} %all_to_all.30), calls=%async_computation | async-start | bytes 8192 | tf_op jit(solution)/shard_map/all_to_all | solution.py:74
  23.4 16.4 %collective-permute-start.3 = (f32[3,1,16,128]{3,0,2,1:T(4,128)S(1)}, f32[3,1,16,128]{3,0,2,1:T(4,128)S(1)}, u32[]{:S(2)}, u32[]{:S(2)}) collective-permute-start(f32[3,1,16,128]{3,0,2,1:T(4,128)S(1)} %get-tuple-element.52), channel_id=1, source_target_pairs={{4,0},{8,4},{12,8},{5,1},{9,5},{13,9},{6,2},{10,6},{14,10},{7,3},{... | collective-permute-start | bytes 73736 | tf_op jit(solution)/shard_map/ppermute | solution.py:19
  27.0 24.4 %copy-start.41 = (pred[128]{0:T(512)(128)(4,1)}, pred[128]{0:T(512)(128)(4,1)S(1)}, u32[]{:S(2)}) copy-start(pred[128]{0:T(512)(128)(4,1)S(1)} %compare_and_fusion.1) | copy-start | bytes 388
  33.3 14.7 %collective-permute-start.4 = (f32[3,18,1,128]{3,1,2,0:T(8,128)S(1)}, f32[3,18,1,128]{3,1,2,0:T(8,128)S(1)}, u32[]{:S(2)}, u32[]{:S(2)}) collective-permute-start(f32[3,18,1,128]{3,1,2,0:T(8,128)S(1)} %copy.132), channel_id=1, source_target_pairs={{0,2},{1,3},{4,6},{5,7},{8,10},{9,11},{12,14},{13,15},{16,18},{17,... | collective-permute-start | bytes 82952 | tf_op jit(solution)/shard_map/ppermute | solution.py:17
  37.3 14.2 %collective-permute-start.6 = (f32[3,18,1,128]{3,1,2,0:T(8,128)S(1)}, f32[3,18,1,128]{3,1,2,0:T(8,128)S(1)}, u32[]{:S(2)}, u32[]{:S(2)}) collective-permute-start(f32[3,18,1,128]{3,1,2,0:T(8,128)S(1)} %copy.133), channel_id=1, source_target_pairs={{2,0},{3,1},{6,4},{7,5},{10,8},{11,9},{14,12},{15,13},{18,16},{19,... | collective-permute-start | bytes 82952 | tf_op jit(solution)/shard_map/ppermute | solution.py:19
  40.4 28.0 %collective-permute-start.5 = (f32[3,18,1,128]{3,0,2,1:T(4,128)S(1)}, f32[3,18,1,128]{3,0,2,1:T(4,128)S(1)}, u32[]{:S(2)}, u32[]{:S(2)}) collective-permute-start(f32[3,18,1,128]{3,0,2,1:T(4,128)S(1)} %get-tuple-element.44), channel_id=1, source_target_pairs={{0,2},{1,3},{4,6},{5,7},{8,10},{9,11},{12,14},{13,15},{16,18},{17,... | collective-permute-start | bytes 82952 | tf_op jit(solution)/shard_map/ppermute | solution.py:17
  45.0 23.5 %collective-permute-start.7 = (f32[3,18,1,128]{3,0,2,1:T(4,128)S(1)}, f32[3,18,1,128]{3,0,2,1:T(4,128)S(1)}, u32[]{:S(2)}, u32[]{:S(2)}) collective-permute-start(f32[3,18,1,128]{3,0,2,1:T(4,128)S(1)} %get-tuple-element.45), channel_id=1, source_target_pairs={{2,0},{3,1},{6,4},{7,5},{10,8},{11,9},{14,12},{15,13},{18,16},{19,... | collective-permute-start | bytes 82952 | tf_op jit(solution)/shard_map/ppermute | solution.py:19
  65.2 23.6 %collective-permute-start.8 = (f32[3,18,18,1]{2,1,3,0:T(8,128)}, f32[3,18,18,1]{2,1,3,0:T(8,128)}, u32[]{:S(2)}, u32[]{:S(2)}) collective-permute-start(f32[3,18,18,1]{2,1,3,0:T(8,128)} %get-tuple-element.29), channel_id=1, source_target_pairs={{0,1},{2,3},{4,5},{6,7},{8,9},{10,11},{12,13},{14,15},{16,17},{18,... | collective-permute-start | bytes 11672 | tf_op jit(solution)/shard_map/ppermute | solution.py:17
  67.1 23.7 %collective-permute-start.10 = (f32[3,18,18,1]{2,1,3,0:T(8,128)}, f32[3,18,18,1]{2,1,3,0:T(8,128)}, u32[]{:S(2)}, u32[]{:S(2)}) collective-permute-start(f32[3,18,18,1]{2,1,3,0:T(8,128)} %get-tuple-element.28), channel_id=1, source_target_pairs={{1,0},{3,2},{5,4},{7,6},{9,8},{11,10},{13,12},{15,14},{17,16},{19,... | collective-permute-start | bytes 11672 | tf_op jit(solution)/shard_map/ppermute | solution.py:19
  69.1 26.6 %all-to-all-start.1 = ((f32[8,32,128]{2,1,0:T(8,128)}), f32[8,32,128]{2,1,0:T(8,128)}, u32[]{:S(2)}, u32[]{:S(2)}) async-start(f32[8,32,128]{2,1,0:T(8,128)} %bitcast.15), calls=%async_computation.1 | async-start | bytes 262144 | tf_op jit(solution)/shard_map/all_to_all | solution.py:87
  77.7 15.2 %collective-permute-start.9 = (f32[3,18,18,1]{2,3,1,0:T(1,128)S(1)}, f32[3,18,18,1]{2,3,1,0:T(1,128)S(1)}, u32[]{:S(2)}, u32[]{:S(2)}) collective-permute-start(f32[3,18,18,1]{2,3,1,0:T(1,128)S(1)} %copy.111), channel_id=1, source_target_pairs={{0,1},{2,3},{4,5},{6,7},{8,9},{10,11},{12,13},{14,15},{16,17},{18,... | collective-permute-start | bytes 11672 | tf_op jit(solution)/shard_map/ppermute | solution.py:17
  81.1 22.4 %copy-start.2 = (f32[3,16,16,128]{3,2,1,0:T(8,128)S(1)}, f32[3,16,16,128]{3,2,1,0:T(8,128)}, u32[]{:S(2)}) copy-start(f32[3,16,16,128]{3,2,1,0:T(8,128)} %param.12) | copy-start | bytes 1179652
  81.1 22.4 %copy-start.31 = (f32[3,1,16,128]{3,2,1,0:T(8,128)S(1)}, f32[3,1,16,128]{3,2,1,0:T(8,128)}, u32[]{:S(2)}) copy-start(f32[3,1,16,128]{3,2,1,0:T(8,128)} %copy-done.30) | copy-start | bytes 73732
  81.1 22.4 %copy-start.33 = (f32[3,1,16,128]{3,2,1,0:T(8,128)S(1)}, f32[3,1,16,128]{3,2,1,0:T(8,128)}, u32[]{:S(2)}) copy-start(f32[3,1,16,128]{3,2,1,0:T(8,128)} %copy-done.32) | copy-start | bytes 73732
  81.5 21.9 %copy-start.6 = (f32[3,18,16,128]{3,2,1,0:T(8,128)S(1)}, f32[3,18,16,128]{3,2,1,0:T(8,128)}, u32[]{:S(2)}) copy-start(f32[3,18,16,128]{3,2,1,0:T(8,128)} %copy-done.5) | copy-start | bytes 1327108
  81.5 12.7 %collective-permute-start.11 = (f32[3,18,18,1]{2,3,1,0:T(1,128)S(1)}, f32[3,18,18,1]{2,3,1,0:T(1,128)S(1)}, u32[]{:S(2)}, u32[]{:S(2)}) collective-permute-start(f32[3,18,18,1]{2,3,1,0:T(1,128)S(1)} %copy.115), channel_id=1, source_target_pairs={{1,0},{3,2},{5,4},{7,6},{9,8},{11,10},{13,12},{15,14},{17,16},{19,... | collective-permute-start | bytes 11672 | tf_op jit(solution)/shard_map/ppermute | solution.py:19
  83.0 28.7 %copy-start.27 = (s32[1024]{0:T(1024)}, s32[1024]{0:T(1024)S(1)}, u32[]{:S(2)}) copy-start(s32[1024]{0:T(1024)S(1)} %pad_clamp_fusion) | copy-start | bytes 12292
  84.3 54.7 %copy-start.34 = (s32[256]{0:T(256)}, s32[256]{0:T(256)S(1)}, u32[]{:S(2)}) copy-start(s32[256]{0:T(256)S(1)} %eq.51) | copy-start | bytes 3076
  88.7 23.0 %copy-start.38 = (pred[128]{0:T(512)(128)(4,1)S(1)}, pred[128]{0:T(512)(128)(4,1)}, u32[]{:S(2)}) copy-start(pred[128]{0:T(512)(128)(4,1)} %get-tuple-element.19) | copy-start | bytes 388
  88.7 24.6 %copy-start.7 = (f32[16,16,128]{2,1,0:T(8,128)S(1)}, f32[16,16,128]{2,1,0:T(8,128)}, u32[]{:S(2)}) copy-start(f32[16,16,128]{2,1,0:T(8,128)} %param.13) | copy-start | bytes 393220
  97.7 13.9 %all-to-all-start.2 = ((f32[8,32,128]{2,1,0:T(8,128)}), f32[8,32,128]{2,1,0:T(8,128)S(1)}, u32[]{:S(2)}, u32[]{:S(2)}) async-start(f32[8,32,128]{2,1,0:T(8,128)} %bitcast.17), calls=%async_computation.2 | async-start | bytes 262144 | tf_op jit(solution)/shard_map/all_to_all | solution.py:98
  105.0 33.8 %copy-start.36 = (f32[8,128]{1,0:T(8,128)S(1)}, f32[8,128]{1,0:T(8,128)}, u32[]{:S(2)}) copy-start(f32[8,128]{1,0:T(8,128)} %param.19) | copy-start | bytes 12292
  118.2 10.6 %collective-permute-start.12 = (f32[3,1,16,128]{3,0,2,1:T(4,128)S(1)}, f32[3,1,16,128]{3,0,2,1:T(4,128)S(1)}, u32[]{:S(2)}, u32[]{:S(2)}) collective-permute-start(f32[3,1,16,128]{3,0,2,1:T(4,128)S(1)} %get-tuple-element.50), channel_id=1, source_target_pairs={{0,4},{4,8},{8,12},{1,5},{5,9},{9,13},{2,6},{6,10},{10,14},{3,7},{... | collective-permute-start | bytes 73736 | tf_op jit(solution)/shard_map/ppermute | solution.py:17
  120.0 8.8 %collective-permute-start.13 = (f32[3,1,16,128]{3,0,2,1:T(4,128)S(1)}, f32[3,1,16,128]{3,0,2,1:T(4,128)S(1)}, u32[]{:S(2)}, u32[]{:S(2)}) collective-permute-start(f32[3,1,16,128]{3,0,2,1:T(4,128)S(1)} %get-tuple-element.51), channel_id=1, source_target_pairs={{4,0},{8,4},{12,8},{5,1},{9,5},{13,9},{6,2},{10,6},{14,10},{7,3},{... | collective-permute-start | bytes 73736 | tf_op jit(solution)/shard_map/ppermute | solution.py:19
  123.3 15.5 %all-to-all-start.3 = ((f32[8,32,128]{2,1,0:T(8,128)}), f32[8,32,128]{2,1,0:T(8,128)S(1)}, u32[]{:S(2)}, u32[]{:S(2)}) async-start(f32[8,32,128]{2,1,0:T(8,128)} %bitcast.22), calls=%async_computation.3 | async-start | bytes 262144 | tf_op jit(solution)/shard_map/all_to_all | solution.py:87
  128.8 22.8 %copy-start.10 = (f32[3,1,16,128]{3,0,2,1:T(4,128)}, f32[3,1,16,128]{3,0,2,1:T(4,128)S(1)}, u32[]{:S(2)}) copy-start(f32[3,1,16,128]{3,0,2,1:T(4,128)S(1)} %collective-permute-done.12) | copy-start | bytes 73732
  128.8 22.8 %copy-start.12 = (f32[3,1,16,128]{3,0,2,1:T(4,128)}, f32[3,1,16,128]{3,0,2,1:T(4,128)S(1)}, u32[]{:S(2)}) copy-start(f32[3,1,16,128]{3,0,2,1:T(4,128)S(1)} %collective-permute-done.13) | copy-start | bytes 73732
  128.9 5.5 %collective-permute-start.14 = (f32[3,18,1,128]{3,0,2,1:T(4,128)S(1)}, f32[3,18,1,128]{3,0,2,1:T(4,128)S(1)}, u32[]{:S(2)}, u32[]{:S(2)}) collective-permute-start(f32[3,18,1,128]{3,0,2,1:T(4,128)S(1)} %get-tuple-element.42), channel_id=1, source_target_pairs={{0,2},{1,3},{4,6},{5,7},{8,10},{9,11},{12,14},{13,15},{16,18},{17,... | collective-permute-start | bytes 82952 | tf_op jit(solution)/shard_map/ppermute | solution.py:17
  132.8 5.9 %collective-permute-start.15 = (f32[3,18,1,128]{3,0,2,1:T(4,128)S(1)}, f32[3,18,1,128]{3,0,2,1:T(4,128)S(1)}, u32[]{:S(2)}, u32[]{:S(2)}) collective-permute-start(f32[3,18,1,128]{3,0,2,1:T(4,128)S(1)} %get-tuple-element.43), channel_id=1, source_target_pairs={{2,0},{3,1},{6,4},{7,5},{10,8},{11,9},{14,12},{15,13},{18,16},{19,... | collective-permute-start | bytes 82952 | tf_op jit(solution)/shard_map/ppermute | solution.py:19
  140.0 14.9 %all-to-all-start.4 = ((f32[8,32,128]{2,1,0:T(8,128)}), f32[8,32,128]{2,1,0:T(8,128)}, u32[]{:S(2)}, u32[]{:S(2)}) async-start(f32[8,32,128]{2,1,0:T(8,128)} %bitcast.24), calls=%async_computation.4 | async-start | bytes 262144 | tf_op jit(solution)/shard_map/all_to_all | solution.py:98
  147.5 4.1 %collective-permute-start.16 = (f32[3,18,18,1]{2,3,1,0:T(1,128)S(1)}, f32[3,18,18,1]{2,3,1,0:T(1,128)S(1)}, u32[]{:S(2)}, u32[]{:S(2)}) collective-permute-start(f32[3,18,18,1]{2,3,1,0:T(1,128)S(1)} %copy.118), channel_id=1, source_target_pairs={{0,1},{2,3},{4,5},{6,7},{8,9},{10,11},{12,13},{14,15},{16,17},{18,... | collective-permute-start | bytes 11672 | tf_op jit(solution)/shard_map/ppermute | solution.py:17
  150.3 3.1 %collective-permute-start.17 = (f32[3,18,18,1]{2,3,1,0:T(1,128)S(1)}, f32[3,18,18,1]{2,3,1,0:T(1,128)S(1)}, u32[]{:S(2)}, u32[]{:S(2)}) collective-permute-start(f32[3,18,18,1]{2,3,1,0:T(1,128)S(1)} %copy.120), channel_id=1, source_target_pairs={{1,0},{3,2},{5,4},{7,6},{9,8},{11,10},{13,12},{15,14},{17,16},{19,... | collective-permute-start | bytes 11672 | tf_op jit(solution)/shard_map/ppermute | solution.py:19
  161.9 41.2 %copy-start.28 = (s32[1024]{0:T(1024)S(1)}, s32[1024]{0:T(1024)}, u32[]{:S(2)}) copy-start(s32[1024]{0:T(1024)} %copy-done.27) | copy-start | bytes 12292
  161.9 41.2 %copy-start.39 = (pred[128]{0:T(512)(128)(4,1)S(1)}, pred[128]{0:T(512)(128)(4,1)}, u32[]{:S(2)}) copy-start(pred[128]{0:T(512)(128)(4,1)} %get-tuple-element.19) | copy-start | bytes 388
  162.0 13.8 %collective-permute-start.18 = (f32[3,1,16,128]{3,0,2,1:T(4,128)S(1)}, f32[3,1,16,128]{3,0,2,1:T(4,128)S(1)}, u32[]{:S(2)}, u32[]{:S(2)}) collective-permute-start(f32[3,1,16,128]{3,0,2,1:T(4,128)S(1)} %get-tuple-element.48), channel_id=1, source_target_pairs={{0,4},{4,8},{8,12},{1,5},{5,9},{9,13},{2,6},{6,10},{10,14},{3,7},{... | collective-permute-start | bytes 73736 | tf_op jit(solution)/shard_map/ppermute | solution.py:17
  165.9 9.9 %collective-permute-start.19 = (f32[3,1,16,128]{3,0,2,1:T(4,128)S(1)}, f32[3,1,16,128]{3,0,2,1:T(4,128)S(1)}, u32[]{:S(2)}, u32[]{:S(2)}) collective-permute-start(f32[3,1,16,128]{3,0,2,1:T(4,128)S(1)} %get-tuple-element.49), channel_id=1, source_target_pairs={{4,0},{8,4},{12,8},{5,1},{9,5},{13,9},{6,2},{10,6},{14,10},{7,3},{... | collective-permute-start | bytes 73736 | tf_op jit(solution)/shard_map/ppermute | solution.py:19
  169.2 16.6 %all-to-all-start.5 = ((f32[8,32,128]{2,1,0:T(8,128)}), f32[8,32,128]{2,1,0:T(8,128)S(1)}, u32[]{:S(2)}, u32[]{:S(2)}) async-start(f32[8,32,128]{2,1,0:T(8,128)} %bitcast.28), calls=%async_computation.5 | async-start | bytes 262144 | tf_op jit(solution)/shard_map/all_to_all | solution.py:87
  175.8 29.6 %copy-start.11 = (f32[3,1,16,128]{3,0,2,1:T(4,128)}, f32[3,1,16,128]{3,0,2,1:T(4,128)S(1)}, u32[]{:S(2)}) copy-start(f32[3,1,16,128]{3,0,2,1:T(4,128)S(1)} %collective-permute-done.18) | copy-start | bytes 73732
  175.8 29.6 %copy-start.13 = (f32[3,1,16,128]{3,0,2,1:T(4,128)}, f32[3,1,16,128]{3,0,2,1:T(4,128)S(1)}, u32[]{:S(2)}) copy-start(f32[3,1,16,128]{3,0,2,1:T(4,128)S(1)} %collective-permute-done.19) | copy-start | bytes 73732
  175.9 5.5 %collective-permute-start.20 = (f32[3,18,1,128]{3,0,2,1:T(4,128)S(1)}, f32[3,18,1,128]{3,0,2,1:T(4,128)S(1)}, u32[]{:S(2)}, u32[]{:S(2)}) collective-permute-start(f32[3,18,1,128]{3,0,2,1:T(4,128)S(1)} %get-tuple-element.40), channel_id=1, source_target_pairs={{0,2},{1,3},{4,6},{5,7},{8,10},{9,11},{12,14},{13,15},{16,18},{17,... | collective-permute-start | bytes 82952 | tf_op jit(solution)/shard_map/ppermute | solution.py:17
  179.8 5.9 %collective-permute-start.21 = (f32[3,18,1,128]{3,0,2,1:T(4,128)S(1)}, f32[3,18,1,128]{3,0,2,1:T(4,128)S(1)}, u32[]{:S(2)}, u32[]{:S(2)}) collective-permute-start(f32[3,18,1,128]{3,0,2,1:T(4,128)S(1)} %get-tuple-element.41), channel_id=1, source_target_pairs={{2,0},{3,1},{6,4},{7,5},{10,8},{11,9},{14,12},{15,13},{18,16},{19,... | collective-permute-start | bytes 82952 | tf_op jit(solution)/shard_map/ppermute | solution.py:19
  181.4 24.0 %copy-start.21 = (f32[3,18,1,128]{3,0,2,1:T(4,128)}, f32[3,18,1,128]{3,0,2,1:T(4,128)S(1)}, u32[]{:S(2)}) copy-start(f32[3,18,1,128]{3,0,2,1:T(4,128)S(1)} %collective-permute-done.20) | copy-start | bytes 82948
  185.6 19.7 %copy-start.23 = (f32[3,18,1,128]{3,0,2,1:T(4,128)}, f32[3,18,1,128]{3,0,2,1:T(4,128)S(1)}, u32[]{:S(2)}) copy-start(f32[3,18,1,128]{3,0,2,1:T(4,128)S(1)} %collective-permute-done.21) | copy-start | bytes 82948
  188.3 14.9 %all-to-all-start.6 = ((f32[8,32,128]{2,1,0:T(8,128)}), f32[8,32,128]{2,1,0:T(8,128)S(1)}, u32[]{:S(2)}, u32[]{:S(2)}) async-start(f32[8,32,128]{2,1,0:T(8,128)} %bitcast.30), calls=%async_computation.6 | async-start | bytes 262144 | tf_op jit(solution)/shard_map/all_to_all | solution.py:98
  195.9 4.3 %collective-permute-start.22 = (f32[3,18,18,1]{2,3,1,0:T(1,128)S(1)}, f32[3,18,18,1]{2,3,1,0:T(1,128)S(1)}, u32[]{:S(2)}, u32[]{:S(2)}) collective-permute-start(f32[3,18,18,1]{2,3,1,0:T(1,128)S(1)} %copy.122), channel_id=1, source_target_pairs={{0,1},{2,3},{4,5},{6,7},{8,9},{10,11},{12,13},{14,15},{16,17},{18,... | collective-permute-start | bytes 11672 | tf_op jit(solution)/shard_map/ppermute | solution.py:17
  198.7 3.1 %collective-permute-start.23 = (f32[3,18,18,1]{2,3,1,0:T(1,128)S(1)}, f32[3,18,18,1]{2,3,1,0:T(1,128)S(1)}, u32[]{:S(2)}, u32[]{:S(2)}) collective-permute-start(f32[3,18,18,1]{2,3,1,0:T(1,128)S(1)} %copy.124), channel_id=1, source_target_pairs={{1,0},{3,2},{5,4},{7,6},{9,8},{11,10},{13,12},{15,14},{17,16},{19,... | collective-permute-start | bytes 11672 | tf_op jit(solution)/shard_map/ppermute | solution.py:19
  209.3 41.2 %copy-start.29 = (s32[1024]{0:T(1024)S(1)}, s32[1024]{0:T(1024)}, u32[]{:S(2)}) copy-start(s32[1024]{0:T(1024)} %copy-done.27) | copy-start | bytes 12292
  209.3 41.2 %copy-start.40 = (pred[128]{0:T(512)(128)(4,1)S(1)}, pred[128]{0:T(512)(128)(4,1)}, u32[]{:S(2)}) copy-start(pred[128]{0:T(512)(128)(4,1)} %get-tuple-element.19) | copy-start | bytes 388
  209.3 13.8 %collective-permute-start.24 = (f32[3,1,16,128]{3,0,2,1:T(4,128)S(1)}, f32[3,1,16,128]{3,0,2,1:T(4,128)S(1)}, u32[]{:S(2)}, u32[]{:S(2)}) collective-permute-start(f32[3,1,16,128]{3,0,2,1:T(4,128)S(1)} %get-tuple-element.46), channel_id=1, source_target_pairs={{0,4},{4,8},{8,12},{1,5},{5,9},{9,13},{2,6},{6,10},{10,14},{3,7},{... | collective-permute-start | bytes 73736 | tf_op jit(solution)/shard_map/ppermute | solution.py:17
  213.3 9.9 %collective-permute-start.25 = (f32[3,1,16,128]{3,0,2,1:T(4,128)S(1)}, f32[3,1,16,128]{3,0,2,1:T(4,128)S(1)}, u32[]{:S(2)}, u32[]{:S(2)}) collective-permute-start(f32[3,1,16,128]{3,0,2,1:T(4,128)S(1)} %get-tuple-element.47), channel_id=1, source_target_pairs={{4,0},{8,4},{12,8},{5,1},{9,5},{13,9},{6,2},{10,6},{14,10},{7,3},{... | collective-permute-start | bytes 73736 | tf_op jit(solution)/shard_map/ppermute | solution.py:19
  216.5 16.6 %all-to-all-start.7 = ((f32[8,32,128]{2,1,0:T(8,128)}), f32[8,32,128]{2,1,0:T(8,128)S(1)}, u32[]{:S(2)}, u32[]{:S(2)}) async-start(f32[8,32,128]{2,1,0:T(8,128)} %bitcast.34), calls=%async_computation.7 | async-start | bytes 262144 | tf_op jit(solution)/shard_map/all_to_all | solution.py:87
  223.2 5.5 %collective-permute-start.26 = (f32[3,18,1,128]{3,0,2,1:T(4,128)S(1)}, f32[3,18,1,128]{3,0,2,1:T(4,128)S(1)}, u32[]{:S(2)}, u32[]{:S(2)}) collective-permute-start(f32[3,18,1,128]{3,0,2,1:T(4,128)S(1)} %get-tuple-element.38), channel_id=1, source_target_pairs={{0,2},{1,3},{4,6},{5,7},{8,10},{9,11},{12,14},{13,15},{16,18},{17,... | collective-permute-start | bytes 82952 | tf_op jit(solution)/shard_map/ppermute | solution.py:17
  227.2 5.9 %collective-permute-start.27 = (f32[3,18,1,128]{3,0,2,1:T(4,128)S(1)}, f32[3,18,1,128]{3,0,2,1:T(4,128)S(1)}, u32[]{:S(2)}, u32[]{:S(2)}) collective-permute-start(f32[3,18,1,128]{3,0,2,1:T(4,128)S(1)} %get-tuple-element.39), channel_id=1, source_target_pairs={{2,0},{3,1},{6,4},{7,5},{10,8},{11,9},{14,12},{15,13},{18,16},{19,... | collective-permute-start | bytes 82952 | tf_op jit(solution)/shard_map/ppermute | solution.py:19
  234.0 21.5 %copy-start.37 = (f32[8,128]{1,0:T(8,128)}, f32[8,128]{1,0:T(8,128)S(1)}, u32[]{:S(2)}) copy-start(f32[8,128]{1,0:T(8,128)S(1)} %fusion.110) | copy-start | bytes 12292
  235.7 14.9 %all-to-all-start.8 = ((f32[8,32,128]{2,1,0:T(8,128)}), f32[8,32,128]{2,1,0:T(8,128)S(1)}, u32[]{:S(2)}, u32[]{:S(2)}) async-start(f32[8,32,128]{2,1,0:T(8,128)} %bitcast.36), calls=%async_computation.8 | async-start | bytes 262144 | tf_op jit(solution)/shard_map/all_to_all | solution.py:98
  243.3 4.1 %collective-permute-start.28 = (f32[3,18,18,1]{2,3,1,0:T(1,128)S(1)}, f32[3,18,18,1]{2,3,1,0:T(1,128)S(1)}, u32[]{:S(2)}, u32[]{:S(2)}) collective-permute-start(f32[3,18,18,1]{2,3,1,0:T(1,128)S(1)} %copy.126), channel_id=1, source_target_pairs={{0,1},{2,3},{4,5},{6,7},{8,9},{10,11},{12,13},{14,15},{16,17},{18,... | collective-permute-start | bytes 11672 | tf_op jit(solution)/shard_map/ppermute | solution.py:17
  246.1 3.1 %collective-permute-start.29 = (f32[3,18,18,1]{2,3,1,0:T(1,128)S(1)}, f32[3,18,18,1]{2,3,1,0:T(1,128)S(1)}, u32[]{:S(2)}, u32[]{:S(2)}) collective-permute-start(f32[3,18,18,1]{2,3,1,0:T(1,128)S(1)} %copy.128), channel_id=1, source_target_pairs={{1,0},{3,2},{5,4},{7,6},{9,8},{11,10},{13,12},{15,14},{17,16},{19,... | collective-permute-start | bytes 11672 | tf_op jit(solution)/shard_map/ppermute | solution.py:19
  (21 other events, 170.5 us)
where the time goes:
time: 259 us; the launch traced here: 256 us
  starting transfers between devices  119 us (46%)
  local copies, waits for them, and re-layouts  54 us (21%)
  other arithmetic  48.7 us (19%)
  waiting for transfers between devices  23.8 us (9%)
  matrix products  9.22 us (4%)
    ppermute x15, starting transfers between devices, with_halo(): lax.ppermute(tail, axis, [(i, (i + 1) % count) for i in range(ends)])  48.4 us
    all_to_all x4, starting transfers between devices, local(): lax.all_to_all(outgoing.reshape(owners, capacity, layers), ('gx', 'gy'),...  26.6 us
    ppermute x15, starting transfers between devices, with_halo(): lax.ppermute(head, axis, [((i + 1) % count, i) for i in range(ends)])  19.7 us
    all_to_all x4, starting transfers between devices, local(): lax.all_to_all(returning.reshape(owners, capacity, layers), ('gx', 'gy'),...  19.3 us
    ppermute x15, waiting for transfers between devices, with_halo(): lax.ppermute(head, axis, [((i + 1) % count, i) for i in range(ends)])  16.2 us
    reduce_sum x3, other arithmetic, local(): jnp.sum(mobility_cols * adjoint.reshape(3, columns, layers), axis=0)  12.7 us
    ppermute x7, local copies, waits for them, and re-layouts, with_halo(): lax.ppermute(head, axis, [((i + 1) % count, i) for i in range(ends)])  11.1 us
    slice x13, local copies, waits for them, and re-layouts, with_halo(): lax.slice_in_dim(cells, cells.shape[dim] - width, cells.shape[dim], axis=...  10.8 us
  transfers between devices with their start and end apart: 39, of which 10 were waited for; matrix products, arithmetic and copies ran while one was open for 28% of the time, Pallas kernels for 0%

commit v1 on v0

v1 whole, which is shorter than its diff:
```python
import functools

import jax
import jax.numpy as jnp
from jax import lax
from jax.experimental import pallas as pl
from jax.experimental.pallas import tpu as pltpu
from jax.sharding import PartitionSpec as P

STEPS = 4
F32 = jnp.float32
BF16 = jnp.bfloat16
VMEM = pl.BlockSpec(memory_space=pltpu.VMEM)
SMEM = pl.BlockSpec(memory_space=pltpu.SMEM)
XM, XP, YM, YP, ZM, ZP, Y_ODD, X_ODD, OWNER = range(9)


def harmonic(first, second):
    return 2.0 * first * second / (first + second)


def split(value):
    high = value.astype(BF16)
    rest = value - high.astype(F32)
    middle = rest.astype(BF16)
    low = (rest - middle.astype(F32)).astype(BF16)
    return jnp.concatenate([high, middle, low], axis=1)


def counted(counts, value):
    n = value.shape[1]
    out = jnp.dot(counts, split(value), preferred_element_type=F32)
    return out[:, :n] + (out[:, n : 2 * n] + out[:, 2 * n :])


def start_kernel(
    info, table, adj, perm, rock, column, well, observed,
    mob, index, gain, counts, counts_t, target, msg_y, face_a, face_b, msg_z, combined,
):
    _, nx, ny, nz = adj.shape
    rocks = table.shape[0]
    wells = target.shape[0]
    own = observed.shape[0]
    rows = column.shape[1]
    y_odd = info[Y_ODD] == 1
    x_odd = info[X_ODD] == 1
    well_hit = (lax.broadcasted_iota(jnp.int32, (wells, rows), 0) == well[...]).astype(BF16)
    col_hit = (lax.broadcasted_iota(jnp.int32, (nx * ny, rows), 0) == column[...]).astype(BF16)
    contract = (((1,), (1,)), ((), ()))
    count = lax.dot_general(well_hit, col_hit, contract, preferred_element_type=F32).astype(BF16)
    counts[...] = count
    counts_t[...] = lax.dot_general(
        col_hit, well_hit, contract, preferred_element_type=F32
    ).astype(BF16)
    target[...] = jnp.zeros_like(target)
    target[pl.ds(pl.multiple_of(info[OWNER] * own, own), own), :] = observed[...]
    for x in range(nx):
        kind = rock[x]
        root = jnp.sqrt(perm[0, x] * perm[1, x])
        wi = root / (1.0 + root)
        index[x] = wi
        total = jnp.zeros((ny, nz), F32)
        for p in range(3):
            m = jnp.full((ny, nz), table[0, p], F32)
            for r in range(1, rocks):
                m = jnp.where(kind == r, table[r, p], m)
            mob[p, x] = m
            g = 0.25 * wi * m
            gain[p, x] = g
            total = total + g * adj[p, x]
            msg_z[p, x] = adj[p, x]
            row = wells + p * nx + x
            msg_y[row : row + 1, :] = jnp.where(
                y_odd, adj[p, x, 0:1, :], adj[p, x, ny - 1 : ny, :]
            )
        msg_z[3, x] = perm[2, x]
        row = wells + 3 * nx + x
        msg_y[row : row + 1, :] = jnp.where(
            y_odd, perm[1, x, 0:1, :], perm[1, x, ny - 1 : ny, :]
        )
        combined[x * ny : (x + 1) * ny, :] = total
    for p in range(4):
        low = adj[p, 0] if p < 3 else perm[0, 0]
        high = adj[p, nx - 1] if p < 3 else perm[0, nx - 1]
        face_a[p * ny : (p + 1) * ny, :] = jnp.where(x_odd, low, high)
        face_b[p * ny : (p + 1) * ny, :] = jnp.where(x_odd, high, low)
    msg_y[0:wells, :] = counted(count, combined[...]) - target[...]


def sweep_kernel(first, last, refs_in, *refs):
    names = refs_in
    r = dict(zip(names, refs))
    info, adj = r["info"], r["adj"]
    _, nx, ny, nz = adj.shape
    wells = r["target"].shape[0]
    y_odd = info[Y_ODD] == 1
    x_odd = info[X_ODD] == 1
    total = r["sum0"][...]
    for name in names:
        if name.startswith("more"):
            total = total + r[name][0:wells, :]
    column_sum = counted(r["counts_t"][...], jnp.tanh(total))
    lane = lax.broadcasted_iota(jnp.int32, (ny, nz), 1)
    sub = lax.broadcasted_iota(jnp.int32, (ny, nz), 0)
    at_first, at_last = lane == 0, lane == nz - 1
    top, bottom = sub == 0, sub == ny - 1

    y0 = r["ym"].shape[0] - (4 if first else 3) * nx
    x0 = r["xm"].shape[0] - (4 if first else 3) * ny

    def y_minus(value, p, x):
        edge = r["ym"][y0 + p * nx + x : y0 + p * nx + x + 1, :]
        return jnp.where(top, edge, pltpu.roll(value, 1, 0))

    def y_plus(value, p, x):
        edge = r["yp"][y0 + p * nx + x : y0 + p * nx + x + 1, :]
        return jnp.where(bottom, edge, pltpu.roll(value, ny - 1, 0))

    def z_minus(value, p, x):
        return pltpu.roll(jnp.where(at_last, r["zm"][p, x], value), 1, 1)

    def z_plus(value, p, x):
        return pltpu.roll(jnp.where(at_first, r["zp"][p, x], value), nz - 1, 1)

    def x_face(name, p):
        return r[name][x0 + p * ny : x0 + (p + 1) * ny, :]

    for x in range(nx):
        if first:
            perm = r["perm"]
            k = perm[0, x]
            km = perm[0, x - 1] if x else jnp.where(info[XM] == 1, x_face("xm", 3), 0.0)
            kp = perm[0, x + 1] if x < nx - 1 else jnp.where(info[XP] == 1, x_face("xp", 3), 0.0)
            txm, txp = harmonic(k, km), harmonic(k, kp)
            k = perm[1, x]
            km, kp = y_minus(k, 3, x), y_plus(k, 3, x)
            tym = harmonic(k, jnp.where(top & (info[YM] == 0), 0.0, km))
            typ = harmonic(k, jnp.where(bottom & (info[YP] == 0), 0.0, kp))
            k = perm[2, x]
            km, kp = z_minus(k, 3, x), z_plus(k, 3, x)
            tzm = harmonic(k, jnp.where(at_first & (info[ZM] == 0), 0.0, km))
            tzp = harmonic(k, jnp.where(at_last & (info[ZP] == 0), 0.0, kp))
            weights = (txm, txp, tym, typ, tzm, tzp)
            for f, t in enumerate(weights):
                r["t_out"][f, x] = t
            weight_sum = txm + txp + tym + typ + tzm + tzp
            pore = r["pore"][x]
        else:
            weights = tuple(r["t"][f, x] for f in range(6))
        txm, txp, tym, typ, tzm, tzp = weights
        well_term = r["index"][x] * column_sum[x * ny : (x + 1) * ny, :]
        flow = jnp.zeros((ny, nz), F32)
        for p in range(3):
            if first:
                m = r["mob"][p, x]
                inverse = 1.0 / (pore + m * weight_sum)
                keep, take = pore * inverse, m * inverse
                r["keep_out"][p, x] = keep
                r["take_out"][p, x] = take
            else:
                keep, take = r["keep"][p, x], r["take"][p, x]
            value = adj[p, x]
            before = adj[p, x - 1] if x else x_face("xm", p)
            after = adj[p, x + 1] if x < nx - 1 else x_face("xp", p)
            beside = txm * before + txp * after
            beside = beside + tym * y_minus(value, p, x) + typ * y_plus(value, p, x)
            beside = beside + tzm * z_minus(value, p, x) + tzp * z_plus(value, p, x)
            new = keep * value + take * (beside + well_term)
            r["new"][p, x] = new
            if not last:
                flow = flow + r["gain"][p, x] * new
                row = wells + p * nx + x
                r["msg_y"][row : row + 1, :] = jnp.where(
                    y_odd, new[0:1, :], new[ny - 1 : ny, :]
                )
                if x == 0:
                    low = new
                    r["face_lo"][p * ny : (p + 1) * ny, :] = low
                if x == nx - 1:
                    low = r["face_lo"][p * ny : (p + 1) * ny, :]
                    r["face_a"][p * ny : (p + 1) * ny, :] = jnp.where(x_odd, low, new)
                    r["face_b"][p * ny : (p + 1) * ny, :] = jnp.where(x_odd, new, low)
        if not last:
            r["combined"][x * ny : (x + 1) * ny, :] = flow
    if last:
        sens = r["sens"]
        own = sens.shape[0]
        at = pl.ds(pl.multiple_of(info[OWNER] * own, own), own)
        summed = r["sum0"][at, :]
        for name in names:
            if name.startswith("more"):
                summed = summed + r[name][at, :]
        sens[...] = summed + r["target"][at, :]
    else:
        r["msg_y"][0:wells, :] = counted(r["counts"][...], r["combined"][...]) - r["target"][...]


def call(kernel, ins, outs, scratch):
    return pl.pallas_call(
        kernel,
        in_specs=[SMEM if smem else VMEM for smem, _ in ins],
        out_specs=[VMEM] * len(outs),
        out_shape=[jax.ShapeDtypeStruct(shape, kind) for shape, kind in outs],
        scratch_shapes=scratch,
        compiler_params=pltpu.CompilerParams(vmem_limit_bytes=40 * 1024 * 1024),
    )(*[array for _, array in ins])


def swap(count, bit):
    return [(i, i ^ bit) for i in range(count)]


def neighbours(low, high, axis):
    count = lax.axis_size(axis)
    before = lax.ppermute(high, axis, [(i, i + 1) for i in range(count - 1)])
    after = lax.ppermute(low, axis, [(i + 1, i) for i in range(count - 1)])
    return before, after


def summed_over(value, axis):
    count = lax.axis_size(axis)
    if count & (count - 1):
        return lax.psum(value, axis)
    bit = 1
    while bit < count:
        value = value + lax.ppermute(value, axis, swap(count, bit))
        bit *= 2
    return value


def exchange(msg_y, face_a, face_b, block, edges, wells, x_odd):
    size_x, size_y, size_z = (lax.axis_size(a) for a in ("gx", "gy", "wa"))
    if size_z == 2:
        zm = zp = lax.ppermute(block, "wa", swap(2, 1))
    else:
        zm, zp = neighbours(block, block, "wa")
    if size_y == 2:
        ym = yp = lax.ppermute(msg_y, "gy", swap(2, 1))
        total = msg_y[:wells] + ym[:wells]
    else:
        ym, yp = neighbours(*edges("y"), "gy")
        total = summed_over(msg_y[:wells], "gy")
    if size_x == 4:
        one = lax.ppermute(jnp.concatenate([total, face_a]), "gx", swap(4, 1))
        ring = lax.ppermute(jnp.concatenate([total, face_b]), "gx", swap(4, 3))
        two = lax.ppermute(total, "gx", swap(4, 2))
        sums = (total, one, ring, two)
        xm = jnp.where(x_odd, one[wells:], ring[wells:])
        xp = jnp.where(x_odd, ring[wells:], one[wells:])
    else:
        xm, xp = neighbours(*edges("x"), "gx")
        sums = (summed_over(total, "gx"),)
    return sums, xm, xp, ym, yp, zm, zp


def local(
    adjoint, permeability, pore_volume, rock_type, rock_table,
    perf_column, perf_owner, perf_slot, observed,
):
    size_x, size_y, size_z = (lax.axis_size(a) for a in ("gx", "gy", "wa"))
    gx, gy, wa = (lax.axis_index(a) for a in ("gx", "gy", "wa"))
    _, nx, ny, nz = adjoint.shape
    rows = perf_column.shape[0]
    own = observed.shape[0]
    wells = own * size_x * size_y
    cells = (nx, ny, nz)
    x_odd = gx % 2
    info = jnp.stack(
        [gx > 0, gx < size_x - 1, gy > 0, gy < size_y - 1, wa > 0, wa < size_z - 1,
         gy % 2, x_odd, gx * size_y + gy]
    ).astype(jnp.int32)
    well = perf_owner[:, 0] * own + perf_slot
    outs = [
        ((3,) + cells, F32), (cells, F32), ((3,) + cells, F32),
        ((wells, nx * ny), BF16), ((nx * ny, wells), BF16), ((wells, nz), F32),
        ((wells + 4 * nx, nz), F32), ((4 * ny, nz), F32), ((4 * ny, nz), F32),
        ((4,) + cells, F32),
    ]
    ins = [
        (True, info), (True, rock_table), (False, adjoint), (False, permeability),
        (False, rock_type), (False, perf_column.reshape(1, rows)),
        (False, well.reshape(1, rows)), (False, observed),
    ]
    mob, index, gain, counts, counts_t, target, msg_y, face_a, face_b, block = call(
        start_kernel, ins, outs, [pltpu.VMEM((nx * ny, nz), F32)]
    )

    def edges_of(parts_x, parts_y):
        def edges(axis):
            if axis == "x":
                return (
                    jnp.concatenate([a[0] for a in parts_x]),
                    jnp.concatenate([a[nx - 1] for a in parts_x]),
                )
            return (
                jnp.concatenate([a[:, 0] for a in parts_y]),
                jnp.concatenate([a[:, ny - 1] for a in parts_y]),
            )

        return edges

    phases = [adjoint[p] for p in range(3)]
    edges = edges_of(phases + [permeability[0]], phases + [permeability[1]])
    adj = adjoint
    for step in range(STEPS):
        first, last = step == 0, step == STEPS - 1
        sums, xm, xp, ym, yp, zm, zp = exchange(
            msg_y, face_a, face_b, block, edges, wells, x_odd == 1
        )
        ins = {"info": info, "adj": adj, "target": target, "counts_t": counts_t, "index": index}
        ins.update({("more%d" % i if i else "sum0"): s for i, s in enumerate(sums)})
        ins.update(xm=xm, xp=xp, ym=ym, yp=yp, zm=zm, zp=zp)
        if not last:
            ins.update(gain=gain, counts=counts)
        if first:
            ins.update(perm=permeability, pore=pore_volume, mob=mob)
        else:
            ins.update(t=weights, keep=keep, take=take)
        outs = {"new": ((3,) + cells, F32)}
        if last:
            outs["sens"] = ((own, nz), F32)
        else:
            outs["msg_y"] = ((wells + 3 * nx, nz), F32)
            outs["face_a"] = ((3 * ny, nz), F32)
            outs["face_b"] = ((3 * ny, nz), F32)
        if first:
            outs["t_out"] = ((6,) + cells, F32)
            outs["keep_out"] = ((3,) + cells, F32)
            outs["take_out"] = ((3,) + cells, F32)
        scratch = {} if last else {
            "combined": pltpu.VMEM((nx * ny, nz), F32),
            "face_lo": pltpu.VMEM((3 * ny, nz), F32),
        }
        names = tuple(ins) + tuple(outs) + tuple(scratch)
        result = call(
            functools.partial(sweep_kernel, first, last, names),
            [(name == "info", array) for name, array in ins.items()],
            list(outs.values()),
            list(scratch.values()),
        )
        result = dict(zip(outs, result))
        adj = block = result["new"]
        if first:
            weights, keep, take = (result[k] for k in ("t_out", "keep_out", "take_out"))
        if not last:
            msg_y, face_a, face_b = (result[k] for k in ("msg_y", "face_a", "face_b"))
            phases = [adj[p] for p in range(3)]
            edges = edges_of(phases, phases)
    return (adj, result["sens"])


def solution(mesh):
    cell = P(None, ("members", "gx"), "gy", "wa")
    flat = P(("members", "gx"), "gy", "wa")
    placed = (
        cell, cell, flat, flat, P(), P(("gx", "gy")), P(("gx", "gy"), None), P(("gx", "gy")),
        P(("gx", "gy"), "wa"),
    )
    return jax.shard_map(
        local,
        mesh=mesh,
        in_specs=placed,
        out_specs=(cell, P(("members", "gx", "gy"), "wa")),
        check_vma=False,
    )
```

time: 259 us -> 61.5 us (0.24)
  starting transfers between devices: 119 us -> 25.9 us
  local copies, waits for them, and re-layouts: 54 us -> 5.08 us
  other arithmetic: 48.7 us -> 0.1 us
  matrix products: 9.22 us -> 0 us
  Pallas kernels: 0 us -> 6.65 us
    all_to_all x9 -> x0, starting transfers between devices: 50.7 us -> none  [the longest x4 26.6 us: local(): lax.all_to_all(outgoing.reshape(owners, capacity, layers), ('gx', 'gy'),...]
    ppermute x30 -> x20, starting transfers between devices: 68.1 us -> 25.9 us  [the longest x4 10.4 us: exchange(): ring = lax.ppermute(jnp.concatenate([total, face_b]), 'gx', swap(4, 3))]
    ppermute x14 -> x0, local copies, waits for them, and re-layouts: 19.5 us -> none  [the longest x7 11.1 us: with_halo(): lax.ppermute(head, axis, [((i + 1) % count, i) for i in range(ends)])]
    slice x20 -> x0, local copies, waits for them, and re-layouts: 16.5 us -> none  [the longest x13 10.8 us: with_halo(): lax.slice_in_dim(cells, cells.shape[dim] - width, cells.shape[dim], axis=...]
    reduce_sum x4 -> x0, other arithmetic: 13.6 us -> none  [the longest x3 12.7 us: local(): jnp.sum(mobility_cols * adjoint.reshape(3, columns, layers), axis=0)]
    dot_general x9 -> x0, matrix products: 9.22 us -> none  [the longest x4 5.21 us: local(): returning = jnp.dot(slot_match.T, response, precision=lax.Precision.HIGHEST)]
    scatter-add x4 -> x0, other arithmetic: 8.64 us -> none  [local(): jnp.zeros((columns, layers), jnp.float32).at[perf_column].add(back_rows)]
    concatenate x5 -> x4, other arithmetic: 8.25 us -> 0.05 us  [exchange(): ring = lax.ppermute(jnp.concatenate([total, face_b]), 'gx', swap(4, 3))]
  transfers between devices with their start and end apart: 39 -> 20, of which waited for: 10 -> 16; matrix products, arithmetic and copies ran while one was open for 28% -> 0% of each run, Pallas kernels for 0% -> 0%
where the time goes in v1:
time: 61.5 us; the launch traced here: 61.2 us
  starting transfers between devices  25.9 us (42%)
  waiting for transfers between devices  22.8 us (37%)
  Pallas kernels  6.65 us (11%)
  local copies, waits for them, and re-layouts  5.08 us (8%)
  between operations  0.75 us (1%)
    ppermute x4, starting transfers between devices, exchange(): ring = lax.ppermute(jnp.concatenate([total, face_b]), 'gx', swap(4, 3))  10.4 us
    ppermute x4, waiting for transfers between devices, exchange(): ym = yp = lax.ppermute(msg_y, 'gy', swap(2, 1))  10.3 us
    ppermute x4, starting transfers between devices, exchange(): ym = yp = lax.ppermute(msg_y, 'gy', swap(2, 1))  7.67 us
    ppermute x4, waiting for transfers between devices, exchange(): ring = lax.ppermute(jnp.concatenate([total, face_b]), 'gx', swap(4, 3))  6.96 us
    ppermute x4, starting transfers between devices, exchange(): two = lax.ppermute(total, 'gx', swap(4, 2))  6.74 us
    pallas_call x5, Pallas kernels, call(): pl.pallas_call(kernel, in_specs=[SMEM if smem else VMEM for smem, _ in in...  6.65 us
    unnamed x23, local copies, waits for them, and re-layouts  4.99 us
    ppermute x4, waiting for transfers between devices, exchange(): one = lax.ppermute(jnp.concatenate([total, face_a]), 'gx', swap(4, 1))  3.29 us
  transfers between devices with their start and end apart: 20, of which 16 were waited for; matrix products, arithmetic and copies ran while one was open for 0% of the time, Pallas kernels for 0%

profile of v1, /device:TPU:0, one launch (start us, length us, event | category | flops | bytes accessed | tf_op | source)
XLA Modules:
  0.0 61.2 jit_solution(10725047322661457537)
XLA Ops:
  0.7 0.0 copy-start.8
  0.7 0.7 %copy-done.8 = f32[8,3]{0,1:T(4,128)S(1)} copy-done((f32[8,3]{0,1:T(4,128)S(1)}, f32[8,3]{0,1:T(4,128)}, u32[]{:S(2)}) %copy-start.8) | copy-done | bytes 120
  1.3 0.1 copy.11.table
  1.4 0.0 copy-start.9
  1.4 0.0 copy-start.10
  1.4 0.7 %copy-done.9 = s32[128]{0:T(128)S(1)} copy-done((s32[128]{0:T(128)S(1)}, s32[128]{0:T(128)}, u32[]{:S(2)}) %copy-start.9) | copy-done | bytes 536
  2.1 0.0 copy-done.10
  2.1 0.0 copy-start.6
  2.1 0.1 stack.63.info.refs_0_
  2.2 0.0 copy-start.7
  2.2 0.6 copy-done.6
  2.8 0.1 copy-done.7
  2.8 1.0 %copy-done = f32[3,16,16,128]{3,2,1,0:T(8,128)S(1)} copy-done((f32[3,16,16,128]{3,2,1,0:T(8,128)S(1)}, f32[3,16,16,128]{3,2,1,0:T(8,128)}, u32[]{:S(2)}) %copy-start) | copy-done | bytes 393240
  3.8 1.0 %copy-done.2 = f32[3,16,16,128]{3,2,1,0:T(8,128)S(1)} copy-done((f32[3,16,16,128]{3,2,1,0:T(8,128)S(1)}, f32[3,16,16,128]{3,2,1,0:T(8,128)}, u32[]{:S(2)}) %copy-start.2) | copy-done | bytes 393240
  4.8 0.9 %copy-done.5 = s32[16,16,128]{2,1,0:T(8,128)S(1)} copy-done((s32[16,16,128]{2,1,0:T(8,128)S(1)}, s32[16,16,128]{2,1,0:T(8,128)}, u32[]{:S(2)}) %copy-start.5) | copy-done | bytes 131096
  5.7 1.1 %shard_map.104 = (f32[3,16,16,128]{3,2,1,0:T(8,128)S(1)}, f32[16,16,128]{2,1,0:T(8,128)S(1)}, f32[3,16,16,128]{3,2,1,0:T(8,128)S(1)}, bf16[64,256]{1,0:T(8,128)(...) custom-call(s32[9]{0:T(128)S(1)} %stack.63.info.refs_0_, ...), custom_call_target="tpu_custom_call" | custom-call | tf_op jit(solution)/shard_map/pallas_call | solution.py:199
  6.8 0.0 copy-start.1
  6.8 3.0 %collective-permute-start = (f32[128,128]{1,0:T(8,128)S(1)}, f32[128,128]{1,0:T(8,128)S(1)}, u32[]{:S(2)}, u32[]{:S(2)}) collective-permute-start(f32[128,128]{1,0:T(8,128)S(1)} %get-tuple-element.30), channel_id=1, source_target_pairs={{0,2},{2,0},{1,3},{3,1},{4,6},{6,4},{5,7},{7,5},{8,10},{10,8},{9,1... | collective-permute-start | bytes 196616 | tf_op jit(solution)/shard_map/ppermute | solution.py:238
  9.8 0.0 collective-permute-start.4
  9.8 2.2 %collective-permute-done.refs_11_.refs_12_ = f32[128,128]{1,0:T(8,128)S(1)} collective-permute-done((f32[128,128]{1,0:T(8,128)S(1)}, f32[128,128]{1,0:T(8,128)S(1)}, u32[]{:S(2)}, u32[]{:S(2)}) %collective-permute-start) | collective-permute-done | bytes 65568 | tf_op jit(solution)/shard_map/ppermute | solution.py:238
  12.1 4.2 %collective-permute-start.2 = (f32[128,128]{1,0:T(8,128)S(1)}, f32[128,128]{1,0:T(8,128)S(1)}, u32[]{:S(2)}, u32[]{:S(2)}) collective-permute-start(f32[128,128]{1,0:T(8,128)S(1)} %get-tuple-element.66), channel_id=1, source_target_pairs={{0,12},{4,8},{8,4},{12,0},{1,13},{5,9},{9,5},{13,1},{2,14},{6,10},... | collective-permute-start | bytes 196616 | tf_op jit(solution)/shard_map/ppermute | solution.py:245
  16.3 0.0 collective-permute-start.1
  16.3 0.6 %collective-permute-start.3 = (f32[64,128]{1,0:T(8,128)S(1)}, f32[64,128]{1,0:T(8,128)S(1)}, u32[]{:S(2)}, u32[]{:S(2)}) collective-permute-start(f32[64,128]{1,0:T(8,128)S(1)} %slice_add_fusion.3.refs_5_), channel_id=1, source_target_pairs={{0,8},{4,12},{8,0},{12,4},{1,9},{5,13},{9,1},{13,5},{2,10},{6,14},... | collective-permute-start | bytes 98312 | tf_op jit(solution)/shard_map/ppermute | solution.py:246
  16.9 1.8 %collective-permute-done.2.refs_7_ = f32[128,128]{1,0:T(8,128)S(1)} collective-permute-done((f32[128,128]{1,0:T(8,128)S(1)}, f32[128,128]{1,0:T(8,128)S(1)}, u32[]{:S(2)}, u32[]{:S(2)}) %collective-permute-start.2) | collective-permute-done | bytes 65568 | tf_op jit(solution)/shard_map/ppermute | solution.py:245
  18.7 1.9 %collective-permute-done.1.refs_6_ = f32[128,128]{1,0:T(8,128)S(1)} collective-permute-done((f32[128,128]{1,0:T(8,128)S(1)}, f32[128,128]{1,0:T(8,128)S(1)}, u32[]{:S(2)}, u32[]{:S(2)}) %collective-permute-start.1) | collective-permute-done | bytes 65568 | tf_op jit(solution)/shard_map/ppermute | solution.py:244
  20.6 0.5 collective-permute-done.3.refs_8_
  21.1 0.0 collective-permute-done.4.refs_13_.refs_14_
  21.1 0.0 copy-done.3
  21.1 0.0 copy-done.4
  21.1 0.0 copy-done.1
  21.1 1.4 %shard_map.105 = (f32[3,16,16,128]{3,2,1,0:T(8,128)S(1)}, f32[112,128]{1,0:T(8,128)S(1)}, f32[48,128]{1,0:T(8,128)S(1)}, f32[48,128]{1,0:T(8,128)S(1)}, f32[6,16...) custom-call(s32[9]{0:T(128)S(1)} %stack.63.info.refs_0_, ...), custom_call_target="tpu_custom_call" | custom-call | tf_op jit(solution)/shard_map/pallas_call | solution.py:199
  22.6 1.6 %collective-permute-start.5 = (f32[112,128]{1,0:T(8,128)S(1)}, f32[112,128]{1,0:T(8,128)S(1)}, u32[]{:S(2)}, u32[]{:S(2)}) collective-permute-start(f32[112,128]{1,0:T(8,128)S(1)} %get-tuple-element.38), channel_id=1, source_target_pairs={{0,2},{2,0},{1,3},{3,1},{4,6},{6,4},{5,7},{7,5},{8,10},{10,8},{9,1... | collective-permute-start | bytes 172040 | tf_op jit(solution)/shard_map/ppermute | solution.py:238
  24.1 0.0 collective-permute-start.9
  24.1 2.7 %collective-permute-done.5.refs_11_.refs_12_ = f32[112,128]{1,0:T(8,128)S(1)} collective-permute-done((f32[112,128]{1,0:T(8,128)S(1)}, f32[112,128]{1,0:T(8,128)S(1)}, u32[]{:S(2)}, u32[]{:S(2)}) %collective-permute-start.5) | collective-permute-done | bytes 57376 | tf_op jit(solution)/shard_map/ppermute | solution.py:238
  26.8 1.7 %collective-permute-start.7 = (f32[112,128]{1,0:T(8,128)S(1)}, f32[112,128]{1,0:T(8,128)S(1)}, u32[]{:S(2)}, u32[]{:S(2)}) collective-permute-start(f32[112,128]{1,0:T(8,128)S(1)} %get-tuple-element.64), channel_id=1, source_target_pairs={{0,12},{4,8},{8,4},{12,0},{1,13},{5,9},{9,5},{13,1},{2,14},{6,10},... | collective-permute-start | bytes 172040 | tf_op jit(solution)/shard_map/ppermute | solution.py:245
  28.5 0.5 collective-permute-start.6
  29.0 2.3 %collective-permute-start.8 = (f32[64,128]{1,0:T(8,128)S(1)}, f32[64,128]{1,0:T(8,128)S(1)}, u32[]{:S(2)}, u32[]{:S(2)}) collective-permute-start(f32[64,128]{1,0:T(8,128)S(1)} %slice_add_fusion.2.refs_5_), channel_id=1, source_target_pairs={{0,8},{4,12},{8,0},{12,4},{1,9},{5,13},{9,1},{13,5},{2,10},{6,14},... | collective-permute-start | bytes 98312 | tf_op jit(solution)/shard_map/ppermute | solution.py:246
  31.3 1.7 %collective-permute-done.7.refs_7_ = f32[112,128]{1,0:T(8,128)S(1)} collective-permute-done((f32[112,128]{1,0:T(8,128)S(1)}, f32[112,128]{1,0:T(8,128)S(1)}, u32[]{:S(2)}, u32[]{:S(2)}) %collective-permute-start.7) | collective-permute-done | bytes 57376 | tf_op jit(solution)/shard_map/ppermute | solution.py:245
  33.0 0.3 collective-permute-done.6.refs_6_
  33.3 0.5 collective-permute-done.8.refs_8_
  33.8 0.0 collective-permute-done.9.refs_13_.refs_14_
  33.8 1.2 %shard_map.106 = (f32[3,16,16,128]{3,2,1,0:T(8,128)S(1)}, f32[112,128]{1,0:T(8,128)S(1)}, f32[48,128]{1,0:T(8,128)S(1)}, f32[48,128]{1,0:T(8,128)S(1)}) custom-call(s32[9]{0:T(128)S(1)} %stack.63.info.refs_0_, f32[3,16,16,128]{3,2,1,0:T(8,128)S(1)} %get-tuple-element.37.refs_1_, f32[64,128]{1,0:T(8,128)S(1)} %get-tuple-element.27.refs_2_, ...), custom_call_target="tpu_custom_call" | custom-call | tf_op jit(solution)/shard_map/pallas_call | solution.py:199
  35.0 1.6 %collective-permute-start.10 = (f32[112,128]{1,0:T(8,128)S(1)}, f32[112,128]{1,0:T(8,128)S(1)}, u32[]{:S(2)}, u32[]{:S(2)}) collective-permute-start(f32[112,128]{1,0:T(8,128)S(1)} %get-tuple-element.45), channel_id=1, source_target_pairs={{0,2},{2,0},{1,3},{3,1},{4,6},{6,4},{5,7},{7,5},{8,10},{10,8},{9,1... | collective-permute-start | bytes 172040 | tf_op jit(solution)/shard_map/ppermute | solution.py:238
  36.6 0.0 collective-permute-start.14
  36.6 2.7 %collective-permute-done.10.refs_11_.refs_12_ = f32[112,128]{1,0:T(8,128)S(1)} collective-permute-done((f32[112,128]{1,0:T(8,128)S(1)}, f32[112,128]{1,0:T(8,128)S(1)}, u32[]{:S(2)}, u32[]{:S(2)}) %collective-permute-start.10) | collective-permute-done | bytes 57376 | tf_op jit(solution)/shard_map/ppermute | solution.py:238
  39.3 2.9 %collective-permute-start.12 = (f32[112,128]{1,0:T(8,128)S(1)}, f32[112,128]{1,0:T(8,128)S(1)}, u32[]{:S(2)}, u32[]{:S(2)}) collective-permute-start(f32[112,128]{1,0:T(8,128)S(1)} %get-tuple-element.62), channel_id=1, source_target_pairs={{0,12},{4,8},{8,4},{12,0},{1,13},{5,9},{9,5},{13,1},{2,14},{6,10},... | collective-permute-start | bytes 172040 | tf_op jit(solution)/shard_map/ppermute | solution.py:245
  42.2 0.0 collective-permute-start.11
  42.2 1.5 %collective-permute-start.13 = (f32[64,128]{1,0:T(8,128)S(1)}, f32[64,128]{1,0:T(8,128)S(1)}, u32[]{:S(2)}, u32[]{:S(2)}) collective-permute-start(f32[64,128]{1,0:T(8,128)S(1)} %slice_add_fusion.1.refs_5_), channel_id=1, source_target_pairs={{0,8},{4,12},{8,0},{12,4},{1,9},{5,13},{9,1},{13,5},{2,10},{6,14},... | collective-permute-start | bytes 98312 | tf_op jit(solution)/shard_map/ppermute | solution.py:246
  43.7 1.7 %collective-permute-done.12.refs_7_ = f32[112,128]{1,0:T(8,128)S(1)} collective-permute-done((f32[112,128]{1,0:T(8,128)S(1)}, f32[112,128]{1,0:T(8,128)S(1)}, u32[]{:S(2)}, u32[]{:S(2)}) %collective-permute-start.12) | collective-permute-done | bytes 57376 | tf_op jit(solution)/shard_map/ppermute | solution.py:245
  45.4 0.9 %collective-permute-done.11.refs_6_ = f32[112,128]{1,0:T(8,128)S(1)} collective-permute-done((f32[112,128]{1,0:T(8,128)S(1)}, f32[112,128]{1,0:T(8,128)S(1)}, u32[]{:S(2)}, u32[]{:S(2)}) %collective-permute-start.11) | collective-permute-done | bytes 57376 | tf_op jit(solution)/shard_map/ppermute | solution.py:244
  46.4 0.6 %collective-permute-done.13.refs_8_ = f32[64,128]{1,0:T(8,128)S(1)} collective-permute-done((f32[64,128]{1,0:T(8,128)S(1)}, f32[64,128]{1,0:T(8,128)S(1)}, u32[]{:S(2)}, u32[]{:S(2)}) %collective-permute-start.13) | collective-permute-done | bytes 32800 | tf_op jit(solution)/shard_map/ppermute | solution.py:246
  47.0 0.0 collective-permute-done.14.refs_13_.refs_14_
  47.0 1.2 %shard_map.107 = (f32[3,16,16,128]{3,2,1,0:T(8,128)S(1)}, f32[112,128]{1,0:T(8,128)S(1)}, f32[48,128]{1,0:T(8,128)S(1)}, f32[48,128]{1,0:T(8,128)S(1)}) custom-call(s32[9]{0:T(128)S(1)} %stack.63.info.refs_0_, f32[3,16,16,128]{3,2,1,0:T(8,128)S(1)} %get-tuple-element.44.refs_1_, f32[64,128]{1,0:T(8,128)S(1)} %get-tuple-element.27.refs_2_, ...), custom_call_target="tpu_custom_call" | custom-call | tf_op jit(solution)/shard_map/pallas_call | solution.py:199
  48.2 1.6 %collective-permute-start.15 = (f32[112,128]{1,0:T(8,128)S(1)}, f32[112,128]{1,0:T(8,128)S(1)}, u32[]{:S(2)}, u32[]{:S(2)}) collective-permute-start(f32[112,128]{1,0:T(8,128)S(1)} %get-tuple-element.49), channel_id=1, source_target_pairs={{0,2},{2,0},{1,3},{3,1},{4,6},{6,4},{5,7},{7,5},{8,10},{10,8},{9,1... | collective-permute-start | bytes 172040 | tf_op jit(solution)/shard_map/ppermute | solution.py:238
  49.8 0.0 collective-permute-start.19
  49.8 2.7 %collective-permute-done.15.refs_11_.refs_12_ = f32[112,128]{1,0:T(8,128)S(1)} collective-permute-done((f32[112,128]{1,0:T(8,128)S(1)}, f32[112,128]{1,0:T(8,128)S(1)}, u32[]{:S(2)}, u32[]{:S(2)}) %collective-permute-start.15) | collective-permute-done | bytes 57376 | tf_op jit(solution)/shard_map/ppermute | solution.py:238
  52.5 1.6 %collective-permute-start.17 = (f32[112,128]{1,0:T(8,128)S(1)}, f32[112,128]{1,0:T(8,128)S(1)}, u32[]{:S(2)}, u32[]{:S(2)}) collective-permute-start(f32[112,128]{1,0:T(8,128)S(1)} %get-tuple-element.60), channel_id=1, source_target_pairs={{0,12},{4,8},{8,4},{12,0},{1,13},{5,9},{9,5},{13,1},{2,14},{6,10},... | collective-permute-start | bytes 172040 | tf_op jit(solution)/shard_map/ppermute | solution.py:245
  54.1 0.5 collective-permute-start.16
  54.6 2.3 %collective-permute-start.18 = (f32[64,128]{1,0:T(8,128)S(1)}, f32[64,128]{1,0:T(8,128)S(1)}, u32[]{:S(2)}, u32[]{:S(2)}) collective-permute-start(f32[64,128]{1,0:T(8,128)S(1)} %slice_add_fusion.refs_5_), channel_id=1, source_target_pairs={{0,8},{4,12},{8,0},{12,4},{1,9},{5,13},{9,1},{13,5},{2,10},{6,14},... | collective-permute-start | bytes 98312 | tf_op jit(solution)/shard_map/ppermute | solution.py:246
  56.9 1.8 %collective-permute-done.17.refs_7_ = f32[112,128]{1,0:T(8,128)S(1)} collective-permute-done((f32[112,128]{1,0:T(8,128)S(1)}, f32[112,128]{1,0:T(8,128)S(1)}, u32[]{:S(2)}, u32[]{:S(2)}) %collective-permute-start.17) | collective-permute-done | bytes 57376 | tf_op jit(solution)/shard_map/ppermute | solution.py:245
  58.7 0.2 collective-permute-done.16.refs_6_
  58.9 0.5 collective-permute-done.18.refs_8_
  59.5 0.0 collective-permute-done.19.refs_13_.refs_14_
  59.5 1.8 %shard_map.108 = (f32[3,16,16,128]{3,2,1,0:T(8,128)}, f32[8,128]{1,0:T(8,128)}) custom-call(s32[9]{0:T(128)S(1)} %stack.63.info.refs_0_, f32[3,16,16,128]{3,2,1,0:T(8,128)S(1)} %get-tuple-element.48.refs_1_, f32[64,128]{1,0:T(8,128)S(1)} %get-tuple-element.27.refs_2_, bf16[256,64]{1,0:T(8,128)(2,1)S(1)} %get-tuple-element.28.refs_3_, ...), custom_call_target="tpu_custom_call" | custom-call | tf_op jit(solution)/shard_map/pallas_call | solution.py:199
  (18 shorter events, 0.1 us)
Async XLA Ops:
  0.7 0.7 %copy-start.8 = (f32[8,3]{0,1:T(4,128)S(1)}, f32[8,3]{0,1:T(4,128)}, u32[]{:S(2)}) copy-start(f32[8,3]{0,1:T(4,128)} %param.13) | copy-start | bytes 292
  1.4 0.7 %copy-start.9 = (s32[128]{0:T(128)S(1)}, s32[128]{0:T(128)}, u32[]{:S(2)}) copy-start(s32[128]{0:T(128)} %param.16) | copy-start | bytes 1540
  1.4 0.7 %copy-start.10 = (s32[128,1]{0,1:T(1,128)S(1)}, s32[128,1]{0,1:T(1,128)}, u32[]{:S(2)}) copy-start(s32[128,1]{0,1:T(1,128)} %param.15) | copy-start | bytes 1540
  2.1 0.7 %copy-start.6 = (f32[8,128]{1,0:T(8,128)S(1)}, f32[8,128]{1,0:T(8,128)}, u32[]{:S(2)}) copy-start(f32[8,128]{1,0:T(8,128)} %observed.1) | copy-start | bytes 12292
  2.2 0.7 %copy-start.7 = (s32[128]{0:T(128)S(1)}, s32[128]{0:T(128)}, u32[]{:S(2)}) copy-start(s32[128]{0:T(128)} %param.14) | copy-start | bytes 1540
  2.8 1.0 %copy-start = (f32[3,16,16,128]{3,2,1,0:T(8,128)S(1)}, f32[3,16,16,128]{3,2,1,0:T(8,128)}, u32[]{:S(2)}) copy-start(f32[3,16,16,128]{3,2,1,0:T(8,128)} %refs_1_.1) | copy-start | bytes 1179652
  3.8 1.0 %copy-start.2 = (f32[3,16,16,128]{3,2,1,0:T(8,128)S(1)}, f32[3,16,16,128]{3,2,1,0:T(8,128)}, u32[]{:S(2)}) copy-start(f32[3,16,16,128]{3,2,1,0:T(8,128)} %refs_17_.1) | copy-start | bytes 1179652
  4.8 0.9 %copy-start.5 = (s32[16,16,128]{2,1,0:T(8,128)S(1)}, s32[16,16,128]{2,1,0:T(8,128)}, u32[]{:S(2)}) copy-start(s32[16,16,128]{2,1,0:T(8,128)} %rock.1) | copy-start | bytes 393220
  5.7 15.4 %copy-start.3 = (f32[3,16,16,128]{3,2,1,0:T(8,128)S(1)}, f32[3,16,16,128]{3,2,1,0:T(8,128)}, u32[]{:S(2)}) copy-start(f32[3,16,16,128]{3,2,1,0:T(8,128)} %refs_17_.1) | copy-start | bytes 1179652
  5.7 15.4 %copy-start.4 = (f32[16,16,128]{2,1,0:T(8,128)S(1)}, f32[16,16,128]{2,1,0:T(8,128)}, u32[]{:S(2)}) copy-start(f32[16,16,128]{2,1,0:T(8,128)} %refs_18_.1) | copy-start | bytes 393220
  6.8 14.3 %copy-start.1 = (f32[3,16,16,128]{3,2,1,0:T(8,128)S(1)}, f32[3,16,16,128]{3,2,1,0:T(8,128)}, u32[]{:S(2)}) copy-start(f32[3,16,16,128]{3,2,1,0:T(8,128)} %refs_1_.1) | copy-start | bytes 1179652
  6.8 5.2 %collective-permute-start = (f32[128,128]{1,0:T(8,128)S(1)}, f32[128,128]{1,0:T(8,128)S(1)}, u32[]{:S(2)}, u32[]{:S(2)}) collective-permute-start(f32[128,128]{1,0:T(8,128)S(1)} %get-tuple-element.30), channel_id=1, source_target_pairs={{0,2},{2,0},{1,3},{3,1},{4,6},{6,4},{5,7},{7,5},{8,10},{10,8},{9,1... | collective-permute-start | bytes 196616 | tf_op jit(solution)/shard_map/ppermute | solution.py:238
  9.8 11.3 %collective-permute-start.4 = (f32[4,16,16,128]{3,2,1,0:T(8,128)S(1)}, f32[4,16,16,128]{3,2,1,0:T(8,128)S(1)}, u32[]{:S(2)}, u32[]{:S(2)}) collective-permute-start(f32[4,16,16,128]{3,2,1,0:T(8,128)S(1)} %get-tuple-element.33), channel_id=1, source_target_pairs={{0,1},{1,0},{2,3},{3,2},{4,5},{5,4},{6,7},{7,6},{8,9},{9,8},{10,11... | collective-permute-start | bytes 1572872 | tf_op jit(solution)/shard_map/ppermute | solution.py:234
  12.1 6.6 %collective-permute-start.2 = (f32[128,128]{1,0:T(8,128)S(1)}, f32[128,128]{1,0:T(8,128)S(1)}, u32[]{:S(2)}, u32[]{:S(2)}) collective-permute-start(f32[128,128]{1,0:T(8,128)S(1)} %get-tuple-element.66), channel_id=1, source_target_pairs={{0,12},{4,8},{8,4},{12,0},{1,13},{5,9},{9,5},{13,1},{2,14},{6,10},... | collective-permute-start | bytes 196616 | tf_op jit(solution)/shard_map/ppermute | solution.py:245
  16.3 4.3 %collective-permute-start.1 = (f32[128,128]{1,0:T(8,128)S(1)}, f32[128,128]{1,0:T(8,128)S(1)}, u32[]{:S(2)}, u32[]{:S(2)}) collective-permute-start(f32[128,128]{1,0:T(8,128)S(1)} %get-tuple-element.67), channel_id=1, source_target_pairs={{0,4},{4,0},{8,12},{12,8},{1,5},{5,1},{9,13},{13,9},{2,6},{6,2},{1... | collective-permute-start | bytes 196616 | tf_op jit(solution)/shard_map/ppermute | solution.py:244
  16.3 4.8 %collective-permute-start.3 = (f32[64,128]{1,0:T(8,128)S(1)}, f32[64,128]{1,0:T(8,128)S(1)}, u32[]{:S(2)}, u32[]{:S(2)}) collective-permute-start(f32[64,128]{1,0:T(8,128)S(1)} %slice_add_fusion.3.refs_5_), channel_id=1, source_target_pairs={{0,8},{4,12},{8,0},{12,4},{1,9},{5,13},{9,1},{13,5},{2,10},{6,14},... | collective-permute-start | bytes 98312 | tf_op jit(solution)/shard_map/ppermute | solution.py:246
  22.6 4.2 %collective-permute-start.5 = (f32[112,128]{1,0:T(8,128)S(1)}, f32[112,128]{1,0:T(8,128)S(1)}, u32[]{:S(2)}, u32[]{:S(2)}) collective-permute-start(f32[112,128]{1,0:T(8,128)S(1)} %get-tuple-element.38), channel_id=1, source_target_pairs={{0,2},{2,0},{1,3},{3,1},{4,6},{6,4},{5,7},{7,5},{8,10},{10,8},{9,1... | collective-permute-start | bytes 172040 | tf_op jit(solution)/shard_map/ppermute | solution.py:238
  24.1 9.7 %collective-permute-start.9 = (f32[3,16,16,128]{3,2,1,0:T(8,128)S(1)}, f32[3,16,16,128]{3,2,1,0:T(8,128)S(1)}, u32[]{:S(2)}, u32[]{:S(2)}) collective-permute-start(f32[3,16,16,128]{3,2,1,0:T(8,128)S(1)} %get-tuple-element.37.refs_1_), channel_id=1, source_target_pairs={{0,1},{1,0},{2,3},{3,2},{4,5},{5,4},{6,7},{7,6},{8,9},{9,8},{10,11... | collective-permute-start | bytes 1179656 | tf_op jit(solution)/shard_map/ppermute | solution.py:234
  26.8 6.2 %collective-permute-start.7 = (f32[112,128]{1,0:T(8,128)S(1)}, f32[112,128]{1,0:T(8,128)S(1)}, u32[]{:S(2)}, u32[]{:S(2)}) collective-permute-start(f32[112,128]{1,0:T(8,128)S(1)} %get-tuple-element.64), channel_id=1, source_target_pairs={{0,12},{4,8},{8,4},{12,0},{1,13},{5,9},{9,5},{13,1},{2,14},{6,10},... | collective-permute-start | bytes 172040 | tf_op jit(solution)/shard_map/ppermute | solution.py:245
  28.5 4.8 %collective-permute-start.6 = (f32[112,128]{1,0:T(8,128)S(1)}, f32[112,128]{1,0:T(8,128)S(1)}, u32[]{:S(2)}, u32[]{:S(2)}) collective-permute-start(f32[112,128]{1,0:T(8,128)S(1)} %get-tuple-element.65), channel_id=1, source_target_pairs={{0,4},{4,0},{8,12},{12,8},{1,5},{5,1},{9,13},{13,9},{2,6},{6,2},{1... | collective-permute-start | bytes 172040 | tf_op jit(solution)/shard_map/ppermute | solution.py:244
  29.0 4.8 %collective-permute-start.8 = (f32[64,128]{1,0:T(8,128)S(1)}, f32[64,128]{1,0:T(8,128)S(1)}, u32[]{:S(2)}, u32[]{:S(2)}) collective-permute-start(f32[64,128]{1,0:T(8,128)S(1)} %slice_add_fusion.2.refs_5_), channel_id=1, source_target_pairs={{0,8},{4,12},{8,0},{12,4},{1,9},{5,13},{9,1},{13,5},{2,10},{6,14},... | collective-permute-start | bytes 98312 | tf_op jit(solution)/shard_map/ppermute | solution.py:246
  35.0 4.2 %collective-permute-start.10 = (f32[112,128]{1,0:T(8,128)S(1)}, f32[112,128]{1,0:T(8,128)S(1)}, u32[]{:S(2)}, u32[]{:S(2)}) collective-permute-start(f32[112,128]{1,0:T(8,128)S(1)} %get-tuple-element.45), channel_id=1, source_target_pairs={{0,2},{2,0},{1,3},{3,1},{4,6},{6,4},{5,7},{7,5},{8,10},{10,8},{9,1... | collective-permute-start | bytes 172040 | tf_op jit(solution)/shard_map/ppermute | solution.py:238
  36.6 10.4 %collective-permute-start.14 = (f32[3,16,16,128]{3,2,1,0:T(8,128)S(1)}, f32[3,16,16,128]{3,2,1,0:T(8,128)S(1)}, u32[]{:S(2)}, u32[]{:S(2)}) collective-permute-start(f32[3,16,16,128]{3,2,1,0:T(8,128)S(1)} %get-tuple-element.44.refs_1_), channel_id=1, source_target_pairs={{0,1},{1,0},{2,3},{3,2},{4,5},{5,4},{6,7},{7,6},{8,9},{9,8},{10,11... | collective-permute-start | bytes 1179656 | tf_op jit(solution)/shard_map/ppermute | solution.py:234
  39.3 6.2 %collective-permute-start.12 = (f32[112,128]{1,0:T(8,128)S(1)}, f32[112,128]{1,0:T(8,128)S(1)}, u32[]{:S(2)}, u32[]{:S(2)}) collective-permute-start(f32[112,128]{1,0:T(8,128)S(1)} %get-tuple-element.62), channel_id=1, source_target_pairs={{0,12},{4,8},{8,4},{12,0},{1,13},{5,9},{9,5},{13,1},{2,14},{6,10},... | collective-permute-start | bytes 172040 | tf_op jit(solution)/shard_map/ppermute | solution.py:245
  42.2 4.2 %collective-permute-start.11 = (f32[112,128]{1,0:T(8,128)S(1)}, f32[112,128]{1,0:T(8,128)S(1)}, u32[]{:S(2)}, u32[]{:S(2)}) collective-permute-start(f32[112,128]{1,0:T(8,128)S(1)} %get-tuple-element.63), channel_id=1, source_target_pairs={{0,4},{4,0},{8,12},{12,8},{1,5},{5,1},{9,13},{13,9},{2,6},{6,2},{1... | collective-permute-start | bytes 172040 | tf_op jit(solution)/shard_map/ppermute | solution.py:244
  42.2 4.8 %collective-permute-start.13 = (f32[64,128]{1,0:T(8,128)S(1)}, f32[64,128]{1,0:T(8,128)S(1)}, u32[]{:S(2)}, u32[]{:S(2)}) collective-permute-start(f32[64,128]{1,0:T(8,128)S(1)} %slice_add_fusion.1.refs_5_), channel_id=1, source_target_pairs={{0,8},{4,12},{8,0},{12,4},{1,9},{5,13},{9,1},{13,5},{2,10},{6,14},... | collective-permute-start | bytes 98312 | tf_op jit(solution)/shard_map/ppermute | solution.py:246
  48.2 4.2 %collective-permute-start.15 = (f32[112,128]{1,0:T(8,128)S(1)}, f32[112,128]{1,0:T(8,128)S(1)}, u32[]{:S(2)}, u32[]{:S(2)}) collective-permute-start(f32[112,128]{1,0:T(8,128)S(1)} %get-tuple-element.49), channel_id=1, source_target_pairs={{0,2},{2,0},{1,3},{3,1},{4,6},{6,4},{5,7},{7,5},{8,10},{10,8},{9,1... | collective-permute-start | bytes 172040 | tf_op jit(solution)/shard_map/ppermute | solution.py:238
  49.8 9.7 %collective-permute-start.19 = (f32[3,16,16,128]{3,2,1,0:T(8,128)S(1)}, f32[3,16,16,128]{3,2,1,0:T(8,128)S(1)}, u32[]{:S(2)}, u32[]{:S(2)}) collective-permute-start(f32[3,16,16,128]{3,2,1,0:T(8,128)S(1)} %get-tuple-element.48.refs_1_), channel_id=1, source_target_pairs={{0,1},{1,0},{2,3},{3,2},{4,5},{5,4},{6,7},{7,6},{8,9},{9,8},{10,11... | collective-permute-start | bytes 1179656 | tf_op jit(solution)/shard_map/ppermute | solution.py:234
  52.5 6.2 %collective-permute-start.17 = (f32[112,128]{1,0:T(8,128)S(1)}, f32[112,128]{1,0:T(8,128)S(1)}, u32[]{:S(2)}, u32[]{:S(2)}) collective-permute-start(f32[112,128]{1,0:T(8,128)S(1)} %get-tuple-element.60), channel_id=1, source_target_pairs={{0,12},{4,8},{8,4},{12,0},{1,13},{5,9},{9,5},{13,1},{2,14},{6,10},... | collective-permute-start | bytes 172040 | tf_op jit(solution)/shard_map/ppermute | solution.py:245
  54.1 4.8 %collective-permute-start.16 = (f32[112,128]{1,0:T(8,128)S(1)}, f32[112,128]{1,0:T(8,128)S(1)}, u32[]{:S(2)}, u32[]{:S(2)}) collective-permute-start(f32[112,128]{1,0:T(8,128)S(1)} %get-tuple-element.61), channel_id=1, source_target_pairs={{0,4},{4,0},{8,12},{12,8},{1,5},{5,1},{9,13},{13,9},{2,6},{6,2},{1... | collective-permute-start | bytes 172040 | tf_op jit(solution)/shard_map/ppermute | solution.py:244
  54.6 4.8 %collective-permute-start.18 = (f32[64,128]{1,0:T(8,128)S(1)}, f32[64,128]{1,0:T(8,128)S(1)}, u32[]{:S(2)}, u32[]{:S(2)}) collective-permute-start(f32[64,128]{1,0:T(8,128)S(1)} %slice_add_fusion.refs_5_), channel_id=1, source_target_pairs={{0,8},{4,12},{8,0},{12,4},{1,9},{5,13},{9,1},{13,5},{2,10},{6,14},... | collective-permute-start | bytes 98312 | tf_op jit(solution)/shard_map/ppermute | solution.py:246

commit v2 on v0

v2 whole, which is shorter than its diff:
```python
import functools

import jax
import jax.numpy as jnp
from jax import lax
from jax.experimental import pallas as pl
from jax.experimental.pallas import tpu as pltpu
from jax.sharding import PartitionSpec as P

STEPS = 4
F32 = jnp.float32
BF16 = jnp.bfloat16
VMEM = pl.BlockSpec(memory_space=pltpu.VMEM)
HBM = pl.BlockSpec(memory_space=pltpu.HBM)
SMEM = pl.BlockSpec(memory_space=pltpu.SMEM)
MIB = 1024 * 1024


class Refs(dict):
    __getattr__ = dict.__getitem__


def harmonic(first, second):
    return 2.0 * first * second / (first + second)


def split(value):
    high = value.astype(BF16)
    rest = value - high.astype(F32)
    middle = rest.astype(BF16)
    low = (rest - middle.astype(F32)).astype(BF16)
    return jnp.concatenate([high, middle, low], axis=1)


def counted(counts, value):
    n = value.shape[1]
    out = jnp.dot(counts, split(value), preferred_element_type=F32)
    return out[:, :n] + (out[:, n : 2 * n] + out[:, 2 * n :])


def odd(axis):
    return lax.rem(lax.axis_index(axis), 2) == 1


def own_rows(own):
    owner = lax.axis_index("gx") * lax.axis_size("gy") + lax.axis_index("gy")
    return pl.ds(pl.multiple_of(owner * own, own), own)


def hits(r, wells, own, columns):
    rows = r.column.shape[1]
    well = r.owner[...] * own + r.slot[...]
    well_hit = (lax.broadcasted_iota(jnp.int32, (wells, rows), 0) == well).astype(BF16)
    col_hit = lax.broadcasted_iota(jnp.int32, (columns, rows), 0) == r.column[...]
    return well_hit, col_hit.astype(BF16)


def pairs(first, second):
    out = lax.dot_general(
        first, second, (((1,), (1,)), ((), ())), preferred_element_type=F32
    )
    return out.astype(BF16)


def plane_mobility(r, x):
    kind = r.rock[x]
    root = jnp.sqrt(r.perm[0, x] * r.perm[1, x])
    index = root / (1.0 + root)
    mobility = []
    for p in range(3):
        m = jnp.full(kind.shape, r.table[p, 0], F32)
        for k in range(1, r.table.shape[1]):
            m = jnp.where(kind == k, r.table[p, k], m)
        mobility.append(m)
    return index, mobility


def send_y(r, row, value):
    ny = value.shape[0]
    r.msg_y[row : row + 1, :] = jnp.where(odd("gy"), value[0:1, :], value[ny - 1 : ny, :])


def send_x(r, p, low, high):
    ny = low.shape[0]
    r.face_a[p * ny : (p + 1) * ny, :] = jnp.where(odd("gx"), low, high)
    r.face_b[p * ny : (p + 1) * ny, :] = jnp.where(odd("gx"), high, low)


def first_kernel(names, *refs):
    r = Refs(zip(names, refs))
    moved = ("column", "owner", "slot", "observed", "perm", "rock", "adj")
    copies = {}
    for i, name in enumerate(moved):
        copies[name] = pltpu.make_async_copy(r[name + "_in"], r[name], r.sems.at[i])
        copies[name].start()
    _, nx, ny, nz = r.adj.shape
    own = r.observed.shape[0]
    wells = r.msg_y.shape[0] - 4 * nx
    for name in moved[:4]:
        copies[name].wait()
    well_hit, col_hit = hits(r, wells, own, nx * ny)
    counts = pairs(well_hit, col_hit)
    for name in moved[4:]:
        copies[name].wait()
    for x in range(nx):
        index, mobility = plane_mobility(r, x)
        total = jnp.zeros((ny, nz), F32)
        for p in range(3):
            total = total + mobility[p] * r.adj[p, x]
            send_y(r, wells + p * nx + x, r.adj[p, x])
        send_y(r, wells + 3 * nx + x, r.perm[1, x])
        r.combined[x * ny : (x + 1) * ny, :] = 0.25 * index * total
    for p in range(3):
        send_x(r, p, r.adj[p, 0], r.adj[p, nx - 1])
    send_x(r, 3, r.perm[0, 0], r.perm[0, nx - 1])
    r.msg_y[0:wells, :] = counted(counts, r.combined[...])
    r.msg_y[own_rows(own), :] = r.msg_y[own_rows(own), :] - r.observed[...]


def inner_kernel(first, last, names, *refs):
    r = Refs(zip(names, refs))
    _, nx, ny, nz = r.adj.shape
    lane = lax.broadcasted_iota(jnp.int32, (ny, nz), 1)
    sub = lax.broadcasted_iota(jnp.int32, (ny, nz), 0)
    at_first, at_last = lane == 0, lane == nz - 1
    top, bottom = sub == 0, sub == ny - 1
    y0 = r.ym.shape[0] - (4 if first else 3) * nx

    def y_minus(value, p, x):
        edge = r.ym[y0 + p * nx + x : y0 + p * nx + x + 1, :]
        return jnp.where(top, edge, pltpu.roll(value, 1, 0))

    def y_plus(value, p, x):
        edge = r.yp[y0 + p * nx + x : y0 + p * nx + x + 1, :]
        return jnp.where(bottom, edge, pltpu.roll(value, ny - 1, 0))

    def z_minus(value, beside):
        return pltpu.roll(jnp.where(at_last, beside, value), 1, 1)

    def z_plus(value, beside):
        return pltpu.roll(jnp.where(at_first, beside, value), nz - 1, 1)

    if first:
        own = r.observed.shape[0]
        wells = r.counts.shape[0]
        well_hit, col_hit = hits(r, wells, own, nx * ny)
        r.counts[...] = pairs(well_hit, col_hit)
        r.counts_t[...] = pairs(col_hit, well_hit)
        ends = {a: (lax.axis_index(a) == 0, lax.axis_index(a) == lax.axis_size(a) - 1)
                for a in ("gy", "wa")}
        zero = jnp.zeros((ny, nz), F32)
    for x in range(nx):
        edge = x in (0, nx - 1)
        if first:
            k = r.perm[0, x]
            txm = harmonic(k, r.perm[0, x - 1]) if x else zero
            txp = harmonic(k, r.perm[0, x + 1]) if x < nx - 1 else zero
            k = r.perm[1, x]
            tym = harmonic(k, jnp.where(top & ends["gy"][0], 0.0, y_minus(k, 3, x)))
            typ = harmonic(k, jnp.where(bottom & ends["gy"][1], 0.0, y_plus(k, 3, x)))
            k = r.perm[2, x]
            km, kp = z_minus(k, r.pm[2, x]), z_plus(k, r.pp[2, x])
            tzm = harmonic(k, jnp.where(at_first & ends["wa"][0], 0.0, km))
            tzp = harmonic(k, jnp.where(at_last & ends["wa"][1], 0.0, kp))
            weights = (txm, txp, tym, typ, tzm, tzp)
            for f, t in enumerate(weights):
                r.t[f, x] = t
            weight_sum = txm + txp + tym + typ + tzm + tzp
            r.weight[x] = weight_sum
            pore = r.pore[x]
            index, mobility = plane_mobility(r, x)
            r.index[x] = index
            reply = zero
        else:
            txm, txp, tym, typ, tzm, tzp = (r.t[f, x] for f in range(6))
        flow = jnp.zeros((ny, nz), F32)
        for p in range(3):
            value = r.adj[p, x]
            beside = tym * y_minus(value, p, x) + typ * y_plus(value, p, x)
            beside = beside + tzm * z_minus(value, r.zm[p, x])
            beside = beside + tzp * z_plus(value, r.zp[p, x])
            if x:
                beside = beside + txm * r.adj[p, x - 1]
            if x < nx - 1:
                beside = beside + txp * r.adj[p, x + 1]
            if first:
                m = mobility[p]
                gain = 0.25 * index * m
                r.gain[p, x] = gain
                if edge:
                    r.mob[p, 1 if x else 0] = m
                    r.base[p, x] = beside
                    continue
                inverse = 1.0 / (pore + m * weight_sum)
                keep, take = pore * inverse, m * inverse
                r.keep[p, x] = keep
                r.take[p, x] = take
                q = take * index
                r.q[p, x] = q
                reply = reply + gain * q
            elif edge:
                e = 1 if x else 0
                keep, take = r.edge_keep[p, e], r.edge_take[p, e]
            else:
                keep, take = r.keep[p, x], r.take[p, x]
            base = keep * value + take * beside
            r.base[p, x] = base
            if not last and not edge:
                flow = flow + r.gain[p, x] * base
        if not edge:
            if not last:
                r.flow[x] = flow
            if first:
                r.reply[x] = reply


def well_kernel(first, last, names, *refs):
    r = Refs(zip(names, refs))
    _, nx, ny, nz = r.base.shape
    wells = r.total.shape[0]
    total = r.total[...]
    for name in names:
        if name.startswith("more"):
            total = total + r[name][0:wells, :]
    if last:
        own = r.observed.shape[0]
        r.combined[...] = total
        r.sens[...] = r.combined[own_rows(own), :] + r.observed[...]
    column_sum = counted(r.counts_t[...], jnp.tanh(total))

    def x_face(p, e):
        if "xm" in r:
            return (r.xp if e else r.xm)[p * ny : (p + 1) * ny, :]
        at = slice(wells + p * ny, wells + (p + 1) * ny)
        one, ring = r.more1[at, :], r.more2[at, :]
        return jnp.where(odd("gx"), ring, one) if e else jnp.where(odd("gx"), one, ring)

    part = 4 if nx % 4 == 0 else 1
    copies = []
    gx, size_x = lax.axis_index("gx"), lax.axis_size("gx")
    for x in range(nx):
        edge = x in (0, nx - 1)
        e = 1 if x else 0
        wells_here = column_sum[x * ny : (x + 1) * ny, :]
        flow = None
        if edge:
            well_term = r.index[x] * wells_here
            if first:
                k = jnp.where(gx == (size_x - 1 if e else 0), 0.0, x_face(3, e))
                tx = harmonic(r.perm[0, x], k)
                r.edge_t[e] = tx
                weight_sum = r.weight[x] + tx
                pore = r.pore[x]
            else:
                tx = r.edge_t[e]
        for p in range(3):
            if not edge:
                new = r.base[p, x] + r.q[p, x] * wells_here
            elif first:
                m = r.mob[p, e]
                inverse = 1.0 / (pore + m * weight_sum)
                keep, take = pore * inverse, m * inverse
                r.edge_keep[p, e] = keep
                r.edge_take[p, e] = take
                beside = r.base[p, x] + tx * x_face(p, e)
                new = keep * r.adj[p, x] + take * (beside + well_term)
            else:
                new = r.base[p, x] + r.edge_take[p, e] * (tx * x_face(p, e) + well_term)
            if last:
                r.held[p, x] = new
                continue
            r.new[p, x] = new
            send_y(r, wells + p * nx + x, new)
            if edge:
                term = r.gain[p, x] * new
                flow = term if flow is None else flow + term
                if x:
                    send_x(r, p, r.new[p, 0], new)
        if last:
            if x % part == part - 1:
                at = pl.ds(x - part + 1, part)
                copies.append(
                    pltpu.make_async_copy(
                        r.held.at[:, at], r.new.at[:, at], r.sems.at[x // part]
                    )
                )
                copies[-1].start()
            continue
        if not edge:
            flow = r.flow[x] + r.reply[x] * wells_here
        r.combined[x * ny : (x + 1) * ny, :] = flow
    if last:
        for copy in copies:
            copy.wait()
    else:
        r.msg_y[0:wells, :] = counted(r.counts[...], r.combined[...])
        own = r.observed.shape[0]
        r.msg_y[own_rows(own), :] = r.msg_y[own_rows(own), :] - r.observed[...]


def call(kernel, ins, outs, scratch, limit=24, cost=None):
    names = tuple(ins) + tuple(outs) + tuple(scratch)
    result = pl.pallas_call(
        functools.partial(kernel, names),
        in_specs=[spec for spec, _ in ins.values()],
        out_specs=[spec for spec, _, _ in outs.values()],
        out_shape=[jax.ShapeDtypeStruct(shape, kind) for _, shape, kind in outs.values()],
        scratch_shapes=list(scratch.values()),
        compiler_params=pltpu.CompilerParams(vmem_limit_bytes=limit * MIB),
        cost_estimate=cost,
    )(*[array for _, array in ins.values()])
    return Refs(zip(outs, result))


def in_vmem(**arrays):
    return {name: (VMEM, array) for name, array in arrays.items()}


def swap(count, bit):
    return [(i, i ^ bit) for i in range(count)]


def neighbours(low, high, axis):
    count = lax.axis_size(axis)
    before = lax.ppermute(high, axis, [(i, i + 1) for i in range(count - 1)])
    after = lax.ppermute(low, axis, [(i + 1, i) for i in range(count - 1)])
    return before, after


def beside_z(block):
    if lax.axis_size("wa") == 2:
        both = lax.ppermute(block, "wa", swap(2, 1))
        return both, both
    return neighbours(block, block, "wa")


def summed_over(value, axis):
    count = lax.axis_size(axis)
    if count & (count - 1):
        return lax.psum(value, axis)
    bit = 1
    while bit < count:
        value = value + lax.ppermute(value, axis, swap(count, bit))
        bit *= 2
    return value


def over_gy(msg_y, parts, wells):
    if lax.axis_size("gy") == 2:
        got = lax.ppermute(msg_y, "gy", swap(2, 1))
        return msg_y[:wells] + got[:wells], got, got
    low = jnp.concatenate([a[:, 0] for a in parts])
    high = jnp.concatenate([a[:, -1] for a in parts])
    return (summed_over(msg_y[:wells], "gy"), *neighbours(low, high, "gy"))


def over_gx(total, face_a, face_b, parts):
    if lax.axis_size("gx") == 4:
        more1 = lax.ppermute(jnp.concatenate([total, face_a]), "gx", swap(4, 1))
        more2 = lax.ppermute(jnp.concatenate([total, face_b]), "gx", swap(4, 3))
        more3 = lax.ppermute(total, "gx", swap(4, 2))
        return dict(total=total, more1=more1, more2=more2, more3=more3)
    xm, xp = neighbours(
        jnp.concatenate([a[0] for a in parts]), jnp.concatenate([a[-1] for a in parts]), "gx"
    )
    return dict(total=summed_over(total, "gx"), xm=xm, xp=xp)


def local(
    adjoint, permeability, pore_volume, rock_type, rock_table,
    perf_column, perf_owner, perf_slot, observed,
):
    _, nx, ny, nz = adjoint.shape
    rows = perf_column.shape[0]
    own = observed.shape[0]
    wells = own * lax.axis_size("gx") * lax.axis_size("gy")
    cells = (nx, ny, nz)
    phases, ends = (3,) + cells, (3, 2, ny, nz)
    table = rock_table.T
    perf = dict(
        column=perf_column.reshape(1, rows), owner=perf_owner.reshape(1, rows),
        slot=perf_slot.reshape(1, rows),
    )
    moved = dict(perf, observed=observed, perm=permeability, rock=rock_type, adj=adjoint)
    ins = {"table": (SMEM, table)}
    ins.update({name + "_in": (HBM, array) for name, array in moved.items()})
    outs = {
        "msg_y": (VMEM, (wells + 4 * nx, nz), F32),
        "face_a": (VMEM, (4 * ny, nz), F32),
        "face_b": (VMEM, (4 * ny, nz), F32),
    }
    scratch = {name: pltpu.VMEM(a.shape, a.dtype) for name, a in moved.items()}
    scratch["combined"] = pltpu.VMEM((nx * ny, nz), F32)
    scratch["sems"] = pltpu.SemaphoreType.DMA((len(moved),))
    sent = call(first_kernel, ins, outs, scratch, 60)
    pm, pp = beside_z(permeability)
    adj = adjoint
    cost = pl.CostEstimate(flops=1, bytes_accessed=4 * MIB, transcendentals=0)
    for step in range(STEPS):
        first, last = step == 0, step == STEPS - 1
        parts = [adj[p] for p in range(3)]
        total, ym, yp = over_gy(sent.msg_y, parts + [permeability[1]] * first, wells)
        sums = over_gx(total, sent.face_a, sent.face_b, parts + [permeability[0]] * first)
        zm, zp = beside_z(adj)
        ins = in_vmem(adj=adj, ym=ym, yp=yp, zm=zm, zp=zp)
        outs = {"base": (VMEM, phases, F32)}
        if not last:
            outs["flow"] = (VMEM, cells, F32)
        if first:
            ins["table"] = (SMEM, table)
            ins.update(in_vmem(
                perm=permeability, pm=pm, pp=pp, pore=pore_volume, rock=rock_type,
                observed=observed, **perf,
            ))
            outs.update(
                t=(VMEM, (6,) + cells, F32), weight=(VMEM, cells, F32),
                index=(VMEM, cells, F32), gain=(VMEM, phases, F32), mob=(VMEM, ends, F32),
                keep=(VMEM, phases, F32), take=(VMEM, phases, F32), q=(VMEM, phases, F32),
                reply=(VMEM, cells, F32), counts=(VMEM, (wells, nx * ny), BF16),
                counts_t=(VMEM, (nx * ny, wells), BF16),
            )
        else:
            ins.update(in_vmem(
                t=fixed.t, keep=fixed.keep, take=fixed.take, edge_keep=edge.edge_keep,
                edge_take=edge.edge_take,
            ))
            if not last:
                ins.update(in_vmem(gain=fixed.gain))
        inner = call(functools.partial(inner_kernel, first, last), ins, outs, {}, 24, cost)
        if first:
            fixed = inner
        ins = in_vmem(
            **sums, base=inner.base, observed=observed, counts_t=fixed.counts_t,
            index=fixed.index, q=fixed.q,
        )
        if first:
            ins.update(in_vmem(
                perm=permeability, pore=pore_volume, weight=fixed.weight, mob=fixed.mob, adj=adj
            ))
        else:
            ins.update(in_vmem(edge_t=edge.edge_t, edge_take=edge.edge_take))
        if last:
            outs = {"new": (HBM, phases, F32), "sens": (VMEM, (own, nz), F32)}
            scratch = {
                "combined": pltpu.VMEM((wells, nz), F32),
                "held": pltpu.VMEM(phases, F32),
                "sems": pltpu.SemaphoreType.DMA((nx,)),
            }
        else:
            ins.update(in_vmem(
                gain=fixed.gain, flow=inner.flow, reply=fixed.reply, counts=fixed.counts
            ))
            outs = {
                "new": (VMEM, phases, F32),
                "msg_y": (VMEM, (wells + 3 * nx, nz), F32),
                "face_a": (VMEM, (3 * ny, nz), F32),
                "face_b": (VMEM, (3 * ny, nz), F32),
            }
            scratch = {"combined": pltpu.VMEM((nx * ny, nz), F32)}
        if first:
            outs.update(
                edge_t=(VMEM, (2, ny, nz), F32), edge_keep=(VMEM, ends, F32),
                edge_take=(VMEM, ends, F32),
            )
        sent = call(functools.partial(well_kernel, first, last), ins, outs, scratch)
        if first:
            edge = sent
        adj = sent.new
    return (adj, sent.sens)


def solution(mesh):
    cell = P(None, ("members", "gx"), "gy", "wa")
    flat = P(("members", "gx"), "gy", "wa")
    placed = (
        cell, cell, flat, flat, P(), P(("gx", "gy")), P(("gx", "gy"), None), P(("gx", "gy")),
        P(("gx", "gy"), "wa"),
    )
    return jax.shard_map(
        local,
        mesh=mesh,
        in_specs=placed,
        out_specs=(cell, P(("members", "gx", "gy"), "wa")),
        check_vma=False,
    )
```

time: 259 us -> 58.2 us (0.22)
  starting transfers between devices: 119 us -> 23.6 us
  local copies, waits for them, and re-layouts: 54 us -> 0.06 us
  other arithmetic: 48.7 us -> 0.87 us
  matrix products: 9.22 us -> 0 us
  Pallas kernels: 0 us -> 8.77 us
    all_to_all x9 -> x0, starting transfers between devices: 50.7 us -> none  [the longest x4 26.6 us: local(): lax.all_to_all(outgoing.reshape(owners, capacity, layers), ('gx', 'gy'),...]
    ppermute x30 -> x21, starting transfers between devices: 68.1 us -> 23.6 us  [the longest x4 7.74 us: over_gx(): more2 = lax.ppermute(jnp.concatenate([total, face_b]), 'gx', swap(4, 3))]
    ppermute x14 -> x0, local copies, waits for them, and re-layouts: 19.5 us -> none  [the longest x7 11.1 us: with_halo(): lax.ppermute(head, axis, [((i + 1) % count, i) for i in range(ends)])]
    slice x20 -> x0, local copies, waits for them, and re-layouts: 16.5 us -> none  [the longest x13 10.8 us: with_halo(): lax.slice_in_dim(cells, cells.shape[dim] - width, cells.shape[dim], axis=...]
    reduce_sum x4 -> x0, other arithmetic: 13.6 us -> none  [the longest x3 12.7 us: local(): jnp.sum(mobility_cols * adjoint.reshape(3, columns, layers), axis=0)]
    dot_general x9 -> x0, matrix products: 9.22 us -> none  [the longest x4 5.21 us: local(): returning = jnp.dot(slot_match.T, response, precision=lax.Precision.HIGHEST)]
    pallas_call x0 -> x9, Pallas kernels: none -> 8.77 us  [call(): pl.pallas_call(functools.partial(kernel, names), in_specs=[spec for spec,...]
    scatter-add x4 -> x0, other arithmetic: 8.64 us -> none  [local(): jnp.zeros((columns, layers), jnp.float32).at[perf_column].add(back_rows)]
  transfers between devices with their start and end apart: 39 -> 21, of which waited for: 10 -> 8; matrix products, arithmetic and copies ran while one was open for 28% -> 1% of each run, Pallas kernels for 0% -> 5%
where the time goes in v2:
time: 58.2 us; the launch traced here: 58 us
  waiting for transfers between devices  23.9 us (41%)
  starting transfers between devices  23.6 us (41%)
  Pallas kernels  8.77 us (15%)
  other arithmetic  0.87 us (1%)
  between operations  0.85 us (1%)
    ppermute x4, waiting for transfers between devices, over_gx(): more3 = lax.ppermute(total, 'gx', swap(4, 2))  13.9 us
    ppermute x4, waiting for transfers between devices, over_gy(): got = lax.ppermute(msg_y, 'gy', swap(2, 1))  9.98 us
    pallas_call x9, Pallas kernels, call(): pl.pallas_call(functools.partial(kernel, names), in_specs=[spec for spec,...  8.77 us
    ppermute x4, starting transfers between devices, over_gx(): more2 = lax.ppermute(jnp.concatenate([total, face_b]), 'gx', swap(4, 3))  7.74 us
    ppermute x4, starting transfers between devices, over_gy(): got = lax.ppermute(msg_y, 'gy', swap(2, 1))  7.68 us
    ppermute x4, starting transfers between devices, over_gx(): more3 = lax.ppermute(total, 'gx', swap(4, 2))  4.01 us
    ppermute x4, starting transfers between devices, over_gx(): more1 = lax.ppermute(jnp.concatenate([total, face_a]), 'gx', swap(4, 1))  3.67 us
  transfers between devices with their start and end apart: 21, of which 8 were waited for; matrix products, arithmetic and copies ran while one was open for 1% of the time, Pallas kernels for 5%

profile of v2, /device:TPU:0, one launch (start us, length us, event | category | flops | bytes accessed | tf_op | source)
XLA Modules:
  0.0 58.0 jit_solution(12311623684162925505)
XLA Ops:
  0.6 0.0 copy-start.1
  0.6 0.0 copy-start
  0.6 3.2 %shard_map.104 = (f32[128,128]{1,0:T(8,128)}, f32[64,128]{1,0:T(8,128)}, f32[64,128]{1,0:T(8,128)}) custom-call(f32[3,8]{1,0:T(4,128)} %bitcast.4, s32[1,128]{1,0:T(1,128)} %bitcast.6, s32[1,128]{1,0:T(1,128)} %bitcast.8, s32[1,128]{1,0:T(1,128)} %bitcast.10, f32[8,128]{1,0:T(8,128)} %refs_5_.9, f32[3,16,16,128]{3,2,1,0:T(8,128)} %refs_9_.3, ...), custom_call_target="tpu_custom_call" | custom-call | tf_op jit(solution)/shard_map/pallas_call | solution.py:303
  3.8 0.0 copy-start.9
  3.8 0.0 copy-start.10
  3.8 3.0 %collective-permute-start = (f32[128,128]{1,0:T(8,128)}, f32[128,128]{1,0:T(8,128)S(1)}, u32[]{:S(2)}, u32[]{:S(2)}) collective-permute-start(f32[128,128]{1,0:T(8,128)} %get-tuple-element.37), channel_id=1, source_target_pairs={{0,2},{2,0},{1,3},{3,1},{4,6},{6,4},{5,7},{7,5},{8,10},{10,8},{9,1... | collective-permute-start | bytes 196616 | tf_op jit(solution)/shard_map/ppermute | solution.py:350
  6.9 0.0 copy-done.1
  6.9 0.0 collective-permute-start.4
  6.9 0.0 copy-done
  6.9 0.5 collective-permute-start.5
  7.4 1.9 %collective-permute-done.refs_1_.refs_2_ = f32[128,128]{1,0:T(8,128)S(1)} collective-permute-done((f32[128,128]{1,0:T(8,128)}, f32[128,128]{1,0:T(8,128)S(1)}, u32[]{:S(2)}, u32[]{:S(2)}) %collective-permute-start) | collective-permute-done | bytes 65568 | tf_op jit(solution)/shard_map/ppermute | solution.py:350
  9.3 0.8 %slice_add_fusion.3.refs_0_ = f32[64,128]{1,0:T(8,128)S(1)} fusion(f32[128,128]{1,0:T(8,128)S(1)} %collective-permute-done.refs_1_.refs_2_, f32[128,128]{1,0:T(8,128)} %get-tuple-element.37), kind=kLoop, calls=%fused_computation.11 | loop fusion | flops 8192 | bytes 98304 | tf_op jit(solution)/shard_map/add | solution.py:351
  10.1 0.0 copy-done.9
  10.1 0.0 copy-start.4
  10.2 0.0 copy-start.5
  10.2 0.0 copy-start.6
  10.2 0.0 copy-start.7
  10.2 0.0 copy-start.8
  10.2 2.2 %collective-permute-start.1 = (f32[128,128]{1,0:T(8,128)S(1)}, f32[128,128]{1,0:T(8,128)S(1)}, u32[]{:S(2)}, u32[]{:S(2)}) collective-permute-start(f32[128,128]{1,0:T(8,128)S(1)} %get-tuple-element.79), channel_id=1, source_target_pairs={{0,4},{4,0},{8,12},{12,8},{1,5},{5,1},{9,13},{13,9},{2,6},{6,2},{1... | collective-permute-start | bytes 196616 | tf_op jit(solution)/shard_map/ppermute | solution.py:359
  12.4 2.5 %collective-permute-start.2 = (f32[128,128]{1,0:T(8,128)S(1)}, f32[128,128]{1,0:T(8,128)S(1)}, u32[]{:S(2)}, u32[]{:S(2)}) collective-permute-start(f32[128,128]{1,0:T(8,128)S(1)} %get-tuple-element.78), channel_id=1, source_target_pairs={{0,12},{4,8},{8,4},{12,0},{1,13},{5,9},{9,5},{13,1},{2,14},{6,10},... | collective-permute-start | bytes 196616 | tf_op jit(solution)/shard_map/ppermute | solution.py:360
  14.9 0.1 collective-permute-start.3
  15.0 0.0 collective-permute-done.4.refs_3_.refs_4_
  15.0 0.0 collective-permute-done.5.refs_7_.refs_8_
  15.0 1.5 %shard_map.105 = (f32[3,16,16,128]{3,2,1,0:T(8,128)S(1)}, f32[16,16,128]{2,1,0:T(8,128)S(1)}, f32[6,16,16,128]{3,2,1,0:T(8,128)S(1)}, f32[16,16,128]{2,1,0:T(8,1...) custom-call(f32[3,16,16,128]{3,2,1,0:T(8,128)S(1)} %copy-done.1, ...), custom_call_target="tpu_custom_call" | custom-call | flops 1 | bytes 4194304 | tf_op jit(solution)/shard_map/pallas_call | solution.py:303
  16.6 3.5 %collective-permute-done.3.refs_3_ = f32[64,128]{1,0:T(8,128)S(1)} collective-permute-done((f32[64,128]{1,0:T(8,128)S(1)}, f32[64,128]{1,0:T(8,128)S(1)}, u32[]{:S(2)}, u32[]{:S(2)}) %collective-permute-start.3) | collective-permute-done | bytes 32800 | tf_op jit(solution)/shard_map/ppermute | solution.py:361
  20.0 0.0 collective-permute-done.1.refs_1_
  20.0 0.0 collective-permute-done.2.refs_2_
  20.0 0.4 shard_map.106
  20.4 1.6 %collective-permute-start.6 = (f32[112,128]{1,0:T(8,128)S(1)}, f32[112,128]{1,0:T(8,128)S(1)}, u32[]{:S(2)}, u32[]{:S(2)}) collective-permute-start(f32[112,128]{1,0:T(8,128)S(1)} %get-tuple-element.50), channel_id=1, source_target_pairs={{0,2},{2,0},{1,3},{3,1},{4,6},{6,4},{5,7},{7,5},{8,10},{10,8},{9,1... | collective-permute-start | bytes 172040 | tf_op jit(solution)/shard_map/ppermute | solution.py:350
  22.0 0.0 collective-permute-start.10
  22.0 2.7 %collective-permute-done.6.refs_1_.refs_2_ = f32[112,128]{1,0:T(8,128)S(1)} collective-permute-done((f32[112,128]{1,0:T(8,128)S(1)}, f32[112,128]{1,0:T(8,128)S(1)}, u32[]{:S(2)}, u32[]{:S(2)}) %collective-permute-start.6) | collective-permute-done | bytes 57376 | tf_op jit(solution)/shard_map/ppermute | solution.py:350
  24.7 0.5 collective-permute-start.7
  25.2 1.4 %collective-permute-start.8 = (f32[112,128]{1,0:T(8,128)S(1)}, f32[112,128]{1,0:T(8,128)S(1)}, u32[]{:S(2)}, u32[]{:S(2)}) collective-permute-start(f32[112,128]{1,0:T(8,128)S(1)} %get-tuple-element.76), channel_id=1, source_target_pairs={{0,12},{4,8},{8,4},{12,0},{1,13},{5,9},{9,5},{13,1},{2,14},{6,10},... | collective-permute-start | bytes 172040 | tf_op jit(solution)/shard_map/ppermute | solution.py:360
  26.6 1.6 %collective-permute-start.9 = (f32[64,128]{1,0:T(8,128)S(1)}, f32[64,128]{1,0:T(8,128)S(1)}, u32[]{:S(2)}, u32[]{:S(2)}) collective-permute-start(f32[64,128]{1,0:T(8,128)S(1)} %slice_add_fusion.2.refs_0_), channel_id=1, source_target_pairs={{0,8},{4,12},{8,0},{12,4},{1,9},{5,13},{9,1},{13,5},{2,10},{6,14},... | collective-permute-start | bytes 98312 | tf_op jit(solution)/shard_map/ppermute | solution.py:361
  28.3 0.0 collective-permute-done.10.refs_3_.refs_4_
  28.3 0.4 shard_map.107
  28.7 3.2 %collective-permute-done.9.refs_3_ = f32[64,128]{1,0:T(8,128)S(1)} collective-permute-done((f32[64,128]{1,0:T(8,128)S(1)}, f32[64,128]{1,0:T(8,128)S(1)}, u32[]{:S(2)}, u32[]{:S(2)}) %collective-permute-start.9) | collective-permute-done | bytes 32800 | tf_op jit(solution)/shard_map/ppermute | solution.py:361
  31.9 0.0 collective-permute-done.7.refs_1_
  31.9 0.0 collective-permute-done.8.refs_2_
  31.9 0.4 shard_map.108
  32.3 1.6 %collective-permute-start.11 = (f32[112,128]{1,0:T(8,128)S(1)}, f32[112,128]{1,0:T(8,128)S(1)}, u32[]{:S(2)}, u32[]{:S(2)}) collective-permute-start(f32[112,128]{1,0:T(8,128)S(1)} %get-tuple-element.62), channel_id=1, source_target_pairs={{0,2},{2,0},{1,3},{3,1},{4,6},{6,4},{5,7},{7,5},{8,10},{10,8},{9,1... | collective-permute-start | bytes 172040 | tf_op jit(solution)/shard_map/ppermute | solution.py:350
  33.8 0.0 collective-permute-start.15
  33.8 2.7 %collective-permute-done.11.refs_1_.refs_2_ = f32[112,128]{1,0:T(8,128)S(1)} collective-permute-done((f32[112,128]{1,0:T(8,128)S(1)}, f32[112,128]{1,0:T(8,128)S(1)}, u32[]{:S(2)}, u32[]{:S(2)}) %collective-permute-start.11) | collective-permute-done | bytes 57376 | tf_op jit(solution)/shard_map/ppermute | solution.py:350
  36.6 0.5 collective-permute-start.12
  37.0 2.3 %collective-permute-start.13 = (f32[112,128]{1,0:T(8,128)S(1)}, f32[112,128]{1,0:T(8,128)S(1)}, u32[]{:S(2)}, u32[]{:S(2)}) collective-permute-start(f32[112,128]{1,0:T(8,128)S(1)} %get-tuple-element.74), channel_id=1, source_target_pairs={{0,12},{4,8},{8,4},{12,0},{1,13},{5,9},{9,5},{13,1},{2,14},{6,10},... | collective-permute-start | bytes 172040 | tf_op jit(solution)/shard_map/ppermute | solution.py:360
  39.4 0.7 %collective-permute-start.14 = (f32[64,128]{1,0:T(8,128)S(1)}, f32[64,128]{1,0:T(8,128)S(1)}, u32[]{:S(2)}, u32[]{:S(2)}) collective-permute-start(f32[64,128]{1,0:T(8,128)S(1)} %slice_add_fusion.1.refs_0_), channel_id=1, source_target_pairs={{0,8},{4,12},{8,0},{12,4},{1,9},{5,13},{9,1},{13,5},{2,10},{6,14},... | collective-permute-start | bytes 98312 | tf_op jit(solution)/shard_map/ppermute | solution.py:361
  40.1 0.0 collective-permute-done.15.refs_3_.refs_4_
  40.1 0.4 shard_map.109
  40.5 4.0 %collective-permute-done.14.refs_3_ = f32[64,128]{1,0:T(8,128)S(1)} collective-permute-done((f32[64,128]{1,0:T(8,128)S(1)}, f32[64,128]{1,0:T(8,128)S(1)}, u32[]{:S(2)}, u32[]{:S(2)}) %collective-permute-start.14) | collective-permute-done | bytes 32800 | tf_op jit(solution)/shard_map/ppermute | solution.py:361
  44.5 0.0 collective-permute-done.12.refs_1_
  44.5 0.0 collective-permute-done.13.refs_2_
  44.5 0.4 shard_map.110
  44.9 1.6 %collective-permute-start.16 = (f32[112,128]{1,0:T(8,128)S(1)}, f32[112,128]{1,0:T(8,128)S(1)}, u32[]{:S(2)}, u32[]{:S(2)}) collective-permute-start(f32[112,128]{1,0:T(8,128)S(1)} %get-tuple-element.68), channel_id=1, source_target_pairs={{0,2},{2,0},{1,3},{3,1},{4,6},{6,4},{5,7},{7,5},{8,10},{10,8},{9,1... | collective-permute-start | bytes 172040 | tf_op jit(solution)/shard_map/ppermute | solution.py:350
  46.5 0.0 collective-permute-start.20
  46.5 2.7 %collective-permute-done.16.refs_1_.refs_2_ = f32[112,128]{1,0:T(8,128)S(1)} collective-permute-done((f32[112,128]{1,0:T(8,128)S(1)}, f32[112,128]{1,0:T(8,128)S(1)}, u32[]{:S(2)}, u32[]{:S(2)}) %collective-permute-start.16) | collective-permute-done | bytes 57376 | tf_op jit(solution)/shard_map/ppermute | solution.py:350
  49.2 0.5 collective-permute-start.17
  49.7 1.5 %collective-permute-start.18 = (f32[112,128]{1,0:T(8,128)S(1)}, f32[112,128]{1,0:T(8,128)S(1)}, u32[]{:S(2)}, u32[]{:S(2)}) collective-permute-start(f32[112,128]{1,0:T(8,128)S(1)} %get-tuple-element.72), channel_id=1, source_target_pairs={{0,12},{4,8},{8,4},{12,0},{1,13},{5,9},{9,5},{13,1},{2,14},{6,10},... | collective-permute-start | bytes 172040 | tf_op jit(solution)/shard_map/ppermute | solution.py:360
  51.2 1.5 %collective-permute-start.19 = (f32[64,128]{1,0:T(8,128)S(1)}, f32[64,128]{1,0:T(8,128)S(1)}, u32[]{:S(2)}, u32[]{:S(2)}) collective-permute-start(f32[64,128]{1,0:T(8,128)S(1)} %slice_add_fusion.refs_0_), channel_id=1, source_target_pairs={{0,8},{4,12},{8,0},{12,4},{1,9},{5,13},{9,1},{13,5},{2,10},{6,14},... | collective-permute-start | bytes 98312 | tf_op jit(solution)/shard_map/ppermute | solution.py:361
  52.8 0.0 collective-permute-done.20.refs_3_.refs_4_
  52.8 0.4 shard_map.111.refs_4_
  53.2 3.2 %collective-permute-done.19.refs_3_ = f32[64,128]{1,0:T(8,128)S(1)} collective-permute-done((f32[64,128]{1,0:T(8,128)S(1)}, f32[64,128]{1,0:T(8,128)S(1)}, u32[]{:S(2)}, u32[]{:S(2)}) %collective-permute-start.19) | collective-permute-done | bytes 32800 | tf_op jit(solution)/shard_map/ppermute | solution.py:361
  56.4 0.0 collective-permute-done.17.refs_1_
  56.4 0.0 collective-permute-done.18.refs_2_
  56.4 1.7 %shard_map.112 = (f32[3,16,16,128]{3,2,1,0:T(8,128)}, f32[8,128]{1,0:T(8,128)}) custom-call(f32[64,128]{1,0:T(8,128)S(1)} %slice_add_fusion.refs_0_, f32[112,128]{1,0:T(8,128)S(1)} %collective-permute-done.17.refs_1_, f32[112,128]{1,0:T(8,128)S(1)} %collective-permute-done.18.refs_2_, f32[64,128]{1,0:T(8,128)S(1)} %collective-permute-done.19.refs_3_, ...), custom_call_target="tpu_custom_call" | custom-call | tf_op jit(solution)/shard_map/pallas_call | solution.py:303
  (17 shorter events, 0.1 us)
Async XLA Ops:
  0.6 6.2 %copy-start.1 = (f32[3,16,16,128]{3,2,1,0:T(8,128)S(1)}, f32[3,16,16,128]{3,2,1,0:T(8,128)}, u32[]{:S(2)}) copy-start(f32[3,16,16,128]{3,2,1,0:T(8,128)} %refs_13_.1) | copy-start | bytes 1179652
  0.6 6.2 %copy-start = (f32[3,16,16,128]{3,2,1,0:T(8,128)S(1)}, f32[3,16,16,128]{3,2,1,0:T(8,128)}, u32[]{:S(2)}) copy-start(f32[3,16,16,128]{3,2,1,0:T(8,128)} %refs_9_.3) | copy-start | bytes 1179652
  3.8 6.3 %copy-start.9 = (f32[64,128]{1,0:T(8,128)S(1)}, f32[64,128]{1,0:T(8,128)}, u32[]{:S(2)}) copy-start(f32[64,128]{1,0:T(8,128)} %get-tuple-element.38) | copy-start | bytes 98308
  3.8 6.3 %copy-start.10 = (f32[64,128]{1,0:T(8,128)S(1)}, f32[64,128]{1,0:T(8,128)}, u32[]{:S(2)}) copy-start(f32[64,128]{1,0:T(8,128)} %get-tuple-element.39) | copy-start | bytes 98308
  3.8 5.5 %collective-permute-start = (f32[128,128]{1,0:T(8,128)}, f32[128,128]{1,0:T(8,128)S(1)}, u32[]{:S(2)}, u32[]{:S(2)}) collective-permute-start(f32[128,128]{1,0:T(8,128)} %get-tuple-element.37), channel_id=1, source_target_pairs={{0,2},{2,0},{1,3},{3,1},{4,6},{6,4},{5,7},{7,5},{8,10},{10,8},{9,1... | collective-permute-start | bytes 196616 | tf_op jit(solution)/shard_map/ppermute | solution.py:350
  6.9 8.1 %collective-permute-start.4 = (f32[3,16,16,128]{3,2,1,0:T(8,128)S(1)}, f32[3,16,16,128]{3,2,1,0:T(8,128)S(1)}, u32[]{:S(2)}, u32[]{:S(2)}) collective-permute-start(f32[3,16,16,128]{3,2,1,0:T(8,128)S(1)} %copy-done.1), channel_id=1, source_target_pairs={{0,1},{1,0},{2,3},{3,2},{4,5},{5,4},{6,7},{7,6},{8,9},{9,8},{10,11... | collective-permute-start | bytes 1179656 | tf_op jit(solution)/shard_map/ppermute | solution.py:332
  6.9 8.1 %collective-permute-start.5 = (f32[3,16,16,128]{3,2,1,0:T(8,128)S(1)}, f32[3,16,16,128]{3,2,1,0:T(8,128)S(1)}, u32[]{:S(2)}, u32[]{:S(2)}) collective-permute-start(f32[3,16,16,128]{3,2,1,0:T(8,128)S(1)} %copy-done), channel_id=1, source_target_pairs={{0,1},{1,0},{2,3},{3,2},{4,5},{5,4},{6,7},{7,6},{8,9},{9,8},{10,11... | collective-permute-start | bytes 1179656 | tf_op jit(solution)/shard_map/ppermute | solution.py:332
  9.3 5.7 %copy-start.3 = (s32[16,16,128]{2,1,0:T(8,128)S(1)}, s32[16,16,128]{2,1,0:T(8,128)}, u32[]{:S(2)}) copy-start(s32[16,16,128]{2,1,0:T(8,128)} %refs_10_.2) | copy-start | bytes 393220
  10.1 4.9 %copy-start.2 = (f32[16,16,128]{2,1,0:T(8,128)S(1)}, f32[16,16,128]{2,1,0:T(8,128)}, u32[]{:S(2)}) copy-start(f32[16,16,128]{2,1,0:T(8,128)} %refs_10_.3) | copy-start | bytes 393220
  10.1 4.9 %copy-start.4 = (f32[8,128]{1,0:T(8,128)S(1)}, f32[8,128]{1,0:T(8,128)}, u32[]{:S(2)}) copy-start(f32[8,128]{1,0:T(8,128)} %refs_5_.9) | copy-start | bytes 12292
  10.2 4.9 %copy-start.5 = (f32[8,3]{0,1:T(4,128)S(1)}, f32[8,3]{0,1:T(4,128)}, u32[]{:S(2)}) copy-start(f32[8,3]{0,1:T(4,128)} %param.13) | copy-start | bytes 292
  10.2 4.8 %copy-start.6 = (s32[128]{0:T(128)S(1)}, s32[128]{0:T(128)}, u32[]{:S(2)}) copy-start(s32[128]{0:T(128)} %param.14) | copy-start | bytes 1540
  10.2 4.8 %copy-start.7 = (s32[128,1]{0,1:T(1,128)S(1)}, s32[128,1]{0,1:T(1,128)}, u32[]{:S(2)}) copy-start(s32[128,1]{0,1:T(1,128)} %param.15) | copy-start | bytes 1540
  10.2 4.8 %copy-start.8 = (s32[128]{0:T(128)S(1)}, s32[128]{0:T(128)}, u32[]{:S(2)}) copy-start(s32[128]{0:T(128)} %param.16) | copy-start | bytes 1540
  10.2 9.8 %collective-permute-start.1 = (f32[128,128]{1,0:T(8,128)S(1)}, f32[128,128]{1,0:T(8,128)S(1)}, u32[]{:S(2)}, u32[]{:S(2)}) collective-permute-start(f32[128,128]{1,0:T(8,128)S(1)} %get-tuple-element.79), channel_id=1, source_target_pairs={{0,4},{4,0},{8,12},{12,8},{1,5},{5,1},{9,13},{13,9},{2,6},{6,2},{1... | collective-permute-start | bytes 196616 | tf_op jit(solution)/shard_map/ppermute | solution.py:359
  12.4 7.6 %collective-permute-start.2 = (f32[128,128]{1,0:T(8,128)S(1)}, f32[128,128]{1,0:T(8,128)S(1)}, u32[]{:S(2)}, u32[]{:S(2)}) collective-permute-start(f32[128,128]{1,0:T(8,128)S(1)} %get-tuple-element.78), channel_id=1, source_target_pairs={{0,12},{4,8},{8,4},{12,0},{1,13},{5,9},{9,5},{13,1},{2,14},{6,10},... | collective-permute-start | bytes 196616 | tf_op jit(solution)/shard_map/ppermute | solution.py:360
  14.9 5.2 %collective-permute-start.3 = (f32[64,128]{1,0:T(8,128)S(1)}, f32[64,128]{1,0:T(8,128)S(1)}, u32[]{:S(2)}, u32[]{:S(2)}) collective-permute-start(f32[64,128]{1,0:T(8,128)S(1)} %slice_add_fusion.3.refs_0_), channel_id=1, source_target_pairs={{0,8},{4,12},{8,0},{12,4},{1,9},{5,13},{9,1},{13,5},{2,10},{6,14},... | collective-permute-start | bytes 98312 | tf_op jit(solution)/shard_map/ppermute | solution.py:361
  20.4 4.2 %collective-permute-start.6 = (f32[112,128]{1,0:T(8,128)S(1)}, f32[112,128]{1,0:T(8,128)S(1)}, u32[]{:S(2)}, u32[]{:S(2)}) collective-permute-start(f32[112,128]{1,0:T(8,128)S(1)} %get-tuple-element.50), channel_id=1, source_target_pairs={{0,2},{2,0},{1,3},{3,1},{4,6},{6,4},{5,7},{7,5},{8,10},{10,8},{9,1... | collective-permute-start | bytes 172040 | tf_op jit(solution)/shard_map/ppermute | solution.py:350
  22.0 6.3 %collective-permute-start.10 = (f32[3,16,16,128]{3,2,1,0:T(8,128)S(1)}, f32[3,16,16,128]{3,2,1,0:T(8,128)S(1)}, u32[]{:S(2)}, u32[]{:S(2)}) collective-permute-start(f32[3,16,16,128]{3,2,1,0:T(8,128)S(1)} %get-tuple-element.53.refs_0_), channel_id=1, source_target_pairs={{0,1},{1,0},{2,3},{3,2},{4,5},{5,4},{6,7},{7,6},{8,9},{9,8},{10,11... | collective-permute-start | bytes 1179656 | tf_op jit(solution)/shard_map/ppermute | solution.py:332
  24.7 7.2 %collective-permute-start.7 = (f32[112,128]{1,0:T(8,128)S(1)}, f32[112,128]{1,0:T(8,128)S(1)}, u32[]{:S(2)}, u32[]{:S(2)}) collective-permute-start(f32[112,128]{1,0:T(8,128)S(1)} %get-tuple-element.77), channel_id=1, source_target_pairs={{0,4},{4,0},{8,12},{12,8},{1,5},{5,1},{9,13},{13,9},{2,6},{6,2},{1... | collective-permute-start | bytes 172040 | tf_op jit(solution)/shard_map/ppermute | solution.py:359
  25.2 6.7 %collective-permute-start.8 = (f32[112,128]{1,0:T(8,128)S(1)}, f32[112,128]{1,0:T(8,128)S(1)}, u32[]{:S(2)}, u32[]{:S(2)}) collective-permute-start(f32[112,128]{1,0:T(8,128)S(1)} %get-tuple-element.76), channel_id=1, source_target_pairs={{0,12},{4,8},{8,4},{12,0},{1,13},{5,9},{9,5},{13,1},{2,14},{6,10},... | collective-permute-start | bytes 172040 | tf_op jit(solution)/shard_map/ppermute | solution.py:360
  26.6 5.2 %collective-permute-start.9 = (f32[64,128]{1,0:T(8,128)S(1)}, f32[64,128]{1,0:T(8,128)S(1)}, u32[]{:S(2)}, u32[]{:S(2)}) collective-permute-start(f32[64,128]{1,0:T(8,128)S(1)} %slice_add_fusion.2.refs_0_), channel_id=1, source_target_pairs={{0,8},{4,12},{8,0},{12,4},{1,9},{5,13},{9,1},{13,5},{2,10},{6,14},... | collective-permute-start | bytes 98312 | tf_op jit(solution)/shard_map/ppermute | solution.py:361
  32.3 4.2 %collective-permute-start.11 = (f32[112,128]{1,0:T(8,128)S(1)}, f32[112,128]{1,0:T(8,128)S(1)}, u32[]{:S(2)}, u32[]{:S(2)}) collective-permute-start(f32[112,128]{1,0:T(8,128)S(1)} %get-tuple-element.62), channel_id=1, source_target_pairs={{0,2},{2,0},{1,3},{3,1},{4,6},{6,4},{5,7},{7,5},{8,10},{10,8},{9,1... | collective-permute-start | bytes 172040 | tf_op jit(solution)/shard_map/ppermute | solution.py:350
  33.8 6.3 %collective-permute-start.15 = (f32[3,16,16,128]{3,2,1,0:T(8,128)S(1)}, f32[3,16,16,128]{3,2,1,0:T(8,128)S(1)}, u32[]{:S(2)}, u32[]{:S(2)}) collective-permute-start(f32[3,16,16,128]{3,2,1,0:T(8,128)S(1)} %get-tuple-element.65.refs_0_), channel_id=1, source_target_pairs={{0,1},{1,0},{2,3},{3,2},{4,5},{5,4},{6,7},{7,6},{8,9},{9,8},{10,11... | collective-permute-start | bytes 1179656 | tf_op jit(solution)/shard_map/ppermute | solution.py:332
  36.6 8.0 %collective-permute-start.12 = (f32[112,128]{1,0:T(8,128)S(1)}, f32[112,128]{1,0:T(8,128)S(1)}, u32[]{:S(2)}, u32[]{:S(2)}) collective-permute-start(f32[112,128]{1,0:T(8,128)S(1)} %get-tuple-element.75), channel_id=1, source_target_pairs={{0,4},{4,0},{8,12},{12,8},{1,5},{5,1},{9,13},{13,9},{2,6},{6,2},{1... | collective-permute-start | bytes 172040 | tf_op jit(solution)/shard_map/ppermute | solution.py:359
  37.0 7.5 %collective-permute-start.13 = (f32[112,128]{1,0:T(8,128)S(1)}, f32[112,128]{1,0:T(8,128)S(1)}, u32[]{:S(2)}, u32[]{:S(2)}) collective-permute-start(f32[112,128]{1,0:T(8,128)S(1)} %get-tuple-element.74), channel_id=1, source_target_pairs={{0,12},{4,8},{8,4},{12,0},{1,13},{5,9},{9,5},{13,1},{2,14},{6,10},... | collective-permute-start | bytes 172040 | tf_op jit(solution)/shard_map/ppermute | solution.py:360
  39.4 5.2 %collective-permute-start.14 = (f32[64,128]{1,0:T(8,128)S(1)}, f32[64,128]{1,0:T(8,128)S(1)}, u32[]{:S(2)}, u32[]{:S(2)}) collective-permute-start(f32[64,128]{1,0:T(8,128)S(1)} %slice_add_fusion.1.refs_0_), channel_id=1, source_target_pairs={{0,8},{4,12},{8,0},{12,4},{1,9},{5,13},{9,1},{13,5},{2,10},{6,14},... | collective-permute-start | bytes 98312 | tf_op jit(solution)/shard_map/ppermute | solution.py:361
  44.9 4.2 %collective-permute-start.16 = (f32[112,128]{1,0:T(8,128)S(1)}, f32[112,128]{1,0:T(8,128)S(1)}, u32[]{:S(2)}, u32[]{:S(2)}) collective-permute-start(f32[112,128]{1,0:T(8,128)S(1)} %get-tuple-element.68), channel_id=1, source_target_pairs={{0,2},{2,0},{1,3},{3,1},{4,6},{6,4},{5,7},{7,5},{8,10},{10,8},{9,1... | collective-permute-start | bytes 172040 | tf_op jit(solution)/shard_map/ppermute | solution.py:350
  46.5 6.3 %collective-permute-start.20 = (f32[3,16,16,128]{3,2,1,0:T(8,128)S(1)}, f32[3,16,16,128]{3,2,1,0:T(8,128)S(1)}, u32[]{:S(2)}, u32[]{:S(2)}) collective-permute-start(f32[3,16,16,128]{3,2,1,0:T(8,128)S(1)} %get-tuple-element.71.refs_0_), channel_id=1, source_target_pairs={{0,1},{1,0},{2,3},{3,2},{4,5},{5,4},{6,7},{7,6},{8,9},{9,8},{10,11... | collective-permute-start | bytes 1179656 | tf_op jit(solution)/shard_map/ppermute | solution.py:332
  49.2 7.2 %collective-permute-start.17 = (f32[112,128]{1,0:T(8,128)S(1)}, f32[112,128]{1,0:T(8,128)S(1)}, u32[]{:S(2)}, u32[]{:S(2)}) collective-permute-start(f32[112,128]{1,0:T(8,128)S(1)} %get-tuple-element.73), channel_id=1, source_target_pairs={{0,4},{4,0},{8,12},{12,8},{1,5},{5,1},{9,13},{13,9},{2,6},{6,2},{1... | collective-permute-start | bytes 172040 | tf_op jit(solution)/shard_map/ppermute | solution.py:359
  49.7 6.7 %collective-permute-start.18 = (f32[112,128]{1,0:T(8,128)S(1)}, f32[112,128]{1,0:T(8,128)S(1)}, u32[]{:S(2)}, u32[]{:S(2)}) collective-permute-start(f32[112,128]{1,0:T(8,128)S(1)} %get-tuple-element.72), channel_id=1, source_target_pairs={{0,12},{4,8},{8,4},{12,0},{1,13},{5,9},{9,5},{13,1},{2,14},{6,10},... | collective-permute-start | bytes 172040 | tf_op jit(solution)/shard_map/ppermute | solution.py:360
  51.2 5.2 %collective-permute-start.19 = (f32[64,128]{1,0:T(8,128)S(1)}, f32[64,128]{1,0:T(8,128)S(1)}, u32[]{:S(2)}, u32[]{:S(2)}) collective-permute-start(f32[64,128]{1,0:T(8,128)S(1)} %slice_add_fusion.refs_0_), channel_id=1, source_target_pairs={{0,8},{4,12},{8,0},{12,4},{1,9},{5,13},{9,1},{13,5},{2,10},{6,14},... | collective-permute-start | bytes 98312 | tf_op jit(solution)/shard_map/ppermute | solution.py:361

commit v3 on v2

--- a/solution.py
+++ b/solution.py
@@ -88,7 +88,7 @@
 
 def first_kernel(names, *refs):
     r = Refs(zip(names, refs))
-    moved = ("column", "owner", "slot", "observed", "perm", "rock", "adj")
+    moved = ("column", "owner", "slot", "observed", "table", "perm", "rock", "adj")
     copies = {}
     for i, name in enumerate(moved):
         copies[name] = pltpu.make_async_copy(r[name + "_in"], r[name], r.sems.at[i])
@@ -225,7 +225,9 @@
     if last:
         own = r.observed.shape[0]
         r.combined[...] = total
-        r.sens[...] = r.combined[own_rows(own), :] + r.observed[...]
+        r.sens_held[...] = r.combined[own_rows(own), :] + r.observed[...]
+        copies = [pltpu.make_async_copy(r.sens_held, r.sens, r.sems.at[nx])]
+        copies[0].start()
     column_sum = counted(r.counts_t[...], jnp.tanh(total))
 
     def x_face(p, e):
@@ -236,7 +238,6 @@
         return jnp.where(odd("gx"), ring, one) if e else jnp.where(odd("gx"), one, ring)
 
     part = 4 if nx % 4 == 0 else 1
-    copies = []
     gx, size_x = lax.axis_index("gx"), lax.axis_size("gx")
     for x in range(nx):
         edge = x in (0, nx - 1)
@@ -306,7 +307,7 @@
         out_specs=[spec for spec, _, _ in outs.values()],
         out_shape=[jax.ShapeDtypeStruct(shape, kind) for _, shape, kind in outs.values()],
         scratch_shapes=list(scratch.values()),
-        compiler_params=pltpu.CompilerParams(vmem_limit_bytes=limit * MIB),
+        compiler_params=pltpu.CompilerParams(vmem_limit_bytes=int(limit * MIB)),
         cost_estimate=cost,
     )(*[array for _, array in ins.values()])
     return Refs(zip(outs, result))
@@ -381,18 +382,18 @@
         column=perf_column.reshape(1, rows), owner=perf_owner.reshape(1, rows),
         slot=perf_slot.reshape(1, rows),
     )
-    moved = dict(perf, observed=observed, perm=permeability, rock=rock_type, adj=adjoint)
-    ins = {"table": (SMEM, table)}
-    ins.update({name + "_in": (HBM, array) for name, array in moved.items()})
+    moved = dict(perf, observed=observed, perm=permeability, rock=rock_type, adj=adjoint, table=table)
+    ins = {name + "_in": (HBM, array) for name, array in moved.items()}
     outs = {
         "msg_y": (VMEM, (wells + 4 * nx, nz), F32),
         "face_a": (VMEM, (4 * ny, nz), F32),
         "face_b": (VMEM, (4 * ny, nz), F32),
     }
     scratch = {name: pltpu.VMEM(a.shape, a.dtype) for name, a in moved.items()}
+    scratch["table"] = pltpu.SMEM(table.shape, F32)
     scratch["combined"] = pltpu.VMEM((nx * ny, nz), F32)
     scratch["sems"] = pltpu.SemaphoreType.DMA((len(moved),))
-    sent = call(first_kernel, ins, outs, scratch, 60)
+    sent = call(first_kernel, ins, outs, scratch, 53.75)
     pm, pp = beside_z(permeability)
     adj = adjoint
     cost = pl.CostEstimate(flops=1, bytes_accessed=4 * MIB, transcendentals=0)
@@ -440,11 +441,12 @@
         else:
             ins.update(in_vmem(edge_t=edge.edge_t, edge_take=edge.edge_take))
         if last:
-            outs = {"new": (HBM, phases, F32), "sens": (VMEM, (own, nz), F32)}
+            outs = {"new": (HBM, phases, F32), "sens": (HBM, (own, nz), F32)}
             scratch = {
                 "combined": pltpu.VMEM((wells, nz), F32),
                 "held": pltpu.VMEM(phases, F32),
-                "sems": pltpu.SemaphoreType.DMA((nx,)),
+                "sens_held": pltpu.VMEM((own, nz), F32),
+                "sems": pltpu.SemaphoreType.DMA((nx + 1,)),
             }
         else:
             ins.update(in_vmem(

time: 58.2 us -> 55.9 us (0.960)
  Pallas kernels: 8.77 us -> 6.78 us
  other arithmetic: 0.87 us -> 0.07 us
  local copies, waits for them, and re-layouts: 0.06 us -> 0.7 us
    pallas_call x9, Pallas kernels: 8.77 us -> 6.78 us  [call(): pl.pallas_call(functools.partial(kernel, names), in_specs=[spec for spec,...]
    add x4, other arithmetic: 0.82 us -> 0.02 us  [over_gy(): return (msg_y[:wells] + got[:wells], got, got)]
    unnamed x22 -> x18, local copies, waits for them, and re-layouts: 0.06 us -> 0.7 us
  transfers between devices with their start and end apart: 21 -> 21, of which waited for: 8 -> 8; matrix products, arithmetic and copies ran while one was open for 1% -> 0% of each run, Pallas kernels for 5% -> 5%
where the time goes in v3:
time: 55.9 us; the launch traced here: 55.7 us
  waiting for transfers between devices  23.7 us (42%)
  starting transfers between devices  23.6 us (42%)
  Pallas kernels  6.78 us (12%)
  between operations  0.79 us (1%)
  local copies, waits for them, and re-layouts  0.7 us (1%)
    ppermute x4, waiting for transfers between devices, over_gx(): more3 = lax.ppermute(total, 'gx', swap(4, 2))  13.9 us
    ppermute x4, waiting for transfers between devices, over_gy(): got = lax.ppermute(msg_y, 'gy', swap(2, 1))  9.78 us
    ppermute x4, starting transfers between devices, over_gy(): got = lax.ppermute(msg_y, 'gy', swap(2, 1))  7.67 us
    ppermute x4, starting transfers between devices, over_gx(): more2 = lax.ppermute(jnp.concatenate([total, face_b]), 'gx', swap(4, 3))  7.65 us
    pallas_call x9, Pallas kernels, call(): pl.pallas_call(functools.partial(kernel, names), in_specs=[spec for spec,...  6.78 us
    ppermute x4, starting transfers between devices, over_gx(): more3 = lax.ppermute(total, 'gx', swap(4, 2))  4.11 us
    ppermute x4, starting transfers between devices, over_gx(): more1 = lax.ppermute(jnp.concatenate([total, face_a]), 'gx', swap(4, 1))  3.66 us
  transfers between devices with their start and end apart: 21, of which 8 were waited for; matrix products, arithmetic and copies ran while one was open for 0% of the time, Pallas kernels for 5%

profile of v3, /device:TPU:0, one launch (start us, length us, event | category | flops | bytes accessed | tf_op | source)
XLA Modules:
  0.0 55.7 jit_solution(13898688057010706674)
XLA Ops:
  0.6 0.0 copy-start.4
  0.6 0.0 copy-start.5
  0.7 0.0 copy-start.6
  0.7 0.0 copy-start.7
  0.7 0.0 copy-start.8
  0.7 0.6 %copy-done.4 = f32[8,128]{1,0:T(8,128)S(1)} copy-done((f32[8,128]{1,0:T(8,128)S(1)}, f32[8,128]{1,0:T(8,128)}, u32[]{:S(2)}) %copy-start.4) | copy-done | bytes 4120
  1.3 0.0 copy-done.5
  1.3 0.0 copy-done.6
  1.3 0.0 copy-done.7
  1.3 0.0 copy-done.8
  1.4 1.8 %shard_map.104 = (f32[128,128]{1,0:T(8,128)S(1)}, f32[64,128]{1,0:T(8,128)S(1)}, f32[64,128]{1,0:T(8,128)S(1)}) custom-call(s32[1,128]{1,0:T(1,128)S(1)} %bitcast.6, s32[1,128]{1,0:T(1,128)S(1)} %bitcast.8, s32[1,128]{1,0:T(1,128)S(1)} %bitcast.10, f32[8,128]{1,0:T(8,128)S(1)} %copy-done.4, f32[3,16,16,128]{3,2,1,0:T(8,128)} %refs_9_.3, ...), custom_call_target="tpu_custom_call" | custom-call | tf_op jit(solution)/shard_map/pallas_call | solution.py:304
  3.1 3.0 %collective-permute-start = (f32[128,128]{1,0:T(8,128)S(1)}, f32[128,128]{1,0:T(8,128)S(1)}, u32[]{:S(2)}, u32[]{:S(2)}) collective-permute-start(f32[128,128]{1,0:T(8,128)S(1)} %get-tuple-element.37), channel_id=1, source_target_pairs={{0,2},{2,0},{1,3},{3,1},{4,6},{6,4},{5,7},{7,5},{8,10},{10,8},{9,1... | collective-permute-start | bytes 196616 | tf_op jit(solution)/shard_map/ppermute | solution.py:351
  6.1 0.0 copy-done.1
  6.1 0.0 collective-permute-start.4
  6.1 0.5 collective-permute-start.5
  6.6 1.7 %collective-permute-done.refs_1_.refs_2_ = f32[128,128]{1,0:T(8,128)S(1)} collective-permute-done((f32[128,128]{1,0:T(8,128)S(1)}, f32[128,128]{1,0:T(8,128)S(1)}, u32[]{:S(2)}, u32[]{:S(2)}) %collective-permute-start) | collective-permute-done | bytes 65568 | tf_op jit(solution)/shard_map/ppermute | solution.py:351
  8.4 0.0 copy-start.2
  8.4 2.2 %collective-permute-start.1 = (f32[128,128]{1,0:T(8,128)S(1)}, f32[128,128]{1,0:T(8,128)S(1)}, u32[]{:S(2)}, u32[]{:S(2)}) collective-permute-start(f32[128,128]{1,0:T(8,128)S(1)} %get-tuple-element.79), channel_id=1, source_target_pairs={{0,4},{4,0},{8,12},{12,8},{1,5},{5,1},{9,13},{13,9},{2,6},{6,2},{1... | collective-permute-start | bytes 196616 | tf_op jit(solution)/shard_map/ppermute | solution.py:360
  10.6 2.5 %collective-permute-start.2 = (f32[128,128]{1,0:T(8,128)S(1)}, f32[128,128]{1,0:T(8,128)S(1)}, u32[]{:S(2)}, u32[]{:S(2)}) collective-permute-start(f32[128,128]{1,0:T(8,128)S(1)} %get-tuple-element.78), channel_id=1, source_target_pairs={{0,12},{4,8},{8,4},{12,0},{1,13},{5,9},{9,5},{13,1},{2,14},{6,10},... | collective-permute-start | bytes 196616 | tf_op jit(solution)/shard_map/ppermute | solution.py:361
  13.1 0.1 collective-permute-start.3
  13.2 0.0 collective-permute-done.4.refs_3_.refs_4_
  13.2 0.0 collective-permute-done.5.refs_7_.refs_8_
  13.2 0.0 copy-done.2
  13.2 1.5 %shard_map.105 = (f32[3,16,16,128]{3,2,1,0:T(8,128)S(1)}, f32[16,16,128]{2,1,0:T(8,128)S(1)}, f32[6,16,16,128]{3,2,1,0:T(8,128)S(1)}, f32[16,16,128]{2,1,0:T(8,1...) custom-call(f32[3,16,16,128]{3,2,1,0:T(8,128)S(1)} %copy-done.1, ...), custom_call_target="tpu_custom_call" | custom-call | flops 1 | bytes 4194304 | tf_op jit(solution)/shard_map/pallas_call | solution.py:304
  14.7 3.5 %collective-permute-done.3.refs_3_ = f32[64,128]{1,0:T(8,128)S(1)} collective-permute-done((f32[64,128]{1,0:T(8,128)S(1)}, f32[64,128]{1,0:T(8,128)S(1)}, u32[]{:S(2)}, u32[]{:S(2)}) %collective-permute-start.3) | collective-permute-done | bytes 32800 | tf_op jit(solution)/shard_map/ppermute | solution.py:362
  18.2 0.0 collective-permute-done.1.refs_1_
  18.2 0.0 collective-permute-done.2.refs_2_
  18.2 0.4 shard_map.106
  18.6 1.6 %collective-permute-start.6 = (f32[112,128]{1,0:T(8,128)S(1)}, f32[112,128]{1,0:T(8,128)S(1)}, u32[]{:S(2)}, u32[]{:S(2)}) collective-permute-start(f32[112,128]{1,0:T(8,128)S(1)} %get-tuple-element.50), channel_id=1, source_target_pairs={{0,2},{2,0},{1,3},{3,1},{4,6},{6,4},{5,7},{7,5},{8,10},{10,8},{9,1... | collective-permute-start | bytes 172040 | tf_op jit(solution)/shard_map/ppermute | solution.py:351
  20.2 0.0 collective-permute-start.10
  20.2 2.7 %collective-permute-done.6.refs_1_.refs_2_ = f32[112,128]{1,0:T(8,128)S(1)} collective-permute-done((f32[112,128]{1,0:T(8,128)S(1)}, f32[112,128]{1,0:T(8,128)S(1)}, u32[]{:S(2)}, u32[]{:S(2)}) %collective-permute-start.6) | collective-permute-done | bytes 57376 | tf_op jit(solution)/shard_map/ppermute | solution.py:351
  22.9 0.5 collective-permute-start.7
  23.4 1.4 %collective-permute-start.8 = (f32[112,128]{1,0:T(8,128)S(1)}, f32[112,128]{1,0:T(8,128)S(1)}, u32[]{:S(2)}, u32[]{:S(2)}) collective-permute-start(f32[112,128]{1,0:T(8,128)S(1)} %get-tuple-element.76), channel_id=1, source_target_pairs={{0,12},{4,8},{8,4},{12,0},{1,13},{5,9},{9,5},{13,1},{2,14},{6,10},... | collective-permute-start | bytes 172040 | tf_op jit(solution)/shard_map/ppermute | solution.py:361
  24.8 1.6 %collective-permute-start.9 = (f32[64,128]{1,0:T(8,128)S(1)}, f32[64,128]{1,0:T(8,128)S(1)}, u32[]{:S(2)}, u32[]{:S(2)}) collective-permute-start(f32[64,128]{1,0:T(8,128)S(1)} %slice_add_fusion.2.refs_0_), channel_id=1, source_target_pairs={{0,8},{4,12},{8,0},{12,4},{1,9},{5,13},{9,1},{13,5},{2,10},{6,14},... | collective-permute-start | bytes 98312 | tf_op jit(solution)/shard_map/ppermute | solution.py:362
  26.5 0.0 collective-permute-done.10.refs_3_.refs_4_
  26.5 0.4 shard_map.107
  26.9 3.2 %collective-permute-done.9.refs_3_ = f32[64,128]{1,0:T(8,128)S(1)} collective-permute-done((f32[64,128]{1,0:T(8,128)S(1)}, f32[64,128]{1,0:T(8,128)S(1)}, u32[]{:S(2)}, u32[]{:S(2)}) %collective-permute-start.9) | collective-permute-done | bytes 32800 | tf_op jit(solution)/shard_map/ppermute | solution.py:362
  30.1 0.0 collective-permute-done.7.refs_1_
  30.1 0.0 collective-permute-done.8.refs_2_
  30.1 0.4 shard_map.108
  30.5 1.6 %collective-permute-start.11 = (f32[112,128]{1,0:T(8,128)S(1)}, f32[112,128]{1,0:T(8,128)S(1)}, u32[]{:S(2)}, u32[]{:S(2)}) collective-permute-start(f32[112,128]{1,0:T(8,128)S(1)} %get-tuple-element.62), channel_id=1, source_target_pairs={{0,2},{2,0},{1,3},{3,1},{4,6},{6,4},{5,7},{7,5},{8,10},{10,8},{9,1... | collective-permute-start | bytes 172040 | tf_op jit(solution)/shard_map/ppermute | solution.py:351
  32.0 0.0 collective-permute-start.15
  32.0 2.7 %collective-permute-done.11.refs_1_.refs_2_ = f32[112,128]{1,0:T(8,128)S(1)} collective-permute-done((f32[112,128]{1,0:T(8,128)S(1)}, f32[112,128]{1,0:T(8,128)S(1)}, u32[]{:S(2)}, u32[]{:S(2)}) %collective-permute-start.11) | collective-permute-done | bytes 57376 | tf_op jit(solution)/shard_map/ppermute | solution.py:351
  34.8 0.5 collective-permute-start.12
  35.2 2.3 %collective-permute-start.13 = (f32[112,128]{1,0:T(8,128)S(1)}, f32[112,128]{1,0:T(8,128)S(1)}, u32[]{:S(2)}, u32[]{:S(2)}) collective-permute-start(f32[112,128]{1,0:T(8,128)S(1)} %get-tuple-element.74), channel_id=1, source_target_pairs={{0,12},{4,8},{8,4},{12,0},{1,13},{5,9},{9,5},{13,1},{2,14},{6,10},... | collective-permute-start | bytes 172040 | tf_op jit(solution)/shard_map/ppermute | solution.py:361
  37.6 0.7 %collective-permute-start.14 = (f32[64,128]{1,0:T(8,128)S(1)}, f32[64,128]{1,0:T(8,128)S(1)}, u32[]{:S(2)}, u32[]{:S(2)}) collective-permute-start(f32[64,128]{1,0:T(8,128)S(1)} %slice_add_fusion.1.refs_0_), channel_id=1, source_target_pairs={{0,8},{4,12},{8,0},{12,4},{1,9},{5,13},{9,1},{13,5},{2,10},{6,14},... | collective-permute-start | bytes 98312 | tf_op jit(solution)/shard_map/ppermute | solution.py:362
  38.3 0.0 collective-permute-done.15.refs_3_.refs_4_
  38.3 0.4 shard_map.109
  38.7 4.0 %collective-permute-done.14.refs_3_ = f32[64,128]{1,0:T(8,128)S(1)} collective-permute-done((f32[64,128]{1,0:T(8,128)S(1)}, f32[64,128]{1,0:T(8,128)S(1)}, u32[]{:S(2)}, u32[]{:S(2)}) %collective-permute-start.14) | collective-permute-done | bytes 32800 | tf_op jit(solution)/shard_map/ppermute | solution.py:362
  42.7 0.0 collective-permute-done.12.refs_1_
  42.7 0.0 collective-permute-done.13.refs_2_
  42.7 0.4 shard_map.110
  43.2 1.6 %collective-permute-start.16 = (f32[112,128]{1,0:T(8,128)S(1)}, f32[112,128]{1,0:T(8,128)S(1)}, u32[]{:S(2)}, u32[]{:S(2)}) collective-permute-start(f32[112,128]{1,0:T(8,128)S(1)} %get-tuple-element.68), channel_id=1, source_target_pairs={{0,2},{2,0},{1,3},{3,1},{4,6},{6,4},{5,7},{7,5},{8,10},{10,8},{9,1... | collective-permute-start | bytes 172040 | tf_op jit(solution)/shard_map/ppermute | solution.py:351
  44.7 0.0 collective-permute-start.20
  44.7 2.7 %collective-permute-done.16.refs_1_.refs_2_ = f32[112,128]{1,0:T(8,128)S(1)} collective-permute-done((f32[112,128]{1,0:T(8,128)S(1)}, f32[112,128]{1,0:T(8,128)S(1)}, u32[]{:S(2)}, u32[]{:S(2)}) %collective-permute-start.16) | collective-permute-done | bytes 57376 | tf_op jit(solution)/shard_map/ppermute | solution.py:351
  47.4 0.5 collective-permute-start.17
  47.9 1.4 %collective-permute-start.18 = (f32[112,128]{1,0:T(8,128)S(1)}, f32[112,128]{1,0:T(8,128)S(1)}, u32[]{:S(2)}, u32[]{:S(2)}) collective-permute-start(f32[112,128]{1,0:T(8,128)S(1)} %get-tuple-element.72), channel_id=1, source_target_pairs={{0,12},{4,8},{8,4},{12,0},{1,13},{5,9},{9,5},{13,1},{2,14},{6,10},... | collective-permute-start | bytes 172040 | tf_op jit(solution)/shard_map/ppermute | solution.py:361
  49.3 1.6 %collective-permute-start.19 = (f32[64,128]{1,0:T(8,128)S(1)}, f32[64,128]{1,0:T(8,128)S(1)}, u32[]{:S(2)}, u32[]{:S(2)}) collective-permute-start(f32[64,128]{1,0:T(8,128)S(1)} %slice_add_fusion.refs_0_), channel_id=1, source_target_pairs={{0,8},{4,12},{8,0},{12,4},{1,9},{5,13},{9,1},{13,5},{2,10},{6,14},... | collective-permute-start | bytes 98312 | tf_op jit(solution)/shard_map/ppermute | solution.py:362
  51.0 0.0 collective-permute-done.20.refs_3_.refs_4_
  51.0 0.4 shard_map.111.refs_4_
  51.4 3.2 %collective-permute-done.19.refs_3_ = f32[64,128]{1,0:T(8,128)S(1)} collective-permute-done((f32[64,128]{1,0:T(8,128)S(1)}, f32[64,128]{1,0:T(8,128)S(1)}, u32[]{:S(2)}, u32[]{:S(2)}) %collective-permute-start.19) | collective-permute-done | bytes 32800 | tf_op jit(solution)/shard_map/ppermute | solution.py:362
  54.6 0.0 collective-permute-done.17.refs_1_
  54.6 0.0 collective-permute-done.18.refs_2_
  54.6 1.1 %shard_map.112 = (f32[3,16,16,128]{3,2,1,0:T(8,128)}, f32[8,128]{1,0:T(8,128)}) custom-call(f32[64,128]{1,0:T(8,128)S(1)} %slice_add_fusion.refs_0_, f32[112,128]{1,0:T(8,128)S(1)} %collective-permute-done.17.refs_1_, f32[112,128]{1,0:T(8,128)S(1)} %collective-permute-done.18.refs_2_, f32[64,128]{1,0:T(8,128)S(1)} %collective-permute-done.19.refs_3_, ...), custom_call_target="tpu_custom_call" | custom-call | tf_op jit(solution)/shard_map/pallas_call | solution.py:304
  (13 shorter events, 0.1 us)
Async XLA Ops:
  0.6 0.7 %copy-start.4 = (f32[8,128]{1,0:T(8,128)S(1)}, f32[8,128]{1,0:T(8,128)}, u32[]{:S(2)}) copy-start(f32[8,128]{1,0:T(8,128)} %refs_5_.9) | copy-start | bytes 12292
  0.6 0.7 %copy-start.5 = (f32[8,3]{0,1:T(4,128)S(1)}, f32[8,3]{0,1:T(4,128)}, u32[]{:S(2)}) copy-start(f32[8,3]{0,1:T(4,128)} %param.13) | copy-start | bytes 292
  0.7 0.7 %copy-start.6 = (s32[128]{0:T(128)S(1)}, s32[128]{0:T(128)}, u32[]{:S(2)}) copy-start(s32[128]{0:T(128)} %param.14) | copy-start | bytes 1540
  0.7 0.7 %copy-start.7 = (s32[128,1]{0,1:T(1,128)S(1)}, s32[128,1]{0,1:T(1,128)}, u32[]{:S(2)}) copy-start(s32[128,1]{0,1:T(1,128)} %param.15) | copy-start | bytes 1540
  0.7 0.7 %copy-start.8 = (s32[128]{0:T(128)S(1)}, s32[128]{0:T(128)}, u32[]{:S(2)}) copy-start(s32[128]{0:T(128)} %param.16) | copy-start | bytes 1540
  1.4 4.8 %copy-start.1 = (f32[3,16,16,128]{3,2,1,0:T(8,128)S(1)}, f32[3,16,16,128]{3,2,1,0:T(8,128)}, u32[]{:S(2)}) copy-start(f32[3,16,16,128]{3,2,1,0:T(8,128)} %refs_13_.1) | copy-start | bytes 1179652
  1.4 4.8 %copy-start = (f32[3,16,16,128]{3,2,1,0:T(8,128)S(1)}, f32[3,16,16,128]{3,2,1,0:T(8,128)}, u32[]{:S(2)}) copy-start(f32[3,16,16,128]{3,2,1,0:T(8,128)} %refs_9_.3) | copy-start | bytes 1179652
  3.1 5.2 %collective-permute-start = (f32[128,128]{1,0:T(8,128)S(1)}, f32[128,128]{1,0:T(8,128)S(1)}, u32[]{:S(2)}, u32[]{:S(2)}) collective-permute-start(f32[128,128]{1,0:T(8,128)S(1)} %get-tuple-element.37), channel_id=1, source_target_pairs={{0,2},{2,0},{1,3},{3,1},{4,6},{6,4},{5,7},{7,5},{8,10},{10,8},{9,1... | collective-permute-start | bytes 196616 | tf_op jit(solution)/shard_map/ppermute | solution.py:351
  6.1 7.1 %collective-permute-start.4 = (f32[3,16,16,128]{3,2,1,0:T(8,128)S(1)}, f32[3,16,16,128]{3,2,1,0:T(8,128)S(1)}, u32[]{:S(2)}, u32[]{:S(2)}) collective-permute-start(f32[3,16,16,128]{3,2,1,0:T(8,128)S(1)} %copy-done.1), channel_id=1, source_target_pairs={{0,1},{1,0},{2,3},{3,2},{4,5},{5,4},{6,7},{7,6},{8,9},{9,8},{10,11... | collective-permute-start | bytes 1179656 | tf_op jit(solution)/shard_map/ppermute | solution.py:333
  6.1 7.0 %collective-permute-start.5 = (f32[3,16,16,128]{3,2,1,0:T(8,128)S(1)}, f32[3,16,16,128]{3,2,1,0:T(8,128)S(1)}, u32[]{:S(2)}, u32[]{:S(2)}) collective-permute-start(f32[3,16,16,128]{3,2,1,0:T(8,128)S(1)} %copy-done), channel_id=1, source_target_pairs={{0,1},{1,0},{2,3},{3,2},{4,5},{5,4},{6,7},{7,6},{8,9},{9,8},{10,11... | collective-permute-start | bytes 1179656 | tf_op jit(solution)/shard_map/ppermute | solution.py:333
  8.4 4.8 %copy-start.3 = (s32[16,16,128]{2,1,0:T(8,128)S(1)}, s32[16,16,128]{2,1,0:T(8,128)}, u32[]{:S(2)}) copy-start(s32[16,16,128]{2,1,0:T(8,128)} %refs_10_.2) | copy-start | bytes 393220
  8.4 4.8 %copy-start.2 = (f32[16,16,128]{2,1,0:T(8,128)S(1)}, f32[16,16,128]{2,1,0:T(8,128)}, u32[]{:S(2)}) copy-start(f32[16,16,128]{2,1,0:T(8,128)} %refs_10_.3) | copy-start | bytes 393220
  8.4 9.8 %collective-permute-start.1 = (f32[128,128]{1,0:T(8,128)S(1)}, f32[128,128]{1,0:T(8,128)S(1)}, u32[]{:S(2)}, u32[]{:S(2)}) collective-permute-start(f32[128,128]{1,0:T(8,128)S(1)} %get-tuple-element.79), channel_id=1, source_target_pairs={{0,4},{4,0},{8,12},{12,8},{1,5},{5,1},{9,13},{13,9},{2,6},{6,2},{1... | collective-permute-start | bytes 196616 | tf_op jit(solution)/shard_map/ppermute | solution.py:360
  10.6 7.6 %collective-permute-start.2 = (f32[128,128]{1,0:T(8,128)S(1)}, f32[128,128]{1,0:T(8,128)S(1)}, u32[]{:S(2)}, u32[]{:S(2)}) collective-permute-start(f32[128,128]{1,0:T(8,128)S(1)} %get-tuple-element.78), channel_id=1, source_target_pairs={{0,12},{4,8},{8,4},{12,0},{1,13},{5,9},{9,5},{13,1},{2,14},{6,10},... | collective-permute-start | bytes 196616 | tf_op jit(solution)/shard_map/ppermute | solution.py:361
  13.1 5.2 %collective-permute-start.3 = (f32[64,128]{1,0:T(8,128)S(1)}, f32[64,128]{1,0:T(8,128)S(1)}, u32[]{:S(2)}, u32[]{:S(2)}) collective-permute-start(f32[64,128]{1,0:T(8,128)S(1)} %slice_add_fusion.3.refs_0_), channel_id=1, source_target_pairs={{0,8},{4,12},{8,0},{12,4},{1,9},{5,13},{9,1},{13,5},{2,10},{6,14},... | collective-permute-start | bytes 98312 | tf_op jit(solution)/shard_map/ppermute | solution.py:362
  18.6 4.2 %collective-permute-start.6 = (f32[112,128]{1,0:T(8,128)S(1)}, f32[112,128]{1,0:T(8,128)S(1)}, u32[]{:S(2)}, u32[]{:S(2)}) collective-permute-start(f32[112,128]{1,0:T(8,128)S(1)} %get-tuple-element.50), channel_id=1, source_target_pairs={{0,2},{2,0},{1,3},{3,1},{4,6},{6,4},{5,7},{7,5},{8,10},{10,8},{9,1... | collective-permute-start | bytes 172040 | tf_op jit(solution)/shard_map/ppermute | solution.py:351
  20.2 6.3 %collective-permute-start.10 = (f32[3,16,16,128]{3,2,1,0:T(8,128)S(1)}, f32[3,16,16,128]{3,2,1,0:T(8,128)S(1)}, u32[]{:S(2)}, u32[]{:S(2)}) collective-permute-start(f32[3,16,16,128]{3,2,1,0:T(8,128)S(1)} %get-tuple-element.53.refs_0_), channel_id=1, source_target_pairs={{0,1},{1,0},{2,3},{3,2},{4,5},{5,4},{6,7},{7,6},{8,9},{9,8},{10,11... | collective-permute-start | bytes 1179656 | tf_op jit(solution)/shard_map/ppermute | solution.py:333
  22.9 7.2 %collective-permute-start.7 = (f32[112,128]{1,0:T(8,128)S(1)}, f32[112,128]{1,0:T(8,128)S(1)}, u32[]{:S(2)}, u32[]{:S(2)}) collective-permute-start(f32[112,128]{1,0:T(8,128)S(1)} %get-tuple-element.77), channel_id=1, source_target_pairs={{0,4},{4,0},{8,12},{12,8},{1,5},{5,1},{9,13},{13,9},{2,6},{6,2},{1... | collective-permute-start | bytes 172040 | tf_op jit(solution)/shard_map/ppermute | solution.py:360
  23.4 6.7 %collective-permute-start.8 = (f32[112,128]{1,0:T(8,128)S(1)}, f32[112,128]{1,0:T(8,128)S(1)}, u32[]{:S(2)}, u32[]{:S(2)}) collective-permute-start(f32[112,128]{1,0:T(8,128)S(1)} %get-tuple-element.76), channel_id=1, source_target_pairs={{0,12},{4,8},{8,4},{12,0},{1,13},{5,9},{9,5},{13,1},{2,14},{6,10},... | collective-permute-start | bytes 172040 | tf_op jit(solution)/shard_map/ppermute | solution.py:361
  24.8 5.2 %collective-permute-start.9 = (f32[64,128]{1,0:T(8,128)S(1)}, f32[64,128]{1,0:T(8,128)S(1)}, u32[]{:S(2)}, u32[]{:S(2)}) collective-permute-start(f32[64,128]{1,0:T(8,128)S(1)} %slice_add_fusion.2.refs_0_), channel_id=1, source_target_pairs={{0,8},{4,12},{8,0},{12,4},{1,9},{5,13},{9,1},{13,5},{2,10},{6,14},... | collective-permute-start | bytes 98312 | tf_op jit(solution)/shard_map/ppermute | solution.py:362
  30.5 4.2 %collective-permute-start.11 = (f32[112,128]{1,0:T(8,128)S(1)}, f32[112,128]{1,0:T(8,128)S(1)}, u32[]{:S(2)}, u32[]{:S(2)}) collective-permute-start(f32[112,128]{1,0:T(8,128)S(1)} %get-tuple-element.62), channel_id=1, source_target_pairs={{0,2},{2,0},{1,3},{3,1},{4,6},{6,4},{5,7},{7,5},{8,10},{10,8},{9,1... | collective-permute-start | bytes 172040 | tf_op jit(solution)/shard_map/ppermute | solution.py:351
  32.0 6.3 %collective-permute-start.15 = (f32[3,16,16,128]{3,2,1,0:T(8,128)S(1)}, f32[3,16,16,128]{3,2,1,0:T(8,128)S(1)}, u32[]{:S(2)}, u32[]{:S(2)}) collective-permute-start(f32[3,16,16,128]{3,2,1,0:T(8,128)S(1)} %get-tuple-element.65.refs_0_), channel_id=1, source_target_pairs={{0,1},{1,0},{2,3},{3,2},{4,5},{5,4},{6,7},{7,6},{8,9},{9,8},{10,11... | collective-permute-start | bytes 1179656 | tf_op jit(solution)/shard_map/ppermute | solution.py:333
  34.8 8.0 %collective-permute-start.12 = (f32[112,128]{1,0:T(8,128)S(1)}, f32[112,128]{1,0:T(8,128)S(1)}, u32[]{:S(2)}, u32[]{:S(2)}) collective-permute-start(f32[112,128]{1,0:T(8,128)S(1)} %get-tuple-element.75), channel_id=1, source_target_pairs={{0,4},{4,0},{8,12},{12,8},{1,5},{5,1},{9,13},{13,9},{2,6},{6,2},{1... | collective-permute-start | bytes 172040 | tf_op jit(solution)/shard_map/ppermute | solution.py:360
  35.2 7.5 %collective-permute-start.13 = (f32[112,128]{1,0:T(8,128)S(1)}, f32[112,128]{1,0:T(8,128)S(1)}, u32[]{:S(2)}, u32[]{:S(2)}) collective-permute-start(f32[112,128]{1,0:T(8,128)S(1)} %get-tuple-element.74), channel_id=1, source_target_pairs={{0,12},{4,8},{8,4},{12,0},{1,13},{5,9},{9,5},{13,1},{2,14},{6,10},... | collective-permute-start | bytes 172040 | tf_op jit(solution)/shard_map/ppermute | solution.py:361
  37.6 5.2 %collective-permute-start.14 = (f32[64,128]{1,0:T(8,128)S(1)}, f32[64,128]{1,0:T(8,128)S(1)}, u32[]{:S(2)}, u32[]{:S(2)}) collective-permute-start(f32[64,128]{1,0:T(8,128)S(1)} %slice_add_fusion.1.refs_0_), channel_id=1, source_target_pairs={{0,8},{4,12},{8,0},{12,4},{1,9},{5,13},{9,1},{13,5},{2,10},{6,14},... | collective-permute-start | bytes 98312 | tf_op jit(solution)/shard_map/ppermute | solution.py:362
  43.2 4.2 %collective-permute-start.16 = (f32[112,128]{1,0:T(8,128)S(1)}, f32[112,128]{1,0:T(8,128)S(1)}, u32[]{:S(2)}, u32[]{:S(2)}) collective-permute-start(f32[112,128]{1,0:T(8,128)S(1)} %get-tuple-element.68), channel_id=1, source_target_pairs={{0,2},{2,0},{1,3},{3,1},{4,6},{6,4},{5,7},{7,5},{8,10},{10,8},{9,1... | collective-permute-start | bytes 172040 | tf_op jit(solution)/shard_map/ppermute | solution.py:351
  44.7 6.3 %collective-permute-start.20 = (f32[3,16,16,128]{3,2,1,0:T(8,128)S(1)}, f32[3,16,16,128]{3,2,1,0:T(8,128)S(1)}, u32[]{:S(2)}, u32[]{:S(2)}) collective-permute-start(f32[3,16,16,128]{3,2,1,0:T(8,128)S(1)} %get-tuple-element.71.refs_0_), channel_id=1, source_target_pairs={{0,1},{1,0},{2,3},{3,2},{4,5},{5,4},{6,7},{7,6},{8,9},{9,8},{10,11... | collective-permute-start | bytes 1179656 | tf_op jit(solution)/shard_map/ppermute | solution.py:333
  47.4 7.2 %collective-permute-start.17 = (f32[112,128]{1,0:T(8,128)S(1)}, f32[112,128]{1,0:T(8,128)S(1)}, u32[]{:S(2)}, u32[]{:S(2)}) collective-permute-start(f32[112,128]{1,0:T(8,128)S(1)} %get-tuple-element.73), channel_id=1, source_target_pairs={{0,4},{4,0},{8,12},{12,8},{1,5},{5,1},{9,13},{13,9},{2,6},{6,2},{1... | collective-permute-start | bytes 172040 | tf_op jit(solution)/shard_map/ppermute | solution.py:360
  47.9 6.7 %collective-permute-start.18 = (f32[112,128]{1,0:T(8,128)S(1)}, f32[112,128]{1,0:T(8,128)S(1)}, u32[]{:S(2)}, u32[]{:S(2)}) collective-permute-start(f32[112,128]{1,0:T(8,128)S(1)} %get-tuple-element.72), channel_id=1, source_target_pairs={{0,12},{4,8},{8,4},{12,0},{1,13},{5,9},{9,5},{13,1},{2,14},{6,10},... | collective-permute-start | bytes 172040 | tf_op jit(solution)/shard_map/ppermute | solution.py:361
  49.3 5.3 %collective-permute-start.19 = (f32[64,128]{1,0:T(8,128)S(1)}, f32[64,128]{1,0:T(8,128)S(1)}, u32[]{:S(2)}, u32[]{:S(2)}) collective-permute-start(f32[64,128]{1,0:T(8,128)S(1)} %slice_add_fusion.refs_0_), channel_id=1, source_target_pairs={{0,8},{4,12},{8,0},{12,4},{1,9},{5,13},{9,1},{13,5},{2,10},{6,14},... | collective-permute-start | bytes 98312 | tf_op jit(solution)/shard_map/ppermute | solution.py:362

commit v4 on v3

--- a/solution.py
+++ b/solution.py
@@ -360,7 +360,7 @@
         more1 = lax.ppermute(jnp.concatenate([total, face_a]), "gx", swap(4, 1))
         more2 = lax.ppermute(jnp.concatenate([total, face_b]), "gx", swap(4, 3))
         more3 = lax.ppermute(total, "gx", swap(4, 2))
-        return dict(total=total, more1=more1, more2=more2, more3=more3)
+        return dict(more2=more2, more3=more3, more1=more1, total=total)
     xm, xp = neighbours(
         jnp.concatenate([a[0] for a in parts]), jnp.concatenate([a[-1] for a in parts]), "gx"
     )

time: 55.9 us -> 54.4 us (0.973)
  waiting for transfers between devices: 23.7 us -> 19.5 us
  starting transfers between devices: 23.6 us -> 26.4 us
    ppermute x4, waiting for transfers between devices: 13.9 us -> 9.71 us  [over_gx(): more3 = lax.ppermute(total, 'gx', swap(4, 2))]
    ppermute x4, starting transfers between devices: 7.65 us -> 10.4 us  [over_gx(): more2 = lax.ppermute(jnp.concatenate([total, face_b]), 'gx', swap(4, 3))]
    ppermute x4, starting transfers between devices: 3.66 us -> 1.02 us  [over_gx(): more1 = lax.ppermute(jnp.concatenate([total, face_a]), 'gx', swap(4, 1))]
    ppermute x4, starting transfers between devices: 4.11 us -> 6.74 us  [over_gx(): more3 = lax.ppermute(total, 'gx', swap(4, 2))]
where the time goes in v4:
time: 54.4 us; the launch traced here: 54.2 us
  starting transfers between devices  26.4 us (49%)
  waiting for transfers between devices  19.5 us (36%)
  Pallas kernels  6.78 us (12%)
  between operations  0.79 us (1%)
  local copies, waits for them, and re-layouts  0.7 us (1%)
    ppermute x4, starting transfers between devices, over_gx(): more2 = lax.ppermute(jnp.concatenate([total, face_b]), 'gx', swap(4, 3))  10.4 us
    ppermute x4, waiting for transfers between devices, over_gy(): got = lax.ppermute(msg_y, 'gy', swap(2, 1))  9.78 us
    ppermute x4, waiting for transfers between devices, over_gx(): more3 = lax.ppermute(total, 'gx', swap(4, 2))  9.71 us
    ppermute x4, starting transfers between devices, over_gy(): got = lax.ppermute(msg_y, 'gy', swap(2, 1))  7.67 us
    pallas_call x9, Pallas kernels, call(): pl.pallas_call(functools.partial(kernel, names), in_specs=[spec for spec,...  6.78 us
    ppermute x4, starting transfers between devices, over_gx(): more3 = lax.ppermute(total, 'gx', swap(4, 2))  6.74 us
  transfers between devices with their start and end apart: 21, of which 8 were waited for; matrix products, arithmetic and copies ran while one was open for 0% of the time, Pallas kernels for 5%

profile of v4, /device:TPU:0, one launch (start us, length us, event | category | flops | bytes accessed | tf_op | source)
XLA Modules:
  0.0 54.2 jit_solution(2778372014817307260)
XLA Ops:
  0.6 0.0 copy-start.4
  0.6 0.0 copy-start.5
  0.7 0.0 copy-start.6
  0.7 0.0 copy-start.7
  0.7 0.0 copy-start.8
  0.7 0.6 %copy-done.4 = f32[8,128]{1,0:T(8,128)S(1)} copy-done((f32[8,128]{1,0:T(8,128)S(1)}, f32[8,128]{1,0:T(8,128)}, u32[]{:S(2)}) %copy-start.4) | copy-done | bytes 4120
  1.3 0.0 copy-done.5
  1.3 0.0 copy-done.6
  1.3 0.0 copy-done.7
  1.3 0.0 copy-done.8
  1.4 1.8 %shard_map.104 = (f32[128,128]{1,0:T(8,128)S(1)}, f32[64,128]{1,0:T(8,128)S(1)}, f32[64,128]{1,0:T(8,128)S(1)}) custom-call(s32[1,128]{1,0:T(1,128)S(1)} %bitcast.6, s32[1,128]{1,0:T(1,128)S(1)} %bitcast.8, s32[1,128]{1,0:T(1,128)S(1)} %bitcast.10, f32[8,128]{1,0:T(8,128)S(1)} %copy-done.4, f32[3,16,16,128]{3,2,1,0:T(8,128)} %refs_9_.3, ...), custom_call_target="tpu_custom_call" | custom-call | tf_op jit(solution)/shard_map/pallas_call | solution.py:304
  3.1 3.0 %collective-permute-start = (f32[128,128]{1,0:T(8,128)S(1)}, f32[128,128]{1,0:T(8,128)S(1)}, u32[]{:S(2)}, u32[]{:S(2)}) collective-permute-start(f32[128,128]{1,0:T(8,128)S(1)} %get-tuple-element.37), channel_id=1, source_target_pairs={{0,2},{2,0},{1,3},{3,1},{4,6},{6,4},{5,7},{7,5},{8,10},{10,8},{9,1... | collective-permute-start | bytes 196616 | tf_op jit(solution)/shard_map/ppermute | solution.py:351
  6.1 0.0 collective-permute-start.4
  6.1 0.0 copy-done
  6.1 0.5 collective-permute-start.5
  6.6 1.7 %collective-permute-done.refs_1_.refs_2_ = f32[128,128]{1,0:T(8,128)S(1)} collective-permute-done((f32[128,128]{1,0:T(8,128)S(1)}, f32[128,128]{1,0:T(8,128)S(1)}, u32[]{:S(2)}, u32[]{:S(2)}) %collective-permute-start) | collective-permute-done | bytes 65568 | tf_op jit(solution)/shard_map/ppermute | solution.py:351
  8.4 0.0 copy-start.2
  8.4 4.2 %collective-permute-start.1 = (f32[128,128]{1,0:T(8,128)S(1)}, f32[128,128]{1,0:T(8,128)S(1)}, u32[]{:S(2)}, u32[]{:S(2)}) collective-permute-start(f32[128,128]{1,0:T(8,128)S(1)} %get-tuple-element.79), channel_id=1, source_target_pairs={{0,12},{4,8},{8,4},{12,0},{1,13},{5,9},{9,5},{13,1},{2,14},{6,10},... | collective-permute-start | bytes 196616 | tf_op jit(solution)/shard_map/ppermute | solution.py:361
  12.6 0.0 collective-permute-start.3
  12.6 0.6 %collective-permute-start.2 = (f32[64,128]{1,0:T(8,128)S(1)}, f32[64,128]{1,0:T(8,128)S(1)}, u32[]{:S(2)}, u32[]{:S(2)}) collective-permute-start(f32[64,128]{1,0:T(8,128)S(1)} %slice_add_fusion.3.refs_3_), channel_id=1, source_target_pairs={{0,8},{4,12},{8,0},{12,4},{1,9},{5,13},{9,1},{13,5},{2,10},{6,14},... | collective-permute-start | bytes 98312 | tf_op jit(solution)/shard_map/ppermute | solution.py:362
  13.3 0.0 collective-permute-done.4.refs_3_.refs_4_
  13.3 0.0 collective-permute-done.5.refs_7_.refs_8_
  13.3 0.0 copy-done.3
  13.3 1.5 %shard_map.105 = (f32[3,16,16,128]{3,2,1,0:T(8,128)S(1)}, f32[16,16,128]{2,1,0:T(8,128)S(1)}, f32[6,16,16,128]{3,2,1,0:T(8,128)S(1)}, f32[16,16,128]{2,1,0:T(8,1...) custom-call(f32[3,16,16,128]{3,2,1,0:T(8,128)S(1)} %copy-done.1, ...), custom_call_target="tpu_custom_call" | custom-call | flops 1 | bytes 4194304 | tf_op jit(solution)/shard_map/pallas_call | solution.py:304
  14.8 2.7 %collective-permute-done.2.refs_1_ = f32[64,128]{1,0:T(8,128)S(1)} collective-permute-done((f32[64,128]{1,0:T(8,128)S(1)}, f32[64,128]{1,0:T(8,128)S(1)}, u32[]{:S(2)}, u32[]{:S(2)}) %collective-permute-start.2) | collective-permute-done | bytes 32800 | tf_op jit(solution)/shard_map/ppermute | solution.py:362
  17.4 0.0 collective-permute-done.1.refs_0_
  17.4 0.0 collective-permute-done.3.refs_2_
  17.4 0.4 shard_map.106
  17.8 1.6 %collective-permute-start.6 = (f32[112,128]{1,0:T(8,128)S(1)}, f32[112,128]{1,0:T(8,128)S(1)}, u32[]{:S(2)}, u32[]{:S(2)}) collective-permute-start(f32[112,128]{1,0:T(8,128)S(1)} %get-tuple-element.50), channel_id=1, source_target_pairs={{0,2},{2,0},{1,3},{3,1},{4,6},{6,4},{5,7},{7,5},{8,10},{10,8},{9,1... | collective-permute-start | bytes 172040 | tf_op jit(solution)/shard_map/ppermute | solution.py:351
  19.4 0.0 collective-permute-start.10
  19.4 2.7 %collective-permute-done.6.refs_1_.refs_2_ = f32[112,128]{1,0:T(8,128)S(1)} collective-permute-done((f32[112,128]{1,0:T(8,128)S(1)}, f32[112,128]{1,0:T(8,128)S(1)}, u32[]{:S(2)}, u32[]{:S(2)}) %collective-permute-start.6) | collective-permute-done | bytes 57376 | tf_op jit(solution)/shard_map/ppermute | solution.py:351
  22.1 1.7 %collective-permute-start.7 = (f32[112,128]{1,0:T(8,128)S(1)}, f32[112,128]{1,0:T(8,128)S(1)}, u32[]{:S(2)}, u32[]{:S(2)}) collective-permute-start(f32[112,128]{1,0:T(8,128)S(1)} %get-tuple-element.77), channel_id=1, source_target_pairs={{0,12},{4,8},{8,4},{12,0},{1,13},{5,9},{9,5},{13,1},{2,14},{6,10},... | collective-permute-start | bytes 172040 | tf_op jit(solution)/shard_map/ppermute | solution.py:361
  23.8 0.5 collective-permute-start.9
  24.3 2.3 %collective-permute-start.8 = (f32[64,128]{1,0:T(8,128)S(1)}, f32[64,128]{1,0:T(8,128)S(1)}, u32[]{:S(2)}, u32[]{:S(2)}) collective-permute-start(f32[64,128]{1,0:T(8,128)S(1)} %slice_add_fusion.2.refs_3_), channel_id=1, source_target_pairs={{0,8},{4,12},{8,0},{12,4},{1,9},{5,13},{9,1},{13,5},{2,10},{6,14},... | collective-permute-start | bytes 98312 | tf_op jit(solution)/shard_map/ppermute | solution.py:362
  26.6 0.0 collective-permute-done.10.refs_3_.refs_4_
  26.6 0.4 shard_map.107
  27.0 2.1 %collective-permute-done.8.refs_1_ = f32[64,128]{1,0:T(8,128)S(1)} collective-permute-done((f32[64,128]{1,0:T(8,128)S(1)}, f32[64,128]{1,0:T(8,128)S(1)}, u32[]{:S(2)}, u32[]{:S(2)}) %collective-permute-start.8) | collective-permute-done | bytes 32800 | tf_op jit(solution)/shard_map/ppermute | solution.py:362
  29.1 0.0 collective-permute-done.7.refs_0_
  29.1 0.0 collective-permute-done.9.refs_2_
  29.1 0.4 shard_map.108
  29.5 1.6 %collective-permute-start.11 = (f32[112,128]{1,0:T(8,128)S(1)}, f32[112,128]{1,0:T(8,128)S(1)}, u32[]{:S(2)}, u32[]{:S(2)}) collective-permute-start(f32[112,128]{1,0:T(8,128)S(1)} %get-tuple-element.62), channel_id=1, source_target_pairs={{0,2},{2,0},{1,3},{3,1},{4,6},{6,4},{5,7},{7,5},{8,10},{10,8},{9,1... | collective-permute-start | bytes 172040 | tf_op jit(solution)/shard_map/ppermute | solution.py:351
  31.1 0.0 collective-permute-start.15
  31.1 2.7 %collective-permute-done.11.refs_1_.refs_2_ = f32[112,128]{1,0:T(8,128)S(1)} collective-permute-done((f32[112,128]{1,0:T(8,128)S(1)}, f32[112,128]{1,0:T(8,128)S(1)}, u32[]{:S(2)}, u32[]{:S(2)}) %collective-permute-start.11) | collective-permute-done | bytes 57376 | tf_op jit(solution)/shard_map/ppermute | solution.py:351
  33.8 2.9 %collective-permute-start.12 = (f32[112,128]{1,0:T(8,128)S(1)}, f32[112,128]{1,0:T(8,128)S(1)}, u32[]{:S(2)}, u32[]{:S(2)}) collective-permute-start(f32[112,128]{1,0:T(8,128)S(1)} %get-tuple-element.75), channel_id=1, source_target_pairs={{0,12},{4,8},{8,4},{12,0},{1,13},{5,9},{9,5},{13,1},{2,14},{6,10},... | collective-permute-start | bytes 172040 | tf_op jit(solution)/shard_map/ppermute | solution.py:361
  36.7 0.0 collective-permute-start.14
  36.7 1.5 %collective-permute-start.13 = (f32[64,128]{1,0:T(8,128)S(1)}, f32[64,128]{1,0:T(8,128)S(1)}, u32[]{:S(2)}, u32[]{:S(2)}) collective-permute-start(f32[64,128]{1,0:T(8,128)S(1)} %slice_add_fusion.1.refs_3_), channel_id=1, source_target_pairs={{0,8},{4,12},{8,0},{12,4},{1,9},{5,13},{9,1},{13,5},{2,10},{6,14},... | collective-permute-start | bytes 98312 | tf_op jit(solution)/shard_map/ppermute | solution.py:362
  38.2 0.0 collective-permute-done.15.refs_3_.refs_4_
  38.2 0.4 shard_map.109
  38.7 2.9 %collective-permute-done.13.refs_1_ = f32[64,128]{1,0:T(8,128)S(1)} collective-permute-done((f32[64,128]{1,0:T(8,128)S(1)}, f32[64,128]{1,0:T(8,128)S(1)}, u32[]{:S(2)}, u32[]{:S(2)}) %collective-permute-start.13) | collective-permute-done | bytes 32800 | tf_op jit(solution)/shard_map/ppermute | solution.py:362
  41.5 0.0 collective-permute-done.12.refs_0_
  41.5 0.0 collective-permute-done.14.refs_2_
  41.5 0.4 shard_map.110
  41.9 1.6 %collective-permute-start.16 = (f32[112,128]{1,0:T(8,128)S(1)}, f32[112,128]{1,0:T(8,128)S(1)}, u32[]{:S(2)}, u32[]{:S(2)}) collective-permute-start(f32[112,128]{1,0:T(8,128)S(1)} %get-tuple-element.68), channel_id=1, source_target_pairs={{0,2},{2,0},{1,3},{3,1},{4,6},{6,4},{5,7},{7,5},{8,10},{10,8},{9,1... | collective-permute-start | bytes 172040 | tf_op jit(solution)/shard_map/ppermute | solution.py:351
  43.5 0.0 collective-permute-start.20
  43.5 2.7 %collective-permute-done.16.refs_1_.refs_2_ = f32[112,128]{1,0:T(8,128)S(1)} collective-permute-done((f32[112,128]{1,0:T(8,128)S(1)}, f32[112,128]{1,0:T(8,128)S(1)}, u32[]{:S(2)}, u32[]{:S(2)}) %collective-permute-start.16) | collective-permute-done | bytes 57376 | tf_op jit(solution)/shard_map/ppermute | solution.py:351
  46.2 1.7 %collective-permute-start.17 = (f32[112,128]{1,0:T(8,128)S(1)}, f32[112,128]{1,0:T(8,128)S(1)}, u32[]{:S(2)}, u32[]{:S(2)}) collective-permute-start(f32[112,128]{1,0:T(8,128)S(1)} %get-tuple-element.73), channel_id=1, source_target_pairs={{0,12},{4,8},{8,4},{12,0},{1,13},{5,9},{9,5},{13,1},{2,14},{6,10},... | collective-permute-start | bytes 172040 | tf_op jit(solution)/shard_map/ppermute | solution.py:361
  47.8 0.5 collective-permute-start.19
  48.3 2.3 %collective-permute-start.18 = (f32[64,128]{1,0:T(8,128)S(1)}, f32[64,128]{1,0:T(8,128)S(1)}, u32[]{:S(2)}, u32[]{:S(2)}) collective-permute-start(f32[64,128]{1,0:T(8,128)S(1)} %slice_add_fusion.refs_3_), channel_id=1, source_target_pairs={{0,8},{4,12},{8,0},{12,4},{1,9},{5,13},{9,1},{13,5},{2,10},{6,14},... | collective-permute-start | bytes 98312 | tf_op jit(solution)/shard_map/ppermute | solution.py:362
  50.6 0.0 collective-permute-done.20.refs_3_.refs_4_
  50.6 0.4 shard_map.111.refs_4_
  51.0 2.1 %collective-permute-done.18.refs_1_ = f32[64,128]{1,0:T(8,128)S(1)} collective-permute-done((f32[64,128]{1,0:T(8,128)S(1)}, f32[64,128]{1,0:T(8,128)S(1)}, u32[]{:S(2)}, u32[]{:S(2)}) %collective-permute-start.18) | collective-permute-done | bytes 32800 | tf_op jit(solution)/shard_map/ppermute | solution.py:362
  53.2 0.0 collective-permute-done.17.refs_0_
  53.2 0.0 collective-permute-done.19.refs_2_
  53.2 1.1 %shard_map.112 = (f32[3,16,16,128]{3,2,1,0:T(8,128)}, f32[8,128]{1,0:T(8,128)}) custom-call(f32[112,128]{1,0:T(8,128)S(1)} %collective-permute-done.17.refs_0_, f32[64,128]{1,0:T(8,128)S(1)} %collective-permute-done.18.refs_1_, f32[112,128]{1,0:T(8,128)S(1)} %collective-permute-done.19.refs_2_, f32[64,128]{1,0:T(8,128)S(1)} %slice_add_fusion.refs_3_, ...), custom_call_target="tpu_custom_call" | custom-call | tf_op jit(solution)/shard_map/pallas_call | solution.py:304
  (13 shorter events, 0.1 us)
Async XLA Ops:
  0.6 0.7 %copy-start.4 = (f32[8,128]{1,0:T(8,128)S(1)}, f32[8,128]{1,0:T(8,128)}, u32[]{:S(2)}) copy-start(f32[8,128]{1,0:T(8,128)} %refs_5_.9) | copy-start | bytes 12292
  0.6 0.7 %copy-start.5 = (f32[8,3]{0,1:T(4,128)S(1)}, f32[8,3]{0,1:T(4,128)}, u32[]{:S(2)}) copy-start(f32[8,3]{0,1:T(4,128)} %param.13) | copy-start | bytes 292
  0.7 0.7 %copy-start.6 = (s32[128]{0:T(128)S(1)}, s32[128]{0:T(128)}, u32[]{:S(2)}) copy-start(s32[128]{0:T(128)} %param.14) | copy-start | bytes 1540
  0.7 0.7 %copy-start.7 = (s32[128,1]{0,1:T(1,128)S(1)}, s32[128,1]{0,1:T(1,128)}, u32[]{:S(2)}) copy-start(s32[128,1]{0,1:T(1,128)} %param.15) | copy-start | bytes 1540
  0.7 0.7 %copy-start.8 = (s32[128]{0:T(128)S(1)}, s32[128]{0:T(128)}, u32[]{:S(2)}) copy-start(s32[128]{0:T(128)} %param.16) | copy-start | bytes 1540
  1.4 4.8 %copy-start.1 = (f32[3,16,16,128]{3,2,1,0:T(8,128)S(1)}, f32[3,16,16,128]{3,2,1,0:T(8,128)}, u32[]{:S(2)}) copy-start(f32[3,16,16,128]{3,2,1,0:T(8,128)} %refs_13_.1) | copy-start | bytes 1179652
  1.4 4.8 %copy-start = (f32[3,16,16,128]{3,2,1,0:T(8,128)S(1)}, f32[3,16,16,128]{3,2,1,0:T(8,128)}, u32[]{:S(2)}) copy-start(f32[3,16,16,128]{3,2,1,0:T(8,128)} %refs_9_.3) | copy-start | bytes 1179652
  3.1 5.2 %collective-permute-start = (f32[128,128]{1,0:T(8,128)S(1)}, f32[128,128]{1,0:T(8,128)S(1)}, u32[]{:S(2)}, u32[]{:S(2)}) collective-permute-start(f32[128,128]{1,0:T(8,128)S(1)} %get-tuple-element.37), channel_id=1, source_target_pairs={{0,2},{2,0},{1,3},{3,1},{4,6},{6,4},{5,7},{7,5},{8,10},{10,8},{9,1... | collective-permute-start | bytes 196616 | tf_op jit(solution)/shard_map/ppermute | solution.py:351
  6.1 7.1 %collective-permute-start.4 = (f32[3,16,16,128]{3,2,1,0:T(8,128)S(1)}, f32[3,16,16,128]{3,2,1,0:T(8,128)S(1)}, u32[]{:S(2)}, u32[]{:S(2)}) collective-permute-start(f32[3,16,16,128]{3,2,1,0:T(8,128)S(1)} %copy-done.1), channel_id=1, source_target_pairs={{0,1},{1,0},{2,3},{3,2},{4,5},{5,4},{6,7},{7,6},{8,9},{9,8},{10,11... | collective-permute-start | bytes 1179656 | tf_op jit(solution)/shard_map/ppermute | solution.py:333
  6.1 7.1 %collective-permute-start.5 = (f32[3,16,16,128]{3,2,1,0:T(8,128)S(1)}, f32[3,16,16,128]{3,2,1,0:T(8,128)S(1)}, u32[]{:S(2)}, u32[]{:S(2)}) collective-permute-start(f32[3,16,16,128]{3,2,1,0:T(8,128)S(1)} %copy-done), channel_id=1, source_target_pairs={{0,1},{1,0},{2,3},{3,2},{4,5},{5,4},{6,7},{7,6},{8,9},{9,8},{10,11... | collective-permute-start | bytes 1179656 | tf_op jit(solution)/shard_map/ppermute | solution.py:333
  8.4 4.9 %copy-start.3 = (s32[16,16,128]{2,1,0:T(8,128)S(1)}, s32[16,16,128]{2,1,0:T(8,128)}, u32[]{:S(2)}) copy-start(s32[16,16,128]{2,1,0:T(8,128)} %refs_10_.2) | copy-start | bytes 393220
  8.4 4.9 %copy-start.2 = (f32[16,16,128]{2,1,0:T(8,128)S(1)}, f32[16,16,128]{2,1,0:T(8,128)}, u32[]{:S(2)}) copy-start(f32[16,16,128]{2,1,0:T(8,128)} %refs_10_.3) | copy-start | bytes 393220
  8.4 9.0 %collective-permute-start.1 = (f32[128,128]{1,0:T(8,128)S(1)}, f32[128,128]{1,0:T(8,128)S(1)}, u32[]{:S(2)}, u32[]{:S(2)}) collective-permute-start(f32[128,128]{1,0:T(8,128)S(1)} %get-tuple-element.79), channel_id=1, source_target_pairs={{0,12},{4,8},{8,4},{12,0},{1,13},{5,9},{9,5},{13,1},{2,14},{6,10},... | collective-permute-start | bytes 196616 | tf_op jit(solution)/shard_map/ppermute | solution.py:361
  12.6 4.8 %collective-permute-start.3 = (f32[128,128]{1,0:T(8,128)S(1)}, f32[128,128]{1,0:T(8,128)S(1)}, u32[]{:S(2)}, u32[]{:S(2)}) collective-permute-start(f32[128,128]{1,0:T(8,128)S(1)} %get-tuple-element.78), channel_id=1, source_target_pairs={{0,4},{4,0},{8,12},{12,8},{1,5},{5,1},{9,13},{13,9},{2,6},{6,2},{1... | collective-permute-start | bytes 196616 | tf_op jit(solution)/shard_map/ppermute | solution.py:360
  12.6 4.8 %collective-permute-start.2 = (f32[64,128]{1,0:T(8,128)S(1)}, f32[64,128]{1,0:T(8,128)S(1)}, u32[]{:S(2)}, u32[]{:S(2)}) collective-permute-start(f32[64,128]{1,0:T(8,128)S(1)} %slice_add_fusion.3.refs_3_), channel_id=1, source_target_pairs={{0,8},{4,12},{8,0},{12,4},{1,9},{5,13},{9,1},{13,5},{2,10},{6,14},... | collective-permute-start | bytes 98312 | tf_op jit(solution)/shard_map/ppermute | solution.py:362
  17.8 4.2 %collective-permute-start.6 = (f32[112,128]{1,0:T(8,128)S(1)}, f32[112,128]{1,0:T(8,128)S(1)}, u32[]{:S(2)}, u32[]{:S(2)}) collective-permute-start(f32[112,128]{1,0:T(8,128)S(1)} %get-tuple-element.50), channel_id=1, source_target_pairs={{0,2},{2,0},{1,3},{3,1},{4,6},{6,4},{5,7},{7,5},{8,10},{10,8},{9,1... | collective-permute-start | bytes 172040 | tf_op jit(solution)/shard_map/ppermute | solution.py:351
  19.4 7.2 %collective-permute-start.10 = (f32[3,16,16,128]{3,2,1,0:T(8,128)S(1)}, f32[3,16,16,128]{3,2,1,0:T(8,128)S(1)}, u32[]{:S(2)}, u32[]{:S(2)}) collective-permute-start(f32[3,16,16,128]{3,2,1,0:T(8,128)S(1)} %get-tuple-element.53.refs_0_), channel_id=1, source_target_pairs={{0,1},{1,0},{2,3},{3,2},{4,5},{5,4},{6,7},{7,6},{8,9},{9,8},{10,11... | collective-permute-start | bytes 1179656 | tf_op jit(solution)/shard_map/ppermute | solution.py:333
  22.1 7.0 %collective-permute-start.7 = (f32[112,128]{1,0:T(8,128)S(1)}, f32[112,128]{1,0:T(8,128)S(1)}, u32[]{:S(2)}, u32[]{:S(2)}) collective-permute-start(f32[112,128]{1,0:T(8,128)S(1)} %get-tuple-element.77), channel_id=1, source_target_pairs={{0,12},{4,8},{8,4},{12,0},{1,13},{5,9},{9,5},{13,1},{2,14},{6,10},... | collective-permute-start | bytes 172040 | tf_op jit(solution)/shard_map/ppermute | solution.py:361
  23.8 5.3 %collective-permute-start.9 = (f32[112,128]{1,0:T(8,128)S(1)}, f32[112,128]{1,0:T(8,128)S(1)}, u32[]{:S(2)}, u32[]{:S(2)}) collective-permute-start(f32[112,128]{1,0:T(8,128)S(1)} %get-tuple-element.76), channel_id=1, source_target_pairs={{0,4},{4,0},{8,12},{12,8},{1,5},{5,1},{9,13},{13,9},{2,6},{6,2},{1... | collective-permute-start | bytes 172040 | tf_op jit(solution)/shard_map/ppermute | solution.py:360
  24.3 4.8 %collective-permute-start.8 = (f32[64,128]{1,0:T(8,128)S(1)}, f32[64,128]{1,0:T(8,128)S(1)}, u32[]{:S(2)}, u32[]{:S(2)}) collective-permute-start(f32[64,128]{1,0:T(8,128)S(1)} %slice_add_fusion.2.refs_3_), channel_id=1, source_target_pairs={{0,8},{4,12},{8,0},{12,4},{1,9},{5,13},{9,1},{13,5},{2,10},{6,14},... | collective-permute-start | bytes 98312 | tf_op jit(solution)/shard_map/ppermute | solution.py:362
  29.5 4.2 %collective-permute-start.11 = (f32[112,128]{1,0:T(8,128)S(1)}, f32[112,128]{1,0:T(8,128)S(1)}, u32[]{:S(2)}, u32[]{:S(2)}) collective-permute-start(f32[112,128]{1,0:T(8,128)S(1)} %get-tuple-element.62), channel_id=1, source_target_pairs={{0,2},{2,0},{1,3},{3,1},{4,6},{6,4},{5,7},{7,5},{8,10},{10,8},{9,1... | collective-permute-start | bytes 172040 | tf_op jit(solution)/shard_map/ppermute | solution.py:351
  31.1 7.2 %collective-permute-start.15 = (f32[3,16,16,128]{3,2,1,0:T(8,128)S(1)}, f32[3,16,16,128]{3,2,1,0:T(8,128)S(1)}, u32[]{:S(2)}, u32[]{:S(2)}) collective-permute-start(f32[3,16,16,128]{3,2,1,0:T(8,128)S(1)} %get-tuple-element.65.refs_0_), channel_id=1, source_target_pairs={{0,1},{1,0},{2,3},{3,2},{4,5},{5,4},{6,7},{7,6},{8,9},{9,8},{10,11... | collective-permute-start | bytes 1179656 | tf_op jit(solution)/shard_map/ppermute | solution.py:333
  33.8 7.7 %collective-permute-start.12 = (f32[112,128]{1,0:T(8,128)S(1)}, f32[112,128]{1,0:T(8,128)S(1)}, u32[]{:S(2)}, u32[]{:S(2)}) collective-permute-start(f32[112,128]{1,0:T(8,128)S(1)} %get-tuple-element.75), channel_id=1, source_target_pairs={{0,12},{4,8},{8,4},{12,0},{1,13},{5,9},{9,5},{13,1},{2,14},{6,10},... | collective-permute-start | bytes 172040 | tf_op jit(solution)/shard_map/ppermute | solution.py:361
  36.7 4.8 %collective-permute-start.14 = (f32[112,128]{1,0:T(8,128)S(1)}, f32[112,128]{1,0:T(8,128)S(1)}, u32[]{:S(2)}, u32[]{:S(2)}) collective-permute-start(f32[112,128]{1,0:T(8,128)S(1)} %get-tuple-element.74), channel_id=1, source_target_pairs={{0,4},{4,0},{8,12},{12,8},{1,5},{5,1},{9,13},{13,9},{2,6},{6,2},{1... | collective-permute-start | bytes 172040 | tf_op jit(solution)/shard_map/ppermute | solution.py:360
  36.7 4.8 %collective-permute-start.13 = (f32[64,128]{1,0:T(8,128)S(1)}, f32[64,128]{1,0:T(8,128)S(1)}, u32[]{:S(2)}, u32[]{:S(2)}) collective-permute-start(f32[64,128]{1,0:T(8,128)S(1)} %slice_add_fusion.1.refs_3_), channel_id=1, source_target_pairs={{0,8},{4,12},{8,0},{12,4},{1,9},{5,13},{9,1},{13,5},{2,10},{6,14},... | collective-permute-start | bytes 98312 | tf_op jit(solution)/shard_map/ppermute | solution.py:362
  41.9 4.2 %collective-permute-start.16 = (f32[112,128]{1,0:T(8,128)S(1)}, f32[112,128]{1,0:T(8,128)S(1)}, u32[]{:S(2)}, u32[]{:S(2)}) collective-permute-start(f32[112,128]{1,0:T(8,128)S(1)} %get-tuple-element.68), channel_id=1, source_target_pairs={{0,2},{2,0},{1,3},{3,1},{4,6},{6,4},{5,7},{7,5},{8,10},{10,8},{9,1... | collective-permute-start | bytes 172040 | tf_op jit(solution)/shard_map/ppermute | solution.py:351
  43.5 7.2 %collective-permute-start.20 = (f32[3,16,16,128]{3,2,1,0:T(8,128)S(1)}, f32[3,16,16,128]{3,2,1,0:T(8,128)S(1)}, u32[]{:S(2)}, u32[]{:S(2)}) collective-permute-start(f32[3,16,16,128]{3,2,1,0:T(8,128)S(1)} %get-tuple-element.71.refs_0_), channel_id=1, source_target_pairs={{0,1},{1,0},{2,3},{3,2},{4,5},{5,4},{6,7},{7,6},{8,9},{9,8},{10,11... | collective-permute-start | bytes 1179656 | tf_op jit(solution)/shard_map/ppermute | solution.py:333
  46.2 7.0 %collective-permute-start.17 = (f32[112,128]{1,0:T(8,128)S(1)}, f32[112,128]{1,0:T(8,128)S(1)}, u32[]{:S(2)}, u32[]{:S(2)}) collective-permute-start(f32[112,128]{1,0:T(8,128)S(1)} %get-tuple-element.73), channel_id=1, source_target_pairs={{0,12},{4,8},{8,4},{12,0},{1,13},{5,9},{9,5},{13,1},{2,14},{6,10},... | collective-permute-start | bytes 172040 | tf_op jit(solution)/shard_map/ppermute | solution.py:361
  47.8 5.3 %collective-permute-start.19 = (f32[112,128]{1,0:T(8,128)S(1)}, f32[112,128]{1,0:T(8,128)S(1)}, u32[]{:S(2)}, u32[]{:S(2)}) collective-permute-start(f32[112,128]{1,0:T(8,128)S(1)} %get-tuple-element.72), channel_id=1, source_target_pairs={{0,4},{4,0},{8,12},{12,8},{1,5},{5,1},{9,13},{13,9},{2,6},{6,2},{1... | collective-permute-start | bytes 172040 | tf_op jit(solution)/shard_map/ppermute | solution.py:360
  48.3 4.8 %collective-permute-start.18 = (f32[64,128]{1,0:T(8,128)S(1)}, f32[64,128]{1,0:T(8,128)S(1)}, u32[]{:S(2)}, u32[]{:S(2)}) collective-permute-start(f32[64,128]{1,0:T(8,128)S(1)} %slice_add_fusion.refs_3_), channel_id=1, source_target_pairs={{0,8},{4,12},{8,0},{12,4},{1,9},{5,13},{9,1},{13,5},{2,10},{6,14},... | collective-permute-start | bytes 98312 | tf_op jit(solution)/shard_map/ppermute | solution.py:362
